TPU v7x, 256 devices: a whole 4x4x8 slice. The times are simulated.
256 devices in a mesh: users: 64 (over z, x, core), camp: 4 (over y).
Axes of the slice: x: 4, y: 4, z: 8, core: 2. Of those that a mesh axis runs over, the one named last changes fastest.
Arguments:
- user_emb: bfloat16 [524288, 256], P('users'), may hold values from -6 to 6
- camp_emb: bfloat16 [16384, 256], P(('camp', 'users')), may hold values from -0.375 to 0.375
- block_ids: int32 [4, 16384], P('camp', 'users'), may hold values from 0 to 2047, as said below
- block_count: int32 [4, 64], P('camp', 'users'), may hold values from 1 to 256, as said below
- capacity: int32 [16384], P('camp'), may hold values from 4096 to 21845
- user_limit: int32 [524288], P('users'), may hold values from 128 to 682
Outputs:
- duals: float32 [16384], P('camp')
- user_duals: float32 [524288], P('users')
- load_ratio: float32 [16384], P('camp')
- user_value: float32 [524288], P('users')
Inputs may be any that keep to these rules, and one draw needn't show every extreme that they name: `block_ids`: within one device's 256 entries all ids differ. `block_count`: some device has all 256 entries eligible.
All inputs are finite; a program needn't handle non-finite values.
Results may differ from a plain program's by a relative error of at most 0.0005.
Values may be sent and summed in bfloat16 or wider, within the bound.
No kernel may reach another device: no remote copies, remote signals or barrier semaphores. Data moves between devices by JAX's collectives and lax.ppermute only.
A program may use at most 64 MiB of HBM per device.

v0:
```python
import math

import jax
import jax.numpy as jnp
from jax import lax
from jax.sharding import PartitionSpec as P

BLOCK = 128
SLOTS = 256
ITERS = 3


def shards(user_emb, camp_emb, block_ids, block_count, capacity, user_limit):
    hp = lax.Precision.HIGHEST
    panel = lax.all_gather(camp_emb, "users", axis=0, tiled=True)
    ub = user_emb.shape[0] // BLOCK
    cb = panel.shape[0] // BLOCK
    users = user_emb.reshape(ub, BLOCK, -1)
    camps = panel.reshape(cb, BLOCK, -1)
    ids = block_ids[0]
    count = block_count[0, 0]
    ublk = ids // cb
    cblk = ids % cb
    group = math.gcd(SLOTS, 32)
    turns = (count + group - 1) // group
    cap_full = capacity.astype(jnp.float32)
    cap = cap_full.reshape(cb, BLOCK)
    lim = user_limit.astype(jnp.float32).reshape(ub, BLOCK)
    cand_c = jnp.arange(cb, dtype=jnp.int32)
    cand_u = jnp.arange(ub, dtype=jnp.int32)

    def scores_of(start):
        u_part = jnp.take(users, lax.dynamic_slice_in_dim(ublk, start, group), axis=0)
        c_part = jnp.take(camps, lax.dynamic_slice_in_dim(cblk, start, group), axis=0)
        return jnp.einsum(
            "sue,sce->suc", u_part, c_part, preferred_element_type=jnp.float32
        ).astype(jnp.bfloat16)

    lam = jnp.zeros((cb, BLOCK), jnp.float32)
    mu = jnp.zeros((ub, BLOCK), jnp.float32)
    lam_bar = lam
    mu_bar = mu
    load = lam
    value = mu
    for step in range(ITERS):

        def accumulate(g, carry):
            load_acc, row_acc, value_acc = carry
            start = g * group
            s_val = scores_of(start).astype(jnp.float32)
            slot_pos = start + jnp.arange(group, dtype=jnp.int32)
            live = (slot_pos < count).astype(jnp.float32)
            c_sel = lax.dynamic_slice_in_dim(cblk, start, group)
            u_sel = lax.dynamic_slice_in_dim(ublk, start, group)
            onehot_c = (c_sel[:, None] == cand_c[None, :]).astype(jnp.float32)
            onehot_u = (u_sel[:, None] == cand_u[None, :]).astype(jnp.float32)
            lam_rows = jnp.dot(onehot_c, lam_bar, precision=hp)
            mu_rows = jnp.dot(onehot_u, mu_bar, precision=hp)
            alloc = (
                jnp.clip(s_val - lam_rows[:, None, :] - mu_rows[:, :, None], 0.0, 1.0)
                * live[:, None, None]
            )
            load_acc = load_acc + jnp.einsum("sk,sb->kb", onehot_c, alloc.sum(1), precision=hp)
            row_acc = row_acc + jnp.einsum("sk,sb->kb", onehot_u, alloc.sum(2), precision=hp)
            value_acc = value_acc + jnp.einsum(
                "sk,sb->kb", onehot_u, (alloc * s_val).sum(2), precision=hp
            )
            return (load_acc, row_acc, value_acc)

        zeros_c = jnp.zeros((cb, BLOCK), jnp.float32)
        zeros_u = jnp.zeros((ub, BLOCK), jnp.float32)
        loadp, rowp, valp = lax.fori_loop(0, turns, accumulate, (zeros_c, zeros_u, zeros_u))
        rows, value = lax.psum((rowp, valp), "camp")
        load = lax.psum(loadp, "users")
        lam_new = jnp.maximum(0.0, lam + (load - cap) / cap)
        mu_new = jnp.maximum(0.0, mu + (rows - lim) / lim)
        lam_bar = 2.0 * lam_new - lam
        mu_bar = 2.0 * mu_new - mu
        lam = lam_new
        mu = mu_new
    return (lam.reshape(-1), mu.reshape(-1), (load / cap).reshape(-1), (value / lim).reshape(-1))


def solution(mesh):
    return jax.shard_map(
        shards,
        mesh=mesh,
        in_specs=(
            P("users", None),
            P(("camp", "users"), None),
            P("camp", "users"),
            P("camp", "users"),
            P("camp"),
            P("users"),
        ),
        out_specs=(P("camp"), P("users"), P("camp"), P("users")),
        check_vma=False,
    )
```

profile of v0, /device:TPU:1, one launch (start us, length us, event | category | flops | bytes accessed | tf_op | source)
XLA Modules:
  0.0 1188.6 jit_solution(10908634113693634424)
XLA Ops:
  9.3 82.9 %all-gather.2.cloned.1.call-done = bf16[4096,256]{1,0:T(8,128)(2,1)} async-done(((bf16[64,256]{1,0:T(8,128)(2,1)}), bf16[4096,256]{1,0:T(8,128)(2,1)}) %all-gather.2.cloned.1.call-update) | async-done | bytes 2097168 | tf_op jit(solution)/shard_map/all_gather | solution.py:15
  92.2 46.9 %while.45 = (s32[]{:T(128)}, f32[32,128]{1,0:T(8,128)S(1)}, f32[64,128]{1,0:T(8,128)S(1)}, s32[]{:T(128)}, s32[256]{0:T(256)S(1)}, /*index=5*/s32[256]{0:T(256)S...) while((s32[]{:T(128)}, f32[32,128]{1,0:T(8,128)S(1)}, ...), condition=%wide.region_3.6_spmd.clone, body=%wide.region_0.5_spmd.clone.sunk | while | flops 284177056 | bytes 21211732 | solution.py:72
  93.4 4.3 gather_fusion.1
  99.8 3.6 fusion.134
  105.2 4.3 gather_fusion.1
  111.5 3.6 fusion.134
  116.9 4.3 gather_fusion.1
  123.2 3.6 fusion.134
  128.6 4.3 gather_fusion.1
  134.9 3.6 fusion.134
  139.1 60.1 %psum.50 = f32[64,128]{1,0:T(8,128)S(1)} all-reduce(f32[64,128]{1,0:T(8,128)S(1)} %get-tuple-element.270), channel_id=1, replica_groups=mesh['users'=64,'camp'=4] {'camp'}, use_global_device_ids=true, to_apply=%region_5.8 | all-reduce | flops 8192 | bytes 65536 | tf_op jit(solution)/shard_map/psum | solution.py:73
  199.2 242.1 %psum.49 = f32[32,128]{1,0:T(8,128)S(1)} all-reduce(f32[32,128]{1,0:T(8,128)S(1)} %get-tuple-element.269), channel_id=1, replica_groups=mesh['users'=64,'camp'=4] {'users'}, use_global_device_ids=true, to_apply=%region_4.7 | all-reduce | flops 4096 | bytes 32768 | tf_op jit(solution)/shard_map/psum | solution.py:74
  441.4 46.9 %while.46 = (s32[]{:T(128)}, f32[32,128]{1,0:T(8,128)S(1)}, f32[64,128]{1,0:T(8,128)S(1)}, s32[]{:T(128)}, s32[256]{0:T(256)S(1)}, /*index=5*/s32[256]{0:T(256)S...) while((s32[]{:T(128)}, f32[32,128]{1,0:T(8,128)S(1)}, ...), condition=%wide.region_9.12_spmd.clone, body=%wide.region_6.11_spmd.clone.sunk | while | flops 284177056 | bytes 21260900 | solution.py:72
  442.6 4.3 gather_fusion.3
  448.9 3.6 fusion.141
  454.3 4.3 gather_fusion.3
  460.6 3.6 fusion.141
  466.0 4.3 gather_fusion.3
  472.4 3.6 fusion.141
  477.8 4.3 gather_fusion.3
  484.1 3.6 fusion.141
  488.3 58.6 %psum.52 = f32[64,128]{1,0:T(8,128)S(1)} all-reduce(f32[64,128]{1,0:T(8,128)S(1)} %get-tuple-element.272), channel_id=1, replica_groups=mesh['users'=64,'camp'=4] {'camp'}, use_global_device_ids=true, to_apply=%region_11.14 | all-reduce | flops 8192 | bytes 65536 | tf_op jit(solution)/shard_map/psum | solution.py:73
  546.9 244.4 %psum.51 = f32[32,128]{1,0:T(8,128)S(1)} all-reduce(f32[32,128]{1,0:T(8,128)S(1)} %get-tuple-element.271), channel_id=1, replica_groups=mesh['users'=64,'camp'=4] {'users'}, use_global_device_ids=true, to_apply=%region_10.13 | all-reduce | flops 4096 | bytes 32768 | tf_op jit(solution)/shard_map/psum | solution.py:74
  791.3 46.7 %while.47 = (s32[]{:T(128)}, f32[32,128]{1,0:T(8,128)S(1)}, f32[64,128]{1,0:T(8,128)S(1)}, f32[64,128]{1,0:T(8,128)S(1)}, s32[]{:T(128)}, /*index=5*/s32[256]{0:...) while((s32[]{:T(128)}, f32[32,128]{1,0:T(8,128)S(1)}, ...), condition=%wide.region_16.19_spmd.clone, body=%wide.region_12.18_spmd.clone.sunk | while | flops 288377504 | bytes 12970703 | solution.py:72
  794.8 4.2 gather_fusion.5
  799.0 3.1 fusion.149
  806.5 4.2 gather_fusion.5
  818.2 4.2 gather_fusion.5
  829.8 4.2 gather_fusion.5
  834.0 3.1 fusion.149
  838.0 274.5 %psum.53 = f32[32,128]{1,0:T(8,128)S(1)} all-reduce(f32[32,128]{1,0:T(8,128)S(1)} %get-tuple-element.273), channel_id=1, replica_groups=mesh['users'=64,'camp'=4] {'users'}, use_global_device_ids=true, to_apply=%region_17.20 | all-reduce | flops 4096 | bytes 32768 | tf_op jit(solution)/shard_map/psum | solution.py:74
  1113.2 67.1 %all-reduce.3.cloned.1.call-done = (f32[64,128]{1,0:T(8,128)}, f32[64,128]{1,0:T(8,128)}) async-done(((f32[64,128]{1,0:T(8,128)}, f32[64,128]{1,0:T(8,128)}), (f32[64,128]{1,0:T(8,128)}, f32[64,128]{1,0:T(8,128)})) %all-reduce.3.cloned.1.call-update) | async-done | bytes 65552 | tf_op jit(solution)/shard_map/psum | solution.py:73
  (180 shorter events, 56.4 us)
Async XLA Ops:
  7.2 85.0 %all-gather.2.cloned.1.call-start = ((), (), s32[]{:S(2)}) async-start(), calls=%async_computation | async-start | bytes 2129920 | tf_op jit(solution)/shard_map/all_gather | solution.py:15
  7.9 1172.5 %all-reduce.3.cloned.1.call-start = ((), (), s32[]{:S(2)}) async-start(), calls=%async_computation.1 | async-start | bytes 131072 | tf_op jit(solution)/shard_map/psum | solution.py:73
  92.2 349.1 %copy-start.5 = (s32[4096]{0:T(1024)S(1)}, s32[4096]{0:T(1024)}, u32[]{:S(2)}) copy-start(s32[4096]{0:T(1024)} %param.20) | copy-start | bytes 49156
  92.2 349.1 %copy-start.4 = (s32[8192]{0:T(1024)S(1)}, s32[8192]{0:T(1024)}, u32[]{:S(2)}) copy-start(s32[8192]{0:T(1024)} %param.21) | copy-start | bytes 98308
  93.4 4.4 copy-start
  105.1 4.4 copy-start
  116.9 4.4 copy-start
  128.6 4.4 copy-start
  442.6 4.4 copy-start.1
  454.3 4.4 copy-start.1
  466.0 4.4 copy-start.1
  477.8 4.4 copy-start.1
  838.0 274.6 %copy-start.2 = (f32[64,128]{1,0:T(8,128)}, f32[64,128]{1,0:T(8,128)S(1)}, u32[]{:S(2)}) copy-start(f32[64,128]{1,0:T(8,128)S(1)} %get-tuple-element.275) | copy-start | bytes 98308
  838.0 274.5 %copy-start.3 = (f32[64,128]{1,0:T(8,128)}, f32[64,128]{1,0:T(8,128)S(1)}, u32[]{:S(2)}) copy-start(f32[64,128]{1,0:T(8,128)S(1)} %get-tuple-element.274) | copy-start | bytes 98308
Sparse Core Ops, SparseCore 0:
  10.8 81.3 all-gather.1
  1112.7 67.5 all-reduce.2
where the time goes:
time: 1180 us; the launch traced here: 1190 us
  blocking collectives  880 us (75%)
  waiting for transfers between devices  151 us (13%)
  local copies, waits for them, and re-layouts  76.5 us (6%)
  matrix products  54 us (5%)
  between operations  14.8 us (1%)
  other arithmetic  11.9 us (1%)
    psum x3, blocking collectives, shards(): load = lax.psum(loadp, 'users')  761 us
    psum x2, blocking collectives, shards(): rows, value = lax.psum((rowp, valp), 'camp')  119 us
    all_gather x1, waiting for transfers between devices, shards(): panel = lax.all_gather(camp_emb, 'users', axis=0, tiled=True)  82.9 us
    psum x1, waiting for transfers between devices, shards(): rows, value = lax.psum((rowp, valp), 'camp')  67.1 us
    gather x12, local copies, waits for them, and re-layouts, scores_of(): jnp.take(users, lax.dynamic_slice_in_dim(ublk, start, group), axis=0)  51.4 us
    dot_general x12, matrix products, scores_of(): jnp.einsum('sue,sce->suc', u_part, c_part, preferred_element_type=jnp.flo...  41.5 us
    gather x12, local copies, waits for them, and re-layouts, scores_of(): jnp.take(camps, lax.dynamic_slice_in_dim(cblk, start, group), axis=0)  24.9 us
  transfers between devices with their start and end apart: 2, of which 2 were waited for; matrix products, arithmetic and copies ran while one was open for 0% of the time, Pallas kernels for 0%

commit v1 on v0

v1 whole, which is shorter than its diff:
```python
import jax
import jax.numpy as jnp
from jax import lax
from jax.experimental import pallas as pl
from jax.experimental.pallas import tpu as pltpu
from jax.sharding import Mesh, PartitionSpec as P

BLOCK = 128
E = 256
SLOTS = 256
UB = 64
CB = 32
NZ, NX, NCORE, NCAMP = 8, 4, 2, 4
UNROLL = 4
F32 = jnp.float32


def _diagonal():
    row = lax.broadcasted_iota(jnp.int32, (BLOCK, BLOCK), 0)
    col = lax.broadcasted_iota(jnp.int32, (BLOCK, BLOCK), 1)
    return row == col


def _clear(lacc, racc):
    lacc[...] = jnp.zeros_like(lacc)
    racc[...] = jnp.zeros_like(racc)


def _slots(ids, count, one):
    cnt = count[0, 0]

    def turn(g, carry):
        for k in range(UNROLL):
            slot = g * UNROLL + k
            code = ids[0, slot]
            ub = code >> 5
            cb = code & (CB - 1)
            live = slot < cnt
            one(slot, ub, cb, jnp.where(live, ub, UB), jnp.where(live, cb, CB))
        return carry

    lax.fori_loop(0, (cnt + UNROLL - 1) // UNROLL, turn, 0)


def _fold(x):
    return x.reshape(BLOCK // 8, 8, BLOCK).sum(0)


def _finish_load(lacc, keep, give, core):
    eye = _diagonal()

    def row(b):
        total = jnp.sum(lacc[b], axis=1, keepdims=True)
        return jnp.sum(jnp.where(eye, total, 0.0), axis=0, keepdims=True)

    half = CB // 2

    def turn(b, carry):
        keep[pl.ds(b, 1), :] = row(core * half + b)
        give[pl.ds(b, 1), :] = row((1 - core) * half + b)
        return carry

    lax.fori_loop(0, half, turn, 0, unroll=2)


def first_kernel(core, ids, count, users, camps, scores, keep, give, rows, lacc, racc):
    _clear(lacc, racc)

    def one(slot, ub, cb, to_u, to_c):
        s = lax.dot_general(
            camps[cb], users[ub], (((1,), (1,)), ((), ())), preferred_element_type=F32
        ).astype(jnp.bfloat16)
        scores[slot] = s
        x = jnp.clip(s.astype(F32), 0.0, 1.0)
        lacc[to_c] += x
        racc[to_u] += _fold(x)

    _slots(ids, count, one)
    _finish_load(lacc, keep, give, core[0])
    rows[...] = racc[:UB].sum(axis=1)


def _load_of(own, other, core):
    a, b = own[...], other[...]
    first = core == 0
    return jnp.concatenate([jnp.where(first, a, b), jnp.where(first, b, a)], axis=0)


def _duals(core, own, other, r0, r1, r2, r3, cap_i, lim_i, lam_in, mu_in):
    load = _load_of(own, other, core)
    rows = (r0[...] + r2[...]) + (r1[...] + r3[...])
    cap = cap_i[...].astype(F32)
    lim = lim_i[...].astype(F32)
    lam_new = jnp.maximum(0.0, lam_in + (load - cap) / cap)
    mu_new = jnp.maximum(0.0, mu_in + (rows - lim) / lim)
    return load, cap, lim, lam_new, mu_new


def _round_kernel(core, ids, count, scores, own, other, r0, r1, r2, r3, cap_i, lim_i, lam_in, mu_in,
                  keep, give, rows, values, lam_out, mu_out, lacc, racc, vacc, lamb, mub):
    _clear(lacc, racc)
    if vacc is not None:
        vacc[...] = jnp.zeros_like(vacc)
    lam = 0.0 if lam_in is None else lam_in[...]
    mu = 0.0 if mu_in is None else mu_in[...]
    _, _, _, lam_new, mu_new = _duals(core[0], own, other, r0, r1, r2, r3, cap_i, lim_i, lam, mu)
    lam_out[...] = lam_new
    mu_out[...] = mu_new
    lam_bar = 2.0 * lam_new - lam
    mub[:UB] = (2.0 * mu_new - mu)[:, None, :]
    eye = _diagonal()
    for b in range(CB):
        spread = jnp.where(eye, lam_bar[b:b + 1, :], 0.0)
        lamb[b] = jnp.broadcast_to(jnp.sum(spread, axis=1, keepdims=True), (BLOCK, BLOCK))

    def one(slot, ub, cb, to_u, to_c):
        s = scores[slot].astype(F32)
        x = jnp.clip(s - lamb[cb] - mub[ub], 0.0, 1.0)
        lacc[to_c] += x
        racc[to_u] += _fold(x)
        if vacc is not None:
            vacc[to_u] += _fold(x * s)

    _slots(ids, count, one)
    _finish_load(lacc, keep, give, core[0])
    rows[...] = racc[:UB].sum(axis=1)
    if vacc is not None:
        values[...] = vacc[:UB].sum(axis=1)


def second_kernel(core, ids, count, scores, own, other, r0, r1, r2, r3, cap_i, lim_i,
                  keep, give, rows, lam_out, mu_out, lacc, racc, lamb, mub):
    _round_kernel(core, ids, count, scores, own, other, r0, r1, r2, r3, cap_i, lim_i, None, None,
                  keep, give, rows, None, lam_out, mu_out, lacc, racc, None, lamb, mub)


def third_kernel(core, ids, count, scores, own, other, r0, r1, r2, r3, cap_i, lim_i, lam_in, mu_in,
                 keep, give, out, lam_out, mu_out, lacc, racc, vacc, lamb, mub):
    _round_kernel(core, ids, count, scores, own, other, r0, r1, r2, r3, cap_i, lim_i, lam_in, mu_in,
                  keep, give, out.at[0], out.at[1], lam_out, mu_out, lacc, racc, vacc, lamb, mub)


def last_kernel(core, own, other, p0, p1, p2, p3, cap_i, lim_i, lam_in, mu_in, duals, user_duals, ratio, user_value):
    load, cap, lim, lam_new, mu_new = _duals(
        core[0], own, other, p0.at[0], p1.at[0], p2.at[0], p3.at[0], cap_i, lim_i, lam_in[...], mu_in[...])
    duals[...] = lam_new
    user_duals[...] = mu_new
    ratio[...] = load / cap
    user_value[...] = ((p0[1] + p2[1]) + (p1[1] + p3[1])) / lim


SMEM = pl.BlockSpec(memory_space=pltpu.SMEM)
VMEM = pl.BlockSpec(memory_space=pltpu.VMEM)


def _call(kernel, n_smem, args, outs, scratch=()):
    return pl.pallas_call(
        kernel,
        in_specs=[SMEM] * n_smem + [VMEM] * (len(args) - n_smem),
        out_specs=[VMEM] * len(outs),
        out_shape=[jax.ShapeDtypeStruct(s, d) for s, d in outs],
        scratch_shapes=[pltpu.VMEM(s, F32) for s in scratch],
        compiler_params=pltpu.CompilerParams(vmem_limit_bytes=40 * 2 ** 20),
    )(*args)


LACC = (CB + 1, BLOCK, BLOCK)
RACC = (UB + 1, 8, BLOCK)
HALF = ((CB // 2, BLOCK), F32)
ROWS = ((UB, BLOCK), F32)
LAM = ((CB, BLOCK), F32)
MUB = (UB, 1, BLOCK)
LAMB = (CB, BLOCK, BLOCK)


def _spread(x, axes, n):
    return lax.all_to_all(jnp.broadcast_to(x[None], (n,) + x.shape), axes, 0, 0, tiled=True)


def _swap(x):
    return lax.ppermute(x, "core", [(0, 1), (1, 0)])


def _sum_load(keep, give):
    own = keep + _swap(give)
    own = _spread(own, ("z", "x"), NZ * NX).sum(0)
    return own, _swap(own)


def _shift(x, k):
    return lax.ppermute(x, "camp", [((i + k) % NCAMP, i) for i in range(NCAMP)])


def _camp_parts(x):
    return x, _shift(x, 1), _shift(x, 2), _shift(x, 3)


def shards(user_emb, camp_emb, block_ids, block_count, capacity, user_limit):
    core = lax.axis_index("core")
    cap = capacity.reshape(CB, BLOCK)
    lim = user_limit.reshape(UB, BLOCK)
    users = user_emb.reshape(UB, BLOCK, E)

    part = _spread(camp_emb, "z", NZ)
    part = _spread(part.reshape(NZ, 64, E), "x", NX).reshape(NX, NZ, 64, E)
    peer = _swap(part)
    first = core == 0
    both = jnp.stack([jnp.where(first, part, peer), jnp.where(first, peer, part)], axis=2)
    camps = both.transpose(1, 0, 2, 3, 4).reshape(CB, BLOCK, E)

    where = jnp.reshape(core, (1,)).astype(jnp.int32)
    slots = (where, block_ids, block_count)
    scores, keep, give, rows = _call(
        first_kernel, 3, (*slots, users, camps),
        [((SLOTS, BLOCK, BLOCK), jnp.bfloat16), HALF, HALF, ROWS], [LACC, RACC])
    parts = _camp_parts(rows)
    own, other = _sum_load(keep, give)
    keep, give, rows, lam, mu = _call(
        second_kernel, 3, (*slots, scores, own, other, *parts, cap, lim),
        [HALF, HALF, ROWS, LAM, ROWS], [LACC, RACC, LAMB, MUB])
    parts = _camp_parts(rows)
    own, other = _sum_load(keep, give)
    keep, give, both_sums, lam, mu = _call(
        third_kernel, 3, (*slots, scores, own, other, *parts, cap, lim, lam, mu),
        [HALF, HALF, ((2, UB, BLOCK), F32), LAM, ROWS], [LACC, RACC, RACC, LAMB, MUB])
    parts = _camp_parts(both_sums)
    own, other = _sum_load(keep, give)
    duals, user_duals, ratio, value = _call(
        last_kernel, 1, (where, own, other, *parts, cap, lim, lam, mu), [LAM, ROWS, LAM, ROWS])
    return duals.reshape(-1), user_duals.reshape(-1), ratio.reshape(-1), value.reshape(-1)


def solution(mesh):
    fine = Mesh(mesh.devices.reshape(NZ, NX, NCORE, NCAMP), ("z", "x", "core", "camp"))
    users = ("z", "x", "core")
    return jax.shard_map(
        shards,
        mesh=fine,
        in_specs=(P(users, None), P(("camp",) + users, None), P("camp", users), P("camp", users), P("camp"), P(users)),
        out_specs=(P("camp"), P(users), P("camp"), P(users)),
        check_vma=False,
    )
```

time: 1180 us -> 151 us (0.13)
  blocking collectives: 880 us -> 35.1 us
  waiting for transfers between devices: 151 us -> 30 us
  local copies, waits for them, and re-layouts: 76.5 us -> 12 us
  matrix products: 54 us -> 0 us
  starting transfers between devices: 0.08 us -> 48.6 us
  Pallas kernels: 0 us -> 22.6 us
  between operations: 14.8 us -> 1.42 us
    psum x5 -> x0, blocking collectives: 880 us -> none  [the longest x3 761 us: shards(): load = lax.psum(loadp, 'users')]
    all_gather x1 -> x0, waiting for transfers between devices: 82.9 us -> none  [shards(): panel = lax.all_gather(camp_emb, 'users', axis=0, tiled=True)]
    gather x24 -> x0, local copies, waits for them, and re-layouts: 76.4 us -> none  [the longest x12 51.4 us: scores_of(): jnp.take(users, lax.dynamic_slice_in_dim(ublk, start, group), axis=0)]
    psum x1 -> x0, waiting for transfers between devices: 67.1 us -> none  [shards(): rows, value = lax.psum((rowp, valp), 'camp')]
    dot_general x64 -> x0, matrix products: 54 us -> none  [the longest x12 41.5 us: scores_of(): jnp.einsum('sue,sce->suc', u_part, c_part, preferred_element_type=jnp.flo...]
    ppermute x0 -> x16, starting transfers between devices: none -> 36.8 us  [the longest x7 24.6 us: _swap(): return lax.ppermute(x, 'core', [(0, 1), (1, 0)])]
    all_to_all x0 -> x2, blocking collectives: none -> 35.1 us  [_spread(): lax.all_to_all(jnp.broadcast_to(x[None], (n,) + x.shape), axes, 0, 0, til...]
    all_to_all x0 -> x3, waiting for transfers between devices: none -> 23.4 us  [_spread(): lax.all_to_all(jnp.broadcast_to(x[None], (n,) + x.shape), axes, 0, 0, til...]
  transfers between devices with their start and end apart: 2 -> 19, of which waited for: 2 -> 10; matrix products, arithmetic and copies ran while one was open for 0% -> 0% of each run, Pallas kernels for 0% -> 0%
where the time goes in v1:
time: 151 us; the launch traced here: 150 us
  starting transfers between devices  48.6 us (32%)
  blocking collectives  35.1 us (23%)
  waiting for transfers between devices  30 us (20%)
  Pallas kernels  22.6 us (15%)
  local copies, waits for them, and re-layouts  12 us (8%)
    all_to_all x2, blocking collectives, _spread(): lax.all_to_all(jnp.broadcast_to(x[None], (n,) + x.shape), axes, 0, 0, til...  35.1 us
    ppermute x7, starting transfers between devices, _swap(): return lax.ppermute(x, 'core', [(0, 1), (1, 0)])  24.6 us
    all_to_all x3, waiting for transfers between devices, _spread(): lax.all_to_all(jnp.broadcast_to(x[None], (n,) + x.shape), axes, 0, 0, til...  23.4 us
    pallas_call x4, Pallas kernels, _call(): pl.pallas_call(kernel, in_specs=[SMEM] * n_smem + [VMEM] * (len(args) - n...  22.6 us
    ppermute x9, starting transfers between devices, _shift(): return lax.ppermute(x, 'camp', [((i + k) % NCAMP, i) for i in range(NCAMP)])  12.2 us
    all_to_all x3, starting transfers between devices, _spread(): lax.all_to_all(jnp.broadcast_to(x[None], (n,) + x.shape), axes, 0, 0, til...  11.8 us
    unnamed x12, local copies, waits for them, and re-layouts  8.7 us
    ppermute x7, waiting for transfers between devices, _swap(): return lax.ppermute(x, 'core', [(0, 1), (1, 0)])  6.57 us
  transfers between devices with their start and end apart: 19, of which 10 were waited for; matrix products, arithmetic and copies ran while one was open for 0% of the time, Pallas kernels for 0%

profile of v1, /device:TPU:1, one launch (start us, length us, event | category | flops | bytes accessed | tf_op | source)
XLA Modules:
  0.0 150.1 jit_solution(2361386447875992354)
XLA Ops:
  1.4 19.2 %all_to_all.25 = bf16[8,64,256]{2,1,0:T(8,128)(2,1)S(1)} all-to-all(bf16[8,64,256]{2,1,0:T(8,128)(2,1)S(1)} %broadcast_in_dim.10), channel_id=1, replica_groups=mesh['z'=8,'x'=4,'core'=2,'camp'=4] {'z'}, dimensions={0} | all-to-all | bytes 524288 | tf_op jit(solution)/shard_map/all_to_all | solution.py:177
  20.7 15.9 %all_to_all.26 = bf16[4,8,64,256]{3,2,1,0:T(8,128)(2,1)S(1)} all-to-all(bf16[4,8,64,256]{3,2,1,0:T(8,128)(2,1)S(1)} %broadcast_in_dim.11), channel_id=1, replica_groups=mesh['z'=8,'x'=4,'core'=2,'camp'=4] {'x'}, dimensions={0} | all-to-all | bytes 2097152 | tf_op jit(solution)/shard_map/all_to_all | solution.py:177
  36.6 4.0 %collective-permute-start = (bf16[4,8,64,256]{3,2,1,0:T(8,128)(2,1)S(1)}, bf16[4,8,64,256]{3,2,1,0:T(8,128)(2,1)S(1)}, u32[]{:S(2)}, u32[]{:S(2)}) collective-permute-start(bf16[4,8,64,256]{3,2,1,0:T(8,128)(2,1)S(1)} %all_to_all.26), channel_id=1, source_target_pairs={{0,4},{4,0},{1,5},{5,1},{2,6},{6,2},{3,7},{7,3},{8,12},{12,8},{9,1... | collective-permute-start | bytes 3145736 | tf_op jit(solution)/shard_map/ppermute | solution.py:181
  41.2 1.6 %collective-permute-done = bf16[4,8,64,256]{3,2,1,0:T(8,128)(2,1)S(1)} collective-permute-done((bf16[4,8,64,256]{3,2,1,0:T(8,128)(2,1)S(1)}, bf16[4,8,64,256]{3,2,1,0:T(8,128)(2,1)S(1)}, u32[]{:S(2)}, u32[]{:S(2)}) %collective-permute-start) | collective-permute-done | bytes 1048608 | tf_op jit(solution)/shard_map/ppermute | solution.py:181
  43.5 1.9 %copy-done.2 = bf16[8192,256]{1,0:T(8,128)(2,1)S(1)} copy-done((bf16[8192,256]{1,0:T(8,128)(2,1)S(1)}, bf16[8192,256]{1,0:T(8,128)(2,1)}, u32[]{:S(2)}) %copy-start.2) | copy-done | bytes 4194328
  45.4 12.1 %shard_map.93 = (bf16[256,128,128]{2,1,0:T(8,128)(2,1)}, f32[16,128]{1,0:T(8,128)S(1)}, f32[16,128]{1,0:T(8,128)S(1)}, f32[64,128]{1,0:T(8,128)S(1)}) custom-call(s32[1]{0:T(128)} %bitcast.core, s32[1,256]{1,0:T(1,128)S(1)} %copy-done.5, s32[1,1]{1,0:T(1,128)S(6)} %copy.13.count, bf16[64,128,256]{2,1,0:T(8,128)(2,1)S(1)} %bitcast.16, ...), custom_call_target="tpu_custom_call" | custom-call | tf_op jit(solution)/shard_map/pallas_call | solution.py:157
  57.5 8.1 %collective-permute-start.1 = (f32[16,128]{1,0:T(8,128)S(1)}, f32[16,128]{1,0:T(8,128)S(1)}, u32[]{:S(2)}, u32[]{:S(2)}) collective-permute-start(f32[16,128]{1,0:T(8,128)S(1)} %get-tuple-element.24), channel_id=1, source_target_pairs={{0,4},{4,0},{1,5},{5,1},{2,6},{6,2},{3,7},{7,3},{8,12},{12,8},{9,1... | collective-permute-start | bytes 24584 | tf_op jit(solution)/shard_map/ppermute | solution.py:181
  65.6 0.8 collective-permute-done.1
  67.2 3.9 %all-to-all-start.2 = ((f32[32,16,128]{2,1,0:T(8,128)}), f32[32,16,128]{2,1,0:T(8,128)S(1)}, u32[]{:S(2)}, u32[]{:S(2)}) async-start(f32[32,16,128]{2,1,0:T(8,128)} %broadcast_in_dim.12), calls=%async_computation.2 | async-start | bytes 524288 | tf_op jit(solution)/shard_map/all_to_all | solution.py:177
  71.0 1.9 %collective-permute-start.5 = (f32[64,128]{1,0:T(8,128)S(1)}, f32[64,128]{1,0:T(8,128)S(1)}, u32[]{:S(2)}, u32[]{:S(2)}) collective-permute-start(f32[64,128]{1,0:T(8,128)S(1)} %get-tuple-element.25.r0), channel_id=1, source_target_pairs={{3,0},{0,1},{1,2},{2,3},{7,4},{4,5},{5,6},{6,7},{11,8},{8,9},{9,10... | collective-permute-start | bytes 98312 | tf_op jit(solution)/shard_map/ppermute | solution.py:191
  72.9 1.6 %collective-permute-start.4 = (f32[64,128]{1,0:T(8,128)S(1)}, f32[64,128]{1,0:T(8,128)S(1)}, u32[]{:S(2)}, u32[]{:S(2)}) collective-permute-start(f32[64,128]{1,0:T(8,128)S(1)} %get-tuple-element.25.r0), channel_id=1, source_target_pairs={{2,0},{3,1},{0,2},{1,3},{6,4},{7,5},{4,6},{5,7},{10,8},{11,9},{8,1... | collective-permute-start | bytes 98312 | tf_op jit(solution)/shard_map/ppermute | solution.py:191
  74.6 0.9 collective-permute-start.3
  75.4 7.4 %all-to-all-done.2 = f32[32,16,128]{2,1,0:T(8,128)S(1)} async-done(((f32[32,16,128]{2,1,0:T(8,128)}), f32[32,16,128]{2,1,0:T(8,128)S(1)}, u32[]{:S(2)}, u32[]{:S(2)}) %all-to-all-start.2) | async-done | bytes 262176 | tf_op jit(solution)/shard_map/all_to_all | solution.py:177
  82.9 2.3 %collective-permute-start.2 = (f32[16,128]{1,0:T(8,128)S(1)}, f32[16,128]{1,0:T(8,128)S(1)}, u32[]{:S(2)}, u32[]{:S(2)}) collective-permute-start(f32[16,128]{1,0:T(8,128)S(1)} %reduce_sum.27.own), channel_id=1, source_target_pairs={{0,4},{4,0},{1,5},{5,1},{2,6},{6,2},{3,7},{7,3},{8,12},{12,8},{9,1... | collective-permute-start | bytes 24584 | tf_op jit(solution)/shard_map/ppermute | solution.py:181
  86.0 3.4 %copy-done = bf16[256,128,128]{2,1,0:T(8,128)(2,1)S(1)} copy-done((bf16[256,128,128]{2,1,0:T(8,128)(2,1)S(1)}, bf16[256,128,128]{2,1,0:T(8,128)(2,1)}, u32[]{:S(2)}) %copy-start) | copy-done | bytes 8388632
  89.4 4.6 %shard_map.94 = (f32[16,128]{1,0:T(8,128)S(1)}, f32[16,128]{1,0:T(8,128)S(1)}, f32[64,128]{1,0:T(8,128)S(1)}, f32[32,128]{1,0:T(8,128)S(1)}, f32[64,128]{1,0:T(8,128)S(1)}) custom-call(s32[1]{0:T(128)} %bitcast.core, s32[1,256]{1,0:T(1,128)S(1)} %copy-done.5, s32[1,1]{1,0:T(1,128)S(6)} %copy.13.count, bf16[256,128,128]{2,1,0:T(8,128)(2,1)S(1)} %copy-done, ...), custom_call_target="tpu_custom_call" | custom-call | tf_op jit(solution)/shard_map/pallas_call | solution.py:157
  94.0 2.7 %collective-permute-start.6 = (f32[16,128]{1,0:T(8,128)S(1)}, f32[16,128]{1,0:T(8,128)S(1)}, u32[]{:S(2)}, u32[]{:S(2)}) collective-permute-start(f32[16,128]{1,0:T(8,128)S(1)} %get-tuple-element.27), channel_id=1, source_target_pairs={{0,4},{4,0},{1,5},{5,1},{2,6},{6,2},{3,7},{7,3},{8,12},{12,8},{9,1... | collective-permute-start | bytes 24584 | tf_op jit(solution)/shard_map/ppermute | solution.py:181
  96.7 0.8 collective-permute-done.6
  98.3 3.9 %all-to-all-start.3 = ((f32[32,16,128]{2,1,0:T(8,128)}), f32[32,16,128]{2,1,0:T(8,128)S(1)}, u32[]{:S(2)}, u32[]{:S(2)}) async-start(f32[32,16,128]{2,1,0:T(8,128)} %broadcast_in_dim.13), calls=%async_computation.3 | async-start | bytes 524288 | tf_op jit(solution)/shard_map/all_to_all | solution.py:177
  102.2 1.3 collective-permute-start.10
  103.4 2.0 %collective-permute-start.9 = (f32[64,128]{1,0:T(8,128)S(1)}, f32[64,128]{1,0:T(8,128)S(1)}, u32[]{:S(2)}, u32[]{:S(2)}) collective-permute-start(f32[64,128]{1,0:T(8,128)S(1)} %get-tuple-element.28.r0), channel_id=1, source_target_pairs={{2,0},{3,1},{0,2},{1,3},{6,4},{7,5},{4,6},{5,7},{10,8},{11,9},{8,1... | collective-permute-start | bytes 98312 | tf_op jit(solution)/shard_map/ppermute | solution.py:191
  106.2 7.8 %all-to-all-done.3 = f32[32,16,128]{2,1,0:T(8,128)S(1)} async-done(((f32[32,16,128]{2,1,0:T(8,128)}), f32[32,16,128]{2,1,0:T(8,128)S(1)}, u32[]{:S(2)}, u32[]{:S(2)}) %all-to-all-start.3) | async-done | bytes 262176 | tf_op jit(solution)/shard_map/all_to_all | solution.py:177
  114.1 2.1 %collective-permute-start.7 = (f32[16,128]{1,0:T(8,128)S(1)}, f32[16,128]{1,0:T(8,128)S(1)}, u32[]{:S(2)}, u32[]{:S(2)}) collective-permute-start(f32[16,128]{1,0:T(8,128)S(1)} %reduce_sum.28.own), channel_id=1, source_target_pairs={{0,4},{4,0},{1,5},{5,1},{2,6},{6,2},{3,7},{7,3},{8,12},{12,8},{9,1... | collective-permute-start | bytes 24584 | tf_op jit(solution)/shard_map/ppermute | solution.py:181
  117.0 3.4 %copy-done.1 = bf16[256,128,128]{2,1,0:T(8,128)(2,1)S(1)} copy-done((bf16[256,128,128]{2,1,0:T(8,128)(2,1)S(1)}, bf16[256,128,128]{2,1,0:T(8,128)(2,1)}, u32[]{:S(2)}) %copy-start.1) | copy-done | bytes 8388632
  120.4 5.2 %shard_map.95 = (f32[16,128]{1,0:T(8,128)S(1)}, f32[16,128]{1,0:T(8,128)S(1)}, f32[2,64,128]{2,1,0:T(8,128)S(1)}, f32[32,128]{1,0:T(8,128)S(1)}, f32[64,128]{1,0:T(8,128)S(1)}) custom-call(s32[1]{0:T(128)} %bitcast.core, s32[1,256]{1,0:T(1,128)S(1)} %copy-done.5, s32[1,1]{1,0:T(1,128)S(6)} %copy.13.count, bf16[256,128,128]{2,1,0:T(8,128)(2,1)S(1)} %copy-done.1, ...), custom_call_target="tpu_custom_call" | custom-call | tf_op jit(solution)/shard_map/pallas_call | solution.py:157
  125.6 3.3 %collective-permute-start.11 = (f32[16,128]{1,0:T(8,128)S(1)}, f32[16,128]{1,0:T(8,128)S(1)}, u32[]{:S(2)}, u32[]{:S(2)}) collective-permute-start(f32[16,128]{1,0:T(8,128)S(1)} %get-tuple-element.32), channel_id=1, source_target_pairs={{0,4},{4,0},{1,5},{5,1},{2,6},{6,2},{3,7},{7,3},{8,12},{12,8},{9,1... | collective-permute-start | bytes 24584 | tf_op jit(solution)/shard_map/ppermute | solution.py:181
  129.0 0.8 collective-permute-done.11
  130.5 4.0 %all-to-all-start.4 = ((f32[32,16,128]{2,1,0:T(8,128)}), f32[32,16,128]{2,1,0:T(8,128)S(1)}, u32[]{:S(2)}, u32[]{:S(2)}) async-start(f32[32,16,128]{2,1,0:T(8,128)} %broadcast_in_dim.14), calls=%async_computation.4 | async-start | bytes 524288 | tf_op jit(solution)/shard_map/all_to_all | solution.py:177
  134.6 0.9 collective-permute-start.15
  135.4 2.1 %collective-permute-start.14 = (f32[2,64,128]{2,1,0:T(8,128)S(1)}, f32[2,64,128]{2,1,0:T(8,128)S(1)}, u32[]{:S(2)}, u32[]{:S(2)}) collective-permute-start(f32[2,64,128]{2,1,0:T(8,128)S(1)} %get-tuple-element.33.p0), channel_id=1, source_target_pairs={{2,0},{3,1},{0,2},{1,3},{6,4},{7,5},{4,6},{5,7},{10,8},{11,9},{8,1... | collective-permute-start | bytes 196616 | tf_op jit(solution)/shard_map/ppermute | solution.py:191
  138.3 8.1 %all-to-all-done.4 = f32[32,16,128]{2,1,0:T(8,128)S(1)} async-done(((f32[32,16,128]{2,1,0:T(8,128)}), f32[32,16,128]{2,1,0:T(8,128)S(1)}, u32[]{:S(2)}, u32[]{:S(2)}) %all-to-all-start.4) | async-done | bytes 262176 | tf_op jit(solution)/shard_map/all_to_all | solution.py:177
  146.5 2.1 %collective-permute-start.12 = (f32[16,128]{1,0:T(8,128)S(1)}, f32[16,128]{1,0:T(8,128)S(1)}, u32[]{:S(2)}, u32[]{:S(2)}) collective-permute-start(f32[16,128]{1,0:T(8,128)S(1)} %reduce_sum.29.own), channel_id=1, source_target_pairs={{0,4},{4,0},{1,5},{5,1},{2,6},{6,2},{3,7},{7,3},{8,12},{12,8},{9,1... | collective-permute-start | bytes 24584 | tf_op jit(solution)/shard_map/ppermute | solution.py:181
  (38 shorter events, 8.4 us)
Async XLA Ops:
  36.6 6.2 %collective-permute-start = (bf16[4,8,64,256]{3,2,1,0:T(8,128)(2,1)S(1)}, bf16[4,8,64,256]{3,2,1,0:T(8,128)(2,1)S(1)}, u32[]{:S(2)}, u32[]{:S(2)}) collective-permute-start(bf16[4,8,64,256]{3,2,1,0:T(8,128)(2,1)S(1)} %all_to_all.26), channel_id=1, source_target_pairs={{0,4},{4,0},{1,5},{5,1},{2,6},{6,2},{3,7},{7,3},{8,12},{12,8},{9,1... | collective-permute-start | bytes 3145736 | tf_op jit(solution)/shard_map/ppermute | solution.py:181
  43.2 2.2 %copy-start.2 = (bf16[8192,256]{1,0:T(8,128)(2,1)S(1)}, bf16[8192,256]{1,0:T(8,128)(2,1)}, u32[]{:S(2)}) copy-start(bf16[8192,256]{1,0:T(8,128)(2,1)} %param.6) | copy-start | bytes 12582916
  43.2 2.2 %copy-start.5 = (s32[1,256]{1,0:T(1,128)S(1)}, s32[1,256]{1,0:T(1,128)}, u32[]{:S(2)}) copy-start(s32[1,256]{1,0:T(1,128)} %ids.5) | copy-start | bytes 3076
  45.4 40.6 %copy-start.3 = (s32[8192]{0:T(1024)S(1)}, s32[8192]{0:T(1024)}, u32[]{:S(2)}) copy-start(s32[8192]{0:T(1024)} %param.11) | copy-start | bytes 98308
  45.4 40.6 %copy-start.4 = (s32[4096]{0:T(1024)S(1)}, s32[4096]{0:T(1024)}, u32[]{:S(2)}) copy-start(s32[4096]{0:T(1024)} %param.10) | copy-start | bytes 49156
  57.5 9.0 %collective-permute-start.1 = (f32[16,128]{1,0:T(8,128)S(1)}, f32[16,128]{1,0:T(8,128)S(1)}, u32[]{:S(2)}, u32[]{:S(2)}) collective-permute-start(f32[16,128]{1,0:T(8,128)S(1)} %get-tuple-element.24), channel_id=1, source_target_pairs={{0,4},{4,0},{1,5},{5,1},{2,6},{6,2},{3,7},{7,3},{8,12},{12,8},{9,1... | collective-permute-start | bytes 24584 | tf_op jit(solution)/shard_map/ppermute | solution.py:181
  67.2 15.7 %all-to-all-start.2 = ((f32[32,16,128]{2,1,0:T(8,128)}), f32[32,16,128]{2,1,0:T(8,128)S(1)}, u32[]{:S(2)}, u32[]{:S(2)}) async-start(f32[32,16,128]{2,1,0:T(8,128)} %broadcast_in_dim.12), calls=%async_computation.2 | async-start | bytes 524288 | tf_op jit(solution)/shard_map/all_to_all | solution.py:177
  71.0 14.1 %collective-permute-start.5 = (f32[64,128]{1,0:T(8,128)S(1)}, f32[64,128]{1,0:T(8,128)S(1)}, u32[]{:S(2)}, u32[]{:S(2)}) collective-permute-start(f32[64,128]{1,0:T(8,128)S(1)} %get-tuple-element.25.r0), channel_id=1, source_target_pairs={{3,0},{0,1},{1,2},{2,3},{7,4},{4,5},{5,6},{6,7},{11,8},{8,9},{9,10... | collective-permute-start | bytes 98312 | tf_op jit(solution)/shard_map/ppermute | solution.py:191
  72.9 12.3 %collective-permute-start.4 = (f32[64,128]{1,0:T(8,128)S(1)}, f32[64,128]{1,0:T(8,128)S(1)}, u32[]{:S(2)}, u32[]{:S(2)}) collective-permute-start(f32[64,128]{1,0:T(8,128)S(1)} %get-tuple-element.25.r0), channel_id=1, source_target_pairs={{2,0},{3,1},{0,2},{1,3},{6,4},{7,5},{4,6},{5,7},{10,8},{11,9},{8,1... | collective-permute-start | bytes 98312 | tf_op jit(solution)/shard_map/ppermute | solution.py:191
  74.6 10.6 %collective-permute-start.3 = (f32[64,128]{1,0:T(8,128)S(1)}, f32[64,128]{1,0:T(8,128)S(1)}, u32[]{:S(2)}, u32[]{:S(2)}) collective-permute-start(f32[64,128]{1,0:T(8,128)S(1)} %get-tuple-element.25.r0), channel_id=1, source_target_pairs={{1,0},{2,1},{3,2},{0,3},{5,4},{6,5},{7,6},{4,7},{9,8},{10,9},{11,1... | collective-permute-start | bytes 98312 | tf_op jit(solution)/shard_map/ppermute | solution.py:191
  82.9 3.1 %collective-permute-start.2 = (f32[16,128]{1,0:T(8,128)S(1)}, f32[16,128]{1,0:T(8,128)S(1)}, u32[]{:S(2)}, u32[]{:S(2)}) collective-permute-start(f32[16,128]{1,0:T(8,128)S(1)} %reduce_sum.27.own), channel_id=1, source_target_pairs={{0,4},{4,0},{1,5},{5,1},{2,6},{6,2},{3,7},{7,3},{8,12},{12,8},{9,1... | collective-permute-start | bytes 24584 | tf_op jit(solution)/shard_map/ppermute | solution.py:181
  86.0 3.4 %copy-start = (bf16[256,128,128]{2,1,0:T(8,128)(2,1)S(1)}, bf16[256,128,128]{2,1,0:T(8,128)(2,1)}, u32[]{:S(2)}) copy-start(bf16[256,128,128]{2,1,0:T(8,128)(2,1)} %get-tuple-element.22.scores) | copy-start | bytes 25165828
  94.0 3.5 %collective-permute-start.6 = (f32[16,128]{1,0:T(8,128)S(1)}, f32[16,128]{1,0:T(8,128)S(1)}, u32[]{:S(2)}, u32[]{:S(2)}) collective-permute-start(f32[16,128]{1,0:T(8,128)S(1)} %get-tuple-element.27), channel_id=1, source_target_pairs={{0,4},{4,0},{1,5},{5,1},{2,6},{6,2},{3,7},{7,3},{8,12},{12,8},{9,1... | collective-permute-start | bytes 24584 | tf_op jit(solution)/shard_map/ppermute | solution.py:181
  98.3 15.8 %all-to-all-start.3 = ((f32[32,16,128]{2,1,0:T(8,128)}), f32[32,16,128]{2,1,0:T(8,128)S(1)}, u32[]{:S(2)}, u32[]{:S(2)}) async-start(f32[32,16,128]{2,1,0:T(8,128)} %broadcast_in_dim.13), calls=%async_computation.3 | async-start | bytes 524288 | tf_op jit(solution)/shard_map/all_to_all | solution.py:177
  102.2 14.0 %collective-permute-start.10 = (f32[64,128]{1,0:T(8,128)S(1)}, f32[64,128]{1,0:T(8,128)S(1)}, u32[]{:S(2)}, u32[]{:S(2)}) collective-permute-start(f32[64,128]{1,0:T(8,128)S(1)} %get-tuple-element.28.r0), channel_id=1, source_target_pairs={{3,0},{0,1},{1,2},{2,3},{7,4},{4,5},{5,6},{6,7},{11,8},{8,9},{9,10... | collective-permute-start | bytes 98312 | tf_op jit(solution)/shard_map/ppermute | solution.py:191
  103.4 12.7 %collective-permute-start.9 = (f32[64,128]{1,0:T(8,128)S(1)}, f32[64,128]{1,0:T(8,128)S(1)}, u32[]{:S(2)}, u32[]{:S(2)}) collective-permute-start(f32[64,128]{1,0:T(8,128)S(1)} %get-tuple-element.28.r0), channel_id=1, source_target_pairs={{2,0},{3,1},{0,2},{1,3},{6,4},{7,5},{4,6},{5,7},{10,8},{11,9},{8,1... | collective-permute-start | bytes 98312 | tf_op jit(solution)/shard_map/ppermute | solution.py:191
  105.4 10.7 %collective-permute-start.8 = (f32[64,128]{1,0:T(8,128)S(1)}, f32[64,128]{1,0:T(8,128)S(1)}, u32[]{:S(2)}, u32[]{:S(2)}) collective-permute-start(f32[64,128]{1,0:T(8,128)S(1)} %get-tuple-element.28.r0), channel_id=1, source_target_pairs={{1,0},{2,1},{3,2},{0,3},{5,4},{6,5},{7,6},{4,7},{9,8},{10,9},{11,1... | collective-permute-start | bytes 98312 | tf_op jit(solution)/shard_map/ppermute | solution.py:191
  114.1 2.9 %collective-permute-start.7 = (f32[16,128]{1,0:T(8,128)S(1)}, f32[16,128]{1,0:T(8,128)S(1)}, u32[]{:S(2)}, u32[]{:S(2)}) collective-permute-start(f32[16,128]{1,0:T(8,128)S(1)} %reduce_sum.28.own), channel_id=1, source_target_pairs={{0,4},{4,0},{1,5},{5,1},{2,6},{6,2},{3,7},{7,3},{8,12},{12,8},{9,1... | collective-permute-start | bytes 24584 | tf_op jit(solution)/shard_map/ppermute | solution.py:181
  117.0 3.4 %copy-start.1 = (bf16[256,128,128]{2,1,0:T(8,128)(2,1)S(1)}, bf16[256,128,128]{2,1,0:T(8,128)(2,1)}, u32[]{:S(2)}) copy-start(bf16[256,128,128]{2,1,0:T(8,128)(2,1)} %get-tuple-element.22.scores) | copy-start | bytes 25165828
  125.6 4.2 %collective-permute-start.11 = (f32[16,128]{1,0:T(8,128)S(1)}, f32[16,128]{1,0:T(8,128)S(1)}, u32[]{:S(2)}, u32[]{:S(2)}) collective-permute-start(f32[16,128]{1,0:T(8,128)S(1)} %get-tuple-element.32), channel_id=1, source_target_pairs={{0,4},{4,0},{1,5},{5,1},{2,6},{6,2},{3,7},{7,3},{8,12},{12,8},{9,1... | collective-permute-start | bytes 24584 | tf_op jit(solution)/shard_map/ppermute | solution.py:181
  130.5 15.9 %all-to-all-start.4 = ((f32[32,16,128]{2,1,0:T(8,128)}), f32[32,16,128]{2,1,0:T(8,128)S(1)}, u32[]{:S(2)}, u32[]{:S(2)}) async-start(f32[32,16,128]{2,1,0:T(8,128)} %broadcast_in_dim.14), calls=%async_computation.4 | async-start | bytes 524288 | tf_op jit(solution)/shard_map/all_to_all | solution.py:177
  134.6 14.0 %collective-permute-start.15 = (f32[2,64,128]{2,1,0:T(8,128)S(1)}, f32[2,64,128]{2,1,0:T(8,128)S(1)}, u32[]{:S(2)}, u32[]{:S(2)}) collective-permute-start(f32[2,64,128]{2,1,0:T(8,128)S(1)} %get-tuple-element.33.p0), channel_id=1, source_target_pairs={{3,0},{0,1},{1,2},{2,3},{7,4},{4,5},{5,6},{6,7},{11,8},{8,9},{9,10... | collective-permute-start | bytes 196616 | tf_op jit(solution)/shard_map/ppermute | solution.py:191
  135.4 13.2 %collective-permute-start.14 = (f32[2,64,128]{2,1,0:T(8,128)S(1)}, f32[2,64,128]{2,1,0:T(8,128)S(1)}, u32[]{:S(2)}, u32[]{:S(2)}) collective-permute-start(f32[2,64,128]{2,1,0:T(8,128)S(1)} %get-tuple-element.33.p0), channel_id=1, source_target_pairs={{2,0},{3,1},{0,2},{1,3},{6,4},{7,5},{4,6},{5,7},{10,8},{11,9},{8,1... | collective-permute-start | bytes 196616 | tf_op jit(solution)/shard_map/ppermute | solution.py:191
  137.6 11.0 %collective-permute-start.13 = (f32[2,64,128]{2,1,0:T(8,128)S(1)}, f32[2,64,128]{2,1,0:T(8,128)S(1)}, u32[]{:S(2)}, u32[]{:S(2)}) collective-permute-start(f32[2,64,128]{2,1,0:T(8,128)S(1)} %get-tuple-element.33.p0), channel_id=1, source_target_pairs={{1,0},{2,1},{3,2},{0,3},{5,4},{6,5},{7,6},{4,7},{9,8},{10,9},{11,1... | collective-permute-start | bytes 196616 | tf_op jit(solution)/shard_map/ppermute | solution.py:191
  146.5 2.9 %collective-permute-start.12 = (f32[16,128]{1,0:T(8,128)S(1)}, f32[16,128]{1,0:T(8,128)S(1)}, u32[]{:S(2)}, u32[]{:S(2)}) collective-permute-start(f32[16,128]{1,0:T(8,128)S(1)} %reduce_sum.29.own), channel_id=1, source_target_pairs={{0,4},{4,0},{1,5},{5,1},{2,6},{6,2},{3,7},{7,3},{8,12},{12,8},{9,1... | collective-permute-start | bytes 24584 | tf_op jit(solution)/shard_map/ppermute | solution.py:181

commit v2 on v1

--- a/solution.py
+++ b/solution.py
@@ -12,13 +12,9 @@
 CB = 32
 NZ, NX, NCORE, NCAMP = 8, 4, 2, 4
 UNROLL = 4
+GROUP = 32
+LIMIT = 20 * 2 ** 20
 F32 = jnp.float32
-
-
-def _diagonal():
-    row = lax.broadcasted_iota(jnp.int32, (BLOCK, BLOCK), 0)
-    col = lax.broadcasted_iota(jnp.int32, (BLOCK, BLOCK), 1)
-    return row == col
 
 
 def _clear(lacc, racc):
@@ -47,37 +43,81 @@
 
 
 def _finish_load(lacc, keep, give, core):
-    eye = _diagonal()
+    half = CB // 2
 
     def row(b):
-        total = jnp.sum(lacc[b], axis=1, keepdims=True)
-        return jnp.sum(jnp.where(eye, total, 0.0), axis=0, keepdims=True)
-
-    half = CB // 2
+        return jnp.sum(lacc[b].T, axis=0, keepdims=True)
 
     def turn(b, carry):
         keep[pl.ds(b, 1), :] = row(core * half + b)
         give[pl.ds(b, 1), :] = row((1 - core) * half + b)
         return carry
 
-    lax.fori_loop(0, half, turn, 0, unroll=2)
+    lax.fori_loop(0, half, turn, 0, unroll=4)
+
+
+def _group(ids, cnt, g, size):
+    out = []
+    for k in range(size):
+        slot = g * size + k
+        code = ids[0, slot]
+        out.append((slot, code >> 5, code & (CB - 1), slot < cnt))
+    return out
 
 
 def first_kernel(core, ids, count, users, camps, scores, keep, give, rows, lacc, racc):
     _clear(lacc, racc)
-
-    def one(slot, ub, cb, to_u, to_c):
-        s = lax.dot_general(
-            camps[cb], users[ub], (((1,), (1,)), ((), ())), preferred_element_type=F32
-        ).astype(jnp.bfloat16)
-        scores[slot] = s
-        x = jnp.clip(s.astype(F32), 0.0, 1.0)
-        lacc[to_c] += x
-        racc[to_u] += _fold(x)
-
-    _slots(ids, count, one)
+    cnt = count[0, 0]
+    turns = (cnt + GROUP - 1) // GROUP
+
+    def products(g):
+        return [
+            lax.dot_general(
+                camps[cb], users[ub], (((1,), (1,)), ((), ())), preferred_element_type=F32
+            ).astype(jnp.bfloat16)
+            for _, ub, cb, _ in _group(ids, cnt, g, GROUP)
+        ]
+
+    def store(g, blocks):
+        for k, block in enumerate(blocks):
+            scores[g * GROUP + k] = block
+
+    def add(g):
+        for slot, ub, cb, live in _group(ids, cnt, g, GROUP):
+            x = jnp.clip(scores[slot].astype(F32), 0.0, 1.0)
+            lacc[jnp.where(live, cb, CB)] += x
+            racc[jnp.where(live, ub, UB)] += _fold(x)
+
+    store(0, products(0))
+
+    def turn(g, carry):
+        blocks = products(g)
+        add(g - 1)
+        store(g, blocks)
+        return carry
+
+    lax.fori_loop(1, turns, turn, 0)
+    add(turns - 1)
     _finish_load(lacc, keep, give, core[0])
     rows[...] = racc[:UB].sum(axis=1)
+
+
+def fetch_kernel(users, out, sem):
+    copy = pltpu.make_async_copy(users, out, sem)
+    copy.start()
+    copy.wait()
+
+
+def _fetch(users):
+    return pl.pallas_call(
+        fetch_kernel,
+        in_specs=[pl.BlockSpec(memory_space=pl.ANY)],
+        out_specs=VMEM,
+        out_shape=jax.ShapeDtypeStruct(users.shape, users.dtype),
+        scratch_shapes=[pltpu.SemaphoreType.DMA],
+        compiler_params=pltpu.CompilerParams(vmem_limit_bytes=LIMIT),
+        cost_estimate=pl.CostEstimate(flops=0, bytes_accessed=2 * users.size * 2, transcendentals=0),
+    )(users)
 
 
 def _load_of(own, other, core):
@@ -108,10 +148,8 @@
     mu_out[...] = mu_new
     lam_bar = 2.0 * lam_new - lam
     mub[:UB] = (2.0 * mu_new - mu)[:, None, :]
-    eye = _diagonal()
     for b in range(CB):
-        spread = jnp.where(eye, lam_bar[b:b + 1, :], 0.0)
-        lamb[b] = jnp.broadcast_to(jnp.sum(spread, axis=1, keepdims=True), (BLOCK, BLOCK))
+        lamb[b] = jnp.broadcast_to(lam_bar[b:b + 1, :], (BLOCK, BLOCK)).T
 
     def one(slot, ub, cb, to_u, to_c):
         s = scores[slot].astype(F32)
@@ -160,7 +198,7 @@
         out_specs=[VMEM] * len(outs),
         out_shape=[jax.ShapeDtypeStruct(s, d) for s, d in outs],
         scratch_shapes=[pltpu.VMEM(s, F32) for s in scratch],
-        compiler_params=pltpu.CompilerParams(vmem_limit_bytes=40 * 2 ** 20),
+        compiler_params=pltpu.CompilerParams(vmem_limit_bytes=LIMIT),
     )(*args)
 
 
@@ -202,6 +240,8 @@
     users = user_emb.reshape(UB, BLOCK, E)
 
     part = _spread(camp_emb, "z", NZ)
+    part, users = lax.optimization_barrier((part, users))
+    users = _fetch(users)
     part = _spread(part.reshape(NZ, 64, E), "x", NX).reshape(NX, NZ, 64, E)
     peer = _swap(part)
     first = core == 0

time: 151 us -> 140 us (0.927)
  waiting for transfers between devices: 30 us -> 23.5 us
  starting transfers between devices: 48.6 us -> 43.9 us
  local copies, waits for them, and re-layouts: 12 us -> 16 us
  Pallas kernels: 22.6 us -> 19.2 us
    ppermute x7, starting transfers between devices: 24.6 us -> 12.2 us  [_swap(): return lax.ppermute(x, 'core', [(0, 1), (1, 0)])]
    all_to_all x3, waiting for transfers between devices: 23.4 us -> 18.2 us  [_spread(): lax.all_to_all(jnp.broadcast_to(x[None], (n,) + x.shape), axes, 0, 0, til...]
    ppermute x9, starting transfers between devices: 12.2 us -> 17.3 us  [_shift(): return lax.ppermute(x, 'camp', [((i + k) % NCAMP, i) for i in range(NCAMP)])]
    unnamed x12 -> x14, local copies, waits for them, and re-layouts: 8.7 us -> 12.6 us
    pallas_call x4, Pallas kernels: 22.6 us -> 18.9 us  [_call(): pl.pallas_call(kernel, in_specs=[SMEM] * n_smem + [VMEM] * (len(args) - n...]
    all_to_all x3, starting transfers between devices: 11.8 us -> 14.4 us  [_spread(): lax.all_to_all(jnp.broadcast_to(x[None], (n,) + x.shape), axes, 0, 0, til...]
  transfers between devices with their start and end apart: 19 -> 19, of which waited for: 10 -> 9; matrix products, arithmetic and copies ran while one was open for 0% -> 0% of each run, Pallas kernels for 0% -> 0%
where the time goes in v2:
time: 140 us; the launch traced here: 139 us
  starting transfers between devices  43.9 us (31%)
  blocking collectives  35.1 us (25%)
  waiting for transfers between devices  23.5 us (17%)
  Pallas kernels  19.2 us (14%)
  local copies, waits for them, and re-layouts  16 us (11%)
  between operations  1.45 us (1%)
    all_to_all x2, blocking collectives, _spread(): lax.all_to_all(jnp.broadcast_to(x[None], (n,) + x.shape), axes, 0, 0, til...  35.1 us
    pallas_call x4, Pallas kernels, _call(): pl.pallas_call(kernel, in_specs=[SMEM] * n_smem + [VMEM] * (len(args) - n...  18.9 us
    all_to_all x3, waiting for transfers between devices, _spread(): lax.all_to_all(jnp.broadcast_to(x[None], (n,) + x.shape), axes, 0, 0, til...  18.2 us
    ppermute x9, starting transfers between devices, _shift(): return lax.ppermute(x, 'camp', [((i + k) % NCAMP, i) for i in range(NCAMP)])  17.3 us
    all_to_all x3, starting transfers between devices, _spread(): lax.all_to_all(jnp.broadcast_to(x[None], (n,) + x.shape), axes, 0, 0, til...  14.4 us
    unnamed x14, local copies, waits for them, and re-layouts  12.6 us
    ppermute x7, starting transfers between devices, _swap(): return lax.ppermute(x, 'core', [(0, 1), (1, 0)])  12.2 us
    ppermute x7, waiting for transfers between devices, _swap(): return lax.ppermute(x, 'core', [(0, 1), (1, 0)])  5.28 us
  transfers between devices with their start and end apart: 19, of which 9 were waited for; matrix products, arithmetic and copies ran while one was open for 0% of the time, Pallas kernels for 0%

profile of v2, /device:TPU:1, one launch (start us, length us, event | category | flops | bytes accessed | tf_op | source)
XLA Modules:
  0.0 139.5 jit_solution(3741314190639281231)
XLA Ops:
  1.4 19.2 %all_to_all.25 = bf16[8,64,256]{2,1,0:T(8,128)(2,1)S(1)} all-to-all(bf16[8,64,256]{2,1,0:T(8,128)(2,1)S(1)} %broadcast_in_dim.10), channel_id=1, replica_groups=mesh['z'=8,'x'=4,'core'=2,'camp'=4] {'z'}, dimensions={0} | all-to-all | bytes 524288 | tf_op jit(solution)/shard_map/all_to_all | solution.py:215
  20.7 15.9 %all_to_all.26 = bf16[4,8,64,256]{3,2,1,0:T(8,128)(2,1)S(1)} all-to-all(bf16[4,8,64,256]{3,2,1,0:T(8,128)(2,1)S(1)} %broadcast_in_dim.11), channel_id=1, replica_groups=mesh['z'=8,'x'=4,'core'=2,'camp'=4] {'x'}, dimensions={0} | all-to-all | bytes 2097152 | tf_op jit(solution)/shard_map/all_to_all | solution.py:215
  36.6 4.0 %collective-permute-start = (bf16[4,8,64,256]{3,2,1,0:T(8,128)(2,1)S(1)}, bf16[4,8,64,256]{3,2,1,0:T(8,128)(2,1)S(1)}, u32[]{:S(2)}, u32[]{:S(2)}) collective-permute-start(bf16[4,8,64,256]{3,2,1,0:T(8,128)(2,1)S(1)} %all_to_all.26), channel_id=1, source_target_pairs={{0,4},{4,0},{1,5},{5,1},{2,6},{6,2},{3,7},{7,3},{8,12},{12,8},{9,1... | collective-permute-start | bytes 3145736 | tf_op jit(solution)/shard_map/ppermute | solution.py:219
  41.2 2.2 %copy-done.3 = bf16[8192,256]{1,0:T(8,128)(2,1)S(1)} copy-done((bf16[8192,256]{1,0:T(8,128)(2,1)S(1)}, bf16[8192,256]{1,0:T(8,128)(2,1)}, u32[]{:S(2)}) %copy-start.3) | copy-done | bytes 4194328
  44.8 7.0 %shard_map.94 = (bf16[256,128,128]{2,1,0:T(8,128)(2,1)S(1)}, f32[16,128]{1,0:T(8,128)S(1)}, f32[16,128]{1,0:T(8,128)S(1)}, f32[64,128]{1,0:T(8,128)S(1)}) custom-call(s32[1]{0:T(128)} %bitcast.core, s32[1,256]{1,0:T(1,128)S(1)} %copy-done.6, s32[1,1]{1,0:T(1,128)S(6)} %copy.13.count, bf16[64,128,256]{2,1,0:T(8,128)(2,1)S(1)} %shard_map.93.users, ...), custom_call_target="tpu_custom_call" | custom-call | tf_op jit(solution)/shard_map/pallas_call | solution.py:195
  51.8 3.3 %copy-done = bf16[256,128,128]{2,1,0:T(8,128)(2,1)} copy-done((bf16[256,128,128]{2,1,0:T(8,128)(2,1)}, bf16[256,128,128]{2,1,0:T(8,128)(2,1)S(1)}, u32[]{:S(2)}) %copy-start) | copy-done | bytes 8388632
  55.0 1.2 collective-permute-done.1
  56.9 4.8 %all-to-all-start.2 = ((f32[32,16,128]{2,1,0:T(8,128)}), f32[32,16,128]{2,1,0:T(8,128)S(1)}, u32[]{:S(2)}, u32[]{:S(2)}) async-start(f32[32,16,128]{2,1,0:T(8,128)} %broadcast_in_dim.12), calls=%async_computation.2 | async-start | bytes 524288 | tf_op jit(solution)/shard_map/all_to_all | solution.py:215
  61.7 2.0 %collective-permute-start.5 = (f32[64,128]{1,0:T(8,128)S(1)}, f32[64,128]{1,0:T(8,128)S(1)}, u32[]{:S(2)}, u32[]{:S(2)}) collective-permute-start(f32[64,128]{1,0:T(8,128)S(1)} %get-tuple-element.29.r0), channel_id=1, source_target_pairs={{3,0},{0,1},{1,2},{2,3},{7,4},{4,5},{5,6},{6,7},{11,8},{8,9},{9,10... | collective-permute-start | bytes 98312 | tf_op jit(solution)/shard_map/ppermute | solution.py:229
  63.7 2.6 %collective-permute-start.4 = (f32[64,128]{1,0:T(8,128)S(1)}, f32[64,128]{1,0:T(8,128)S(1)}, u32[]{:S(2)}, u32[]{:S(2)}) collective-permute-start(f32[64,128]{1,0:T(8,128)S(1)} %get-tuple-element.29.r0), channel_id=1, source_target_pairs={{2,0},{3,1},{0,2},{1,3},{6,4},{7,5},{4,6},{5,7},{10,8},{11,9},{8,1... | collective-permute-start | bytes 98312 | tf_op jit(solution)/shard_map/ppermute | solution.py:229
  66.3 1.1 collective-permute-start.3
  67.4 6.2 %all-to-all-done.2 = f32[32,16,128]{2,1,0:T(8,128)S(1)} async-done(((f32[32,16,128]{2,1,0:T(8,128)}), f32[32,16,128]{2,1,0:T(8,128)S(1)}, u32[]{:S(2)}, u32[]{:S(2)}) %all-to-all-start.2) | async-done | bytes 262176 | tf_op jit(solution)/shard_map/all_to_all | solution.py:215
  73.6 2.2 %collective-permute-start.2 = (f32[16,128]{1,0:T(8,128)S(1)}, f32[16,128]{1,0:T(8,128)S(1)}, u32[]{:S(2)}, u32[]{:S(2)}) collective-permute-start(f32[16,128]{1,0:T(8,128)S(1)} %reduce_sum.27.own), channel_id=1, source_target_pairs={{0,4},{4,0},{1,5},{5,1},{2,6},{6,2},{3,7},{7,3},{8,12},{12,8},{9,1... | collective-permute-start | bytes 24584 | tf_op jit(solution)/shard_map/ppermute | solution.py:219
  75.8 0.8 collective-permute-done.2.other
  76.7 3.4 %copy-done.1 = bf16[256,128,128]{2,1,0:T(8,128)(2,1)S(1)} copy-done((bf16[256,128,128]{2,1,0:T(8,128)(2,1)S(1)}, bf16[256,128,128]{2,1,0:T(8,128)(2,1)}, u32[]{:S(2)}) %copy-start.1) | copy-done | bytes 8388632
  80.0 5.1 %shard_map.95 = (f32[16,128]{1,0:T(8,128)S(1)}, f32[16,128]{1,0:T(8,128)S(1)}, f32[64,128]{1,0:T(8,128)S(1)}, f32[32,128]{1,0:T(8,128)S(1)}, f32[64,128]{1,0:T(8,128)S(1)}) custom-call(s32[1]{0:T(128)} %bitcast.core, s32[1,256]{1,0:T(1,128)S(1)} %copy-done.6, s32[1,1]{1,0:T(1,128)S(6)} %copy.13.count, bf16[256,128,128]{2,1,0:T(8,128)(2,1)S(1)} %copy-done.1, ...), custom_call_target="tpu_custom_call" | custom-call | tf_op jit(solution)/shard_map/pallas_call | solution.py:195
  85.8 0.8 collective-permute-done.6
  87.4 4.6 %all-to-all-start.3 = ((f32[32,16,128]{2,1,0:T(8,128)}), f32[32,16,128]{2,1,0:T(8,128)S(1)}, u32[]{:S(2)}, u32[]{:S(2)}) async-start(f32[32,16,128]{2,1,0:T(8,128)} %broadcast_in_dim.13), calls=%async_computation.3 | async-start | bytes 524288 | tf_op jit(solution)/shard_map/all_to_all | solution.py:215
  92.0 1.5 %collective-permute-start.10 = (f32[64,128]{1,0:T(8,128)S(1)}, f32[64,128]{1,0:T(8,128)S(1)}, u32[]{:S(2)}, u32[]{:S(2)}) collective-permute-start(f32[64,128]{1,0:T(8,128)S(1)} %get-tuple-element.32.r0), channel_id=1, source_target_pairs={{3,0},{0,1},{1,2},{2,3},{7,4},{4,5},{5,6},{6,7},{11,8},{8,9},{9,10... | collective-permute-start | bytes 98312 | tf_op jit(solution)/shard_map/ppermute | solution.py:229
  93.5 2.6 %collective-permute-start.9 = (f32[64,128]{1,0:T(8,128)S(1)}, f32[64,128]{1,0:T(8,128)S(1)}, u32[]{:S(2)}, u32[]{:S(2)}) collective-permute-start(f32[64,128]{1,0:T(8,128)S(1)} %get-tuple-element.32.r0), channel_id=1, source_target_pairs={{2,0},{3,1},{0,2},{1,3},{6,4},{7,5},{4,6},{5,7},{10,8},{11,9},{8,1... | collective-permute-start | bytes 98312 | tf_op jit(solution)/shard_map/ppermute | solution.py:229
  96.1 1.7 %collective-permute-start.8 = (f32[64,128]{1,0:T(8,128)S(1)}, f32[64,128]{1,0:T(8,128)S(1)}, u32[]{:S(2)}, u32[]{:S(2)}) collective-permute-start(f32[64,128]{1,0:T(8,128)S(1)} %get-tuple-element.32.r0), channel_id=1, source_target_pairs={{1,0},{2,1},{3,2},{0,3},{5,4},{6,5},{7,6},{4,7},{9,8},{10,9},{11,1... | collective-permute-start | bytes 98312 | tf_op jit(solution)/shard_map/ppermute | solution.py:229
  97.8 6.0 %all-to-all-done.3 = f32[32,16,128]{2,1,0:T(8,128)S(1)} async-done(((f32[32,16,128]{2,1,0:T(8,128)}), f32[32,16,128]{2,1,0:T(8,128)S(1)}, u32[]{:S(2)}, u32[]{:S(2)}) %all-to-all-start.3) | async-done | bytes 262176 | tf_op jit(solution)/shard_map/all_to_all | solution.py:215
  103.9 2.4 %collective-permute-start.7 = (f32[16,128]{1,0:T(8,128)S(1)}, f32[16,128]{1,0:T(8,128)S(1)}, u32[]{:S(2)}, u32[]{:S(2)}) collective-permute-start(f32[16,128]{1,0:T(8,128)S(1)} %reduce_sum.28.own), channel_id=1, source_target_pairs={{0,4},{4,0},{1,5},{5,1},{2,6},{6,2},{3,7},{7,3},{8,12},{12,8},{9,1... | collective-permute-start | bytes 24584 | tf_op jit(solution)/shard_map/ppermute | solution.py:219
  107.1 3.4 %copy-done.2 = bf16[256,128,128]{2,1,0:T(8,128)(2,1)S(1)} copy-done((bf16[256,128,128]{2,1,0:T(8,128)(2,1)S(1)}, bf16[256,128,128]{2,1,0:T(8,128)(2,1)}, u32[]{:S(2)}) %copy-start.2) | copy-done | bytes 8388632
  110.5 6.1 %shard_map.96 = (f32[16,128]{1,0:T(8,128)S(1)}, f32[16,128]{1,0:T(8,128)S(1)}, f32[2,64,128]{2,1,0:T(8,128)S(1)}, f32[32,128]{1,0:T(8,128)S(1)}, f32[64,128]{1,0:T(8,128)S(1)}) custom-call(s32[1]{0:T(128)} %bitcast.core, s32[1,256]{1,0:T(1,128)S(1)} %copy-done.6, s32[1,1]{1,0:T(1,128)S(6)} %copy.13.count, bf16[256,128,128]{2,1,0:T(8,128)(2,1)S(1)} %copy-done.2, ...), custom_call_target="tpu_custom_call" | custom-call | tf_op jit(solution)/shard_map/pallas_call | solution.py:195
  117.3 0.8 collective-permute-done.11
  118.9 5.0 %all-to-all-start.4 = ((f32[32,16,128]{2,1,0:T(8,128)}), f32[32,16,128]{2,1,0:T(8,128)S(1)}, u32[]{:S(2)}, u32[]{:S(2)}) async-start(f32[32,16,128]{2,1,0:T(8,128)} %broadcast_in_dim.14), calls=%async_computation.4 | async-start | bytes 524288 | tf_op jit(solution)/shard_map/all_to_all | solution.py:215
  123.9 1.0 collective-permute-start.15
  124.9 2.9 %collective-permute-start.14 = (f32[2,64,128]{2,1,0:T(8,128)S(1)}, f32[2,64,128]{2,1,0:T(8,128)S(1)}, u32[]{:S(2)}, u32[]{:S(2)}) collective-permute-start(f32[2,64,128]{2,1,0:T(8,128)S(1)} %get-tuple-element.37.p0), channel_id=1, source_target_pairs={{2,0},{3,1},{0,2},{1,3},{6,4},{7,5},{4,6},{5,7},{10,8},{11,9},{8,1... | collective-permute-start | bytes 196616 | tf_op jit(solution)/shard_map/ppermute | solution.py:229
  127.7 2.0 %collective-permute-start.13 = (f32[2,64,128]{2,1,0:T(8,128)S(1)}, f32[2,64,128]{2,1,0:T(8,128)S(1)}, u32[]{:S(2)}, u32[]{:S(2)}) collective-permute-start(f32[2,64,128]{2,1,0:T(8,128)S(1)} %get-tuple-element.37.p0), channel_id=1, source_target_pairs={{1,0},{2,1},{3,2},{0,3},{5,4},{6,5},{7,6},{4,7},{9,8},{10,9},{11,1... | collective-permute-start | bytes 196616 | tf_op jit(solution)/shard_map/ppermute | solution.py:229
  129.7 6.0 %all-to-all-done.4 = f32[32,16,128]{2,1,0:T(8,128)S(1)} async-done(((f32[32,16,128]{2,1,0:T(8,128)}), f32[32,16,128]{2,1,0:T(8,128)S(1)}, u32[]{:S(2)}, u32[]{:S(2)}) %all-to-all-start.4) | async-done | bytes 262176 | tf_op jit(solution)/shard_map/all_to_all | solution.py:215
  135.7 2.2 %collective-permute-start.12 = (f32[16,128]{1,0:T(8,128)S(1)}, f32[16,128]{1,0:T(8,128)S(1)}, u32[]{:S(2)}, u32[]{:S(2)}) collective-permute-start(f32[16,128]{1,0:T(8,128)S(1)} %reduce_sum.29.own), channel_id=1, source_target_pairs={{0,4},{4,0},{1,5},{5,1},{2,6},{6,2},{3,7},{7,3},{8,12},{12,8},{9,1... | collective-permute-start | bytes 24584 | tf_op jit(solution)/shard_map/ppermute | solution.py:219
  (41 shorter events, 8.2 us)
Async XLA Ops:
  36.6 7.1 %collective-permute-start = (bf16[4,8,64,256]{3,2,1,0:T(8,128)(2,1)S(1)}, bf16[4,8,64,256]{3,2,1,0:T(8,128)(2,1)S(1)}, u32[]{:S(2)}, u32[]{:S(2)}) collective-permute-start(bf16[4,8,64,256]{3,2,1,0:T(8,128)(2,1)S(1)} %all_to_all.26), channel_id=1, source_target_pairs={{0,4},{4,0},{1,5},{5,1},{2,6},{6,2},{3,7},{7,3},{8,12},{12,8},{9,1... | collective-permute-start | bytes 3145736 | tf_op jit(solution)/shard_map/ppermute | solution.py:219
  41.2 2.2 %copy-start.3 = (bf16[8192,256]{1,0:T(8,128)(2,1)S(1)}, bf16[8192,256]{1,0:T(8,128)(2,1)}, u32[]{:S(2)}) copy-start(bf16[8192,256]{1,0:T(8,128)(2,1)} %param.6) | copy-start | bytes 12582916
  44.1 0.7 copy-start.6
  44.8 31.9 %copy-start.4 = (s32[8192]{0:T(1024)S(1)}, s32[8192]{0:T(1024)}, u32[]{:S(2)}) copy-start(s32[8192]{0:T(1024)} %param.11) | copy-start | bytes 98308
  44.8 31.9 %copy-start.5 = (s32[4096]{0:T(1024)S(1)}, s32[4096]{0:T(1024)}, u32[]{:S(2)}) copy-start(s32[4096]{0:T(1024)} %param.10) | copy-start | bytes 49156
  51.8 3.3 %copy-start = (bf16[256,128,128]{2,1,0:T(8,128)(2,1)}, bf16[256,128,128]{2,1,0:T(8,128)(2,1)S(1)}, u32[]{:S(2)}) copy-start(bf16[256,128,128]{2,1,0:T(8,128)(2,1)S(1)} %get-tuple-element.26.scores) | copy-start | bytes 25165828
  55.0 1.2 collective-permute-start.1
  56.9 16.6 %all-to-all-start.2 = ((f32[32,16,128]{2,1,0:T(8,128)}), f32[32,16,128]{2,1,0:T(8,128)S(1)}, u32[]{:S(2)}, u32[]{:S(2)}) async-start(f32[32,16,128]{2,1,0:T(8,128)} %broadcast_in_dim.12), calls=%async_computation.2 | async-start | bytes 524288 | tf_op jit(solution)/shard_map/all_to_all | solution.py:215
  61.7 14.1 %collective-permute-start.5 = (f32[64,128]{1,0:T(8,128)S(1)}, f32[64,128]{1,0:T(8,128)S(1)}, u32[]{:S(2)}, u32[]{:S(2)}) collective-permute-start(f32[64,128]{1,0:T(8,128)S(1)} %get-tuple-element.29.r0), channel_id=1, source_target_pairs={{3,0},{0,1},{1,2},{2,3},{7,4},{4,5},{5,6},{6,7},{11,8},{8,9},{9,10... | collective-permute-start | bytes 98312 | tf_op jit(solution)/shard_map/ppermute | solution.py:229
  63.7 12.1 %collective-permute-start.4 = (f32[64,128]{1,0:T(8,128)S(1)}, f32[64,128]{1,0:T(8,128)S(1)}, u32[]{:S(2)}, u32[]{:S(2)}) collective-permute-start(f32[64,128]{1,0:T(8,128)S(1)} %get-tuple-element.29.r0), channel_id=1, source_target_pairs={{2,0},{3,1},{0,2},{1,3},{6,4},{7,5},{4,6},{5,7},{10,8},{11,9},{8,1... | collective-permute-start | bytes 98312 | tf_op jit(solution)/shard_map/ppermute | solution.py:229
  66.3 9.5 %collective-permute-start.3 = (f32[64,128]{1,0:T(8,128)S(1)}, f32[64,128]{1,0:T(8,128)S(1)}, u32[]{:S(2)}, u32[]{:S(2)}) collective-permute-start(f32[64,128]{1,0:T(8,128)S(1)} %get-tuple-element.29.r0), channel_id=1, source_target_pairs={{1,0},{2,1},{3,2},{0,3},{5,4},{6,5},{7,6},{4,7},{9,8},{10,9},{11,1... | collective-permute-start | bytes 98312 | tf_op jit(solution)/shard_map/ppermute | solution.py:229
  73.6 3.1 %collective-permute-start.2 = (f32[16,128]{1,0:T(8,128)S(1)}, f32[16,128]{1,0:T(8,128)S(1)}, u32[]{:S(2)}, u32[]{:S(2)}) collective-permute-start(f32[16,128]{1,0:T(8,128)S(1)} %reduce_sum.27.own), channel_id=1, source_target_pairs={{0,4},{4,0},{1,5},{5,1},{2,6},{6,2},{3,7},{7,3},{8,12},{12,8},{9,1... | collective-permute-start | bytes 24584 | tf_op jit(solution)/shard_map/ppermute | solution.py:219
  76.7 3.4 %copy-start.1 = (bf16[256,128,128]{2,1,0:T(8,128)(2,1)S(1)}, bf16[256,128,128]{2,1,0:T(8,128)(2,1)}, u32[]{:S(2)}) copy-start(bf16[256,128,128]{2,1,0:T(8,128)(2,1)} %copy-done) | copy-start | bytes 25165828
  85.2 1.5 %collective-permute-start.6 = (f32[16,128]{1,0:T(8,128)S(1)}, f32[16,128]{1,0:T(8,128)S(1)}, u32[]{:S(2)}, u32[]{:S(2)}) collective-permute-start(f32[16,128]{1,0:T(8,128)S(1)} %get-tuple-element.31), channel_id=1, source_target_pairs={{0,4},{4,0},{1,5},{5,1},{2,6},{6,2},{3,7},{7,3},{8,12},{12,8},{9,1... | collective-permute-start | bytes 24584 | tf_op jit(solution)/shard_map/ppermute | solution.py:219
  87.4 16.5 %all-to-all-start.3 = ((f32[32,16,128]{2,1,0:T(8,128)}), f32[32,16,128]{2,1,0:T(8,128)S(1)}, u32[]{:S(2)}, u32[]{:S(2)}) async-start(f32[32,16,128]{2,1,0:T(8,128)} %broadcast_in_dim.13), calls=%async_computation.3 | async-start | bytes 524288 | tf_op jit(solution)/shard_map/all_to_all | solution.py:215
  92.0 14.3 %collective-permute-start.10 = (f32[64,128]{1,0:T(8,128)S(1)}, f32[64,128]{1,0:T(8,128)S(1)}, u32[]{:S(2)}, u32[]{:S(2)}) collective-permute-start(f32[64,128]{1,0:T(8,128)S(1)} %get-tuple-element.32.r0), channel_id=1, source_target_pairs={{3,0},{0,1},{1,2},{2,3},{7,4},{4,5},{5,6},{6,7},{11,8},{8,9},{9,10... | collective-permute-start | bytes 98312 | tf_op jit(solution)/shard_map/ppermute | solution.py:229
  93.5 12.8 %collective-permute-start.9 = (f32[64,128]{1,0:T(8,128)S(1)}, f32[64,128]{1,0:T(8,128)S(1)}, u32[]{:S(2)}, u32[]{:S(2)}) collective-permute-start(f32[64,128]{1,0:T(8,128)S(1)} %get-tuple-element.32.r0), channel_id=1, source_target_pairs={{2,0},{3,1},{0,2},{1,3},{6,4},{7,5},{4,6},{5,7},{10,8},{11,9},{8,1... | collective-permute-start | bytes 98312 | tf_op jit(solution)/shard_map/ppermute | solution.py:229
  96.1 10.2 %collective-permute-start.8 = (f32[64,128]{1,0:T(8,128)S(1)}, f32[64,128]{1,0:T(8,128)S(1)}, u32[]{:S(2)}, u32[]{:S(2)}) collective-permute-start(f32[64,128]{1,0:T(8,128)S(1)} %get-tuple-element.32.r0), channel_id=1, source_target_pairs={{1,0},{2,1},{3,2},{0,3},{5,4},{6,5},{7,6},{4,7},{9,8},{10,9},{11,1... | collective-permute-start | bytes 98312 | tf_op jit(solution)/shard_map/ppermute | solution.py:229
  103.9 3.3 %collective-permute-start.7 = (f32[16,128]{1,0:T(8,128)S(1)}, f32[16,128]{1,0:T(8,128)S(1)}, u32[]{:S(2)}, u32[]{:S(2)}) collective-permute-start(f32[16,128]{1,0:T(8,128)S(1)} %reduce_sum.28.own), channel_id=1, source_target_pairs={{0,4},{4,0},{1,5},{5,1},{2,6},{6,2},{3,7},{7,3},{8,12},{12,8},{9,1... | collective-permute-start | bytes 24584 | tf_op jit(solution)/shard_map/ppermute | solution.py:219
  107.1 3.4 %copy-start.2 = (bf16[256,128,128]{2,1,0:T(8,128)(2,1)S(1)}, bf16[256,128,128]{2,1,0:T(8,128)(2,1)}, u32[]{:S(2)}) copy-start(bf16[256,128,128]{2,1,0:T(8,128)(2,1)} %copy-done) | copy-start | bytes 25165828
  116.6 1.5 %collective-permute-start.11 = (f32[16,128]{1,0:T(8,128)S(1)}, f32[16,128]{1,0:T(8,128)S(1)}, u32[]{:S(2)}, u32[]{:S(2)}) collective-permute-start(f32[16,128]{1,0:T(8,128)S(1)} %get-tuple-element.36), channel_id=1, source_target_pairs={{0,4},{4,0},{1,5},{5,1},{2,6},{6,2},{3,7},{7,3},{8,12},{12,8},{9,1... | collective-permute-start | bytes 24584 | tf_op jit(solution)/shard_map/ppermute | solution.py:219
  118.9 16.8 %all-to-all-start.4 = ((f32[32,16,128]{2,1,0:T(8,128)}), f32[32,16,128]{2,1,0:T(8,128)S(1)}, u32[]{:S(2)}, u32[]{:S(2)}) async-start(f32[32,16,128]{2,1,0:T(8,128)} %broadcast_in_dim.14), calls=%async_computation.4 | async-start | bytes 524288 | tf_op jit(solution)/shard_map/all_to_all | solution.py:215
  123.9 14.1 %collective-permute-start.15 = (f32[2,64,128]{2,1,0:T(8,128)S(1)}, f32[2,64,128]{2,1,0:T(8,128)S(1)}, u32[]{:S(2)}, u32[]{:S(2)}) collective-permute-start(f32[2,64,128]{2,1,0:T(8,128)S(1)} %get-tuple-element.37.p0), channel_id=1, source_target_pairs={{3,0},{0,1},{1,2},{2,3},{7,4},{4,5},{5,6},{6,7},{11,8},{8,9},{9,10... | collective-permute-start | bytes 196616 | tf_op jit(solution)/shard_map/ppermute | solution.py:229
  124.9 13.1 %collective-permute-start.14 = (f32[2,64,128]{2,1,0:T(8,128)S(1)}, f32[2,64,128]{2,1,0:T(8,128)S(1)}, u32[]{:S(2)}, u32[]{:S(2)}) collective-permute-start(f32[2,64,128]{2,1,0:T(8,128)S(1)} %get-tuple-element.37.p0), channel_id=1, source_target_pairs={{2,0},{3,1},{0,2},{1,3},{6,4},{7,5},{4,6},{5,7},{10,8},{11,9},{8,1... | collective-permute-start | bytes 196616 | tf_op jit(solution)/shard_map/ppermute | solution.py:229
  127.7 10.3 %collective-permute-start.13 = (f32[2,64,128]{2,1,0:T(8,128)S(1)}, f32[2,64,128]{2,1,0:T(8,128)S(1)}, u32[]{:S(2)}, u32[]{:S(2)}) collective-permute-start(f32[2,64,128]{2,1,0:T(8,128)S(1)} %get-tuple-element.37.p0), channel_id=1, source_target_pairs={{1,0},{2,1},{3,2},{0,3},{5,4},{6,5},{7,6},{4,7},{9,8},{10,9},{11,1... | collective-permute-start | bytes 196616 | tf_op jit(solution)/shard_map/ppermute | solution.py:229
  135.7 3.1 %collective-permute-start.12 = (f32[16,128]{1,0:T(8,128)S(1)}, f32[16,128]{1,0:T(8,128)S(1)}, u32[]{:S(2)}, u32[]{:S(2)}) collective-permute-start(f32[16,128]{1,0:T(8,128)S(1)} %reduce_sum.29.own), channel_id=1, source_target_pairs={{0,4},{4,0},{1,5},{5,1},{2,6},{6,2},{3,7},{7,3},{8,12},{12,8},{9,1... | collective-permute-start | bytes 24584 | tf_op jit(solution)/shard_map/ppermute | solution.py:219

commit v3 on v2

v3 whole, which is shorter than its diff:
```python
import jax
import jax.numpy as jnp
from jax import lax
from jax.experimental import pallas as pl
from jax.experimental.pallas import tpu as pltpu
from jax.sharding import Mesh, PartitionSpec as P

BLOCK = 128
E = 256
SLOTS = 256
UB = 64
CB = 32
NZ, NX, NCORE, NCAMP = 8, 4, 2, 4
UNROLL = 4
GROUP = 32
WIDE = 50
F32 = jnp.float32


def _clear(lacc, racc):
    lacc[...] = jnp.zeros_like(lacc)
    racc[...] = jnp.zeros_like(racc)


def _chunk(src, dst, sems, g):
    at = pl.ds(g * GROUP, GROUP)
    return pltpu.make_async_copy(src.at[at], dst.at[at], sems.at[g])


def _each(turns, do):
    def turn(g, carry):
        do(g)
        return carry

    lax.fori_loop(0, turns, turn, 0)


def _fold(x):
    return x.reshape(BLOCK // 8, 8, BLOCK).sum(0)


def _finish_load(lacc, keep, give, core):
    half = CB // 2

    def row(b):
        return jnp.sum(lacc[b].T, axis=0, keepdims=True)

    def turn(b, carry):
        keep[pl.ds(b, 1), :] = row(core * half + b)
        give[pl.ds(b, 1), :] = row((1 - core) * half + b)
        return carry

    lax.fori_loop(0, half, turn, 0, unroll=4)


def _group(ids, cnt, first, size):
    out = []
    for k in range(size):
        slot = first + k
        code = ids[0, slot]
        out.append((slot, code >> 5, code & (CB - 1), slot < cnt))
    return out


def first_kernel(core, ids, count, part, peer, users_in, kept, keep, give, rows, lacc, racc, panel, users, scores,
                 sems, fetched, stored):
    me = core[0]
    fetch = pltpu.make_async_copy(users_in, users, fetched)
    fetch.start()
    copies = [
        pltpu.make_async_copy(src.at[x], panel.at[:, x, half], sems.at[x, k])
        for x in range(NX)
        for k, (src, half) in enumerate(((part, me), (peer, 1 - me)))
    ]
    for copy in copies:
        copy.start()
    _clear(lacc, racc)
    for copy in copies:
        copy.wait()
    fetch.wait()
    camps = panel.reshape(CB, BLOCK, E)
    cnt = count[0, 0]
    turns = (cnt + GROUP - 1) // GROUP

    def products(g):
        return [
            lax.dot_general(
                camps[cb], users[ub], (((1,), (1,)), ((), ())), preferred_element_type=F32
            ).astype(jnp.bfloat16)
            for _, ub, cb, _ in _group(ids, cnt, g * GROUP, GROUP)
        ]

    def store(g, blocks):
        for k, block in enumerate(blocks):
            scores[g * GROUP + k] = block
        _chunk(scores, kept, stored, g).start()

    def add(g):
        for slot, ub, cb, live in _group(ids, cnt, g * GROUP, GROUP):
            x = jnp.clip(scores[slot].astype(F32), 0.0, 1.0)
            lacc[jnp.where(live, cb, CB)] += x
            racc[jnp.where(live, ub, UB)] += _fold(x)

    store(0, products(0))

    def turn(g, carry):
        blocks = products(g)
        add(g - 1)
        store(g, blocks)
        return carry

    lax.fori_loop(1, turns, turn, 0)
    add(turns - 1)
    _finish_load(lacc, keep, give, core[0])
    rows[...] = racc[:UB].sum(axis=1)
    _each(turns, lambda g: _chunk(scores, kept, stored, g).wait())


def _load_of(own, other, core):
    a, b = own[...], other[...]
    first = core == 0
    return jnp.concatenate([jnp.where(first, a, b), jnp.where(first, b, a)], axis=0)


def _duals(core, own, other, r0, r1, r2, r3, cap_i, lim_i, lam_in, mu_in):
    load = _load_of(own, other, core)
    rows = (r0[...] + r2[...]) + (r1[...] + r3[...])
    cap = cap_i[...].astype(F32)
    lim = lim_i[...].astype(F32)
    lam_new = jnp.maximum(0.0, lam_in + (load - cap) / cap)
    mu_new = jnp.maximum(0.0, mu_in + (rows - lim) / lim)
    return load, cap, lim, lam_new, mu_new


def _round_kernel(core, ids, count, kept, own, other, r0, r1, r2, r3, cap_i, lim_i, lam_in, mu_in,
                  keep, give, rows, values, lam_out, mu_out, lacc, racc, vacc, lamb, mub, scores, loaded):
    cnt = count[0, 0]
    turns = (cnt + GROUP - 1) // GROUP
    _each(turns, lambda g: _chunk(kept, scores, loaded, g).start())
    _clear(lacc, racc)
    if vacc is not None:
        vacc[...] = jnp.zeros_like(vacc)
    lam = 0.0 if lam_in is None else lam_in[...]
    mu = 0.0 if mu_in is None else mu_in[...]
    _, _, _, lam_new, mu_new = _duals(core[0], own, other, r0, r1, r2, r3, cap_i, lim_i, lam, mu)
    lam_out[...] = lam_new
    mu_out[...] = mu_new
    lam_bar = 2.0 * lam_new - lam
    mub[:UB] = (2.0 * mu_new - mu)[:, None, :]
    for b in range(CB):
        lamb[b] = jnp.broadcast_to(lam_bar[b:b + 1, :], (BLOCK, BLOCK)).T

    def some(first):
        for slot, ub, cb, live in _group(ids, cnt, first, UNROLL):
            s = scores[slot].astype(F32)
            x = jnp.clip(s - lamb[cb] - mub[ub], 0.0, 1.0)
            lacc[jnp.where(live, cb, CB)] += x
            to_u = jnp.where(live, ub, UB)
            racc[to_u] += _fold(x)
            if vacc is not None:
                vacc[to_u] += _fold(x * s)

    def chunk(g):
        _chunk(kept, scores, loaded, g).wait()
        _each(GROUP // UNROLL, lambda i: some(g * GROUP + i * UNROLL))

    _each(turns, chunk)
    _finish_load(lacc, keep, give, core[0])
    rows[...] = racc[:UB].sum(axis=1)
    if vacc is not None:
        values[...] = vacc[:UB].sum(axis=1)


def second_kernel(core, ids, count, own, other, r0, r1, r2, r3, cap_i, lim_i, kept,
                  keep, give, rows, lam_out, mu_out, lacc, racc, lamb, mub, scores, loaded):
    _round_kernel(core, ids, count, kept, own, other, r0, r1, r2, r3, cap_i, lim_i, None, None,
                  keep, give, rows, None, lam_out, mu_out, lacc, racc, None, lamb, mub, scores, loaded)


def third_kernel(core, ids, count, own, other, r0, r1, r2, r3, cap_i, lim_i, lam_in, mu_in, kept,
                 keep, give, out, lam_out, mu_out, lacc, racc, vacc, lamb, mub, scores, loaded):
    _round_kernel(core, ids, count, kept, own, other, r0, r1, r2, r3, cap_i, lim_i, lam_in, mu_in,
                  keep, give, out.at[0], out.at[1], lam_out, mu_out, lacc, racc, vacc, lamb, mub, scores, loaded)


def last_kernel(core, own, other, p0, p1, p2, p3, cap_i, lim_i, lam_in, mu_in, duals, user_duals, ratio, user_value):
    load, cap, lim, lam_new, mu_new = _duals(
        core[0], own, other, p0.at[0], p1.at[0], p2.at[0], p3.at[0], cap_i, lim_i, lam_in[...], mu_in[...])
    duals[...] = lam_new
    user_duals[...] = mu_new
    ratio[...] = load / cap
    user_value[...] = ((p0[1] + p2[1]) + (p1[1] + p3[1])) / lim


SMEM = pl.BlockSpec(memory_space=pltpu.SMEM)
VMEM = pl.BlockSpec(memory_space=pltpu.VMEM)
ANY = pl.BlockSpec(memory_space=pl.ANY)


def _call(kernel, n_smem, args, outs, scratch=(), more=(), any_in=0, any_out=0, limit=20):
    return pl.pallas_call(
        kernel,
        in_specs=[SMEM] * n_smem + [VMEM] * (len(args) - n_smem - any_in) + [ANY] * any_in,
        out_specs=[ANY] * any_out + [VMEM] * (len(outs) - any_out),
        out_shape=[jax.ShapeDtypeStruct(s, d) for s, d in outs],
        scratch_shapes=[pltpu.VMEM(s, F32) for s in scratch] + list(more),
        compiler_params=pltpu.CompilerParams(vmem_limit_bytes=limit * 2 ** 20),
    )(*args)


LACC = (CB + 1, BLOCK, BLOCK)
RACC = (UB + 1, 8, BLOCK)
HALF = ((CB // 2, BLOCK), F32)
ROWS = ((UB, BLOCK), F32)
LAM = ((CB, BLOCK), F32)
MUB = (UB, 1, BLOCK)
SCORES = ((SLOTS, BLOCK, BLOCK), jnp.bfloat16)
CHUNKS = [pltpu.VMEM(*SCORES), pltpu.SemaphoreType.DMA((SLOTS // GROUP,))]
LAMB = (CB, BLOCK, BLOCK)


def _spread(x, axes, n):
    return lax.all_to_all(jnp.broadcast_to(x[None], (n,) + x.shape), axes, 0, 0, tiled=True)


def _swap(x):
    return lax.ppermute(x, "core", [(0, 1), (1, 0)])


def spread_kernel(keep, got, out):
    out[...] = jnp.broadcast_to((keep[...] + got[...])[None], out.shape)


def sum_kernel(parts, out):
    out[...] = parts[...].sum(0)


def _sum_load(keep, give):
    (wide,) = _call(spread_kernel, 0, (keep, _swap(give)), [((NZ * NX,) + HALF[0], F32)])
    wide = lax.all_to_all(wide, ("z", "x"), 0, 0, tiled=True)
    (own,) = _call(sum_kernel, 0, (wide,), [HALF])
    return own, _swap(own)


def _shift(x, k):
    return lax.ppermute(x, "camp", [((i + k) % NCAMP, i) for i in range(NCAMP)])


def _camp_parts(x):
    return x, _shift(x, 1), _shift(x, 2), _shift(x, 3)


def shards(user_emb, camp_emb, block_ids, block_count, capacity, user_limit):
    where = jnp.reshape(lax.axis_index("core"), (1,)).astype(jnp.int32)
    camp_emb, where = lax.optimization_barrier((camp_emb, where))
    cap = capacity.reshape(CB, BLOCK)
    lim = user_limit.reshape(UB, BLOCK)
    users = user_emb.reshape(UB, BLOCK, E)

    part = _spread(camp_emb, "z", NZ)
    part = _spread(part.reshape(NZ, 64, E), "x", NX).reshape(NX, NZ, 64, E)
    peer = _swap(part)

    slots = (where, block_ids, block_count)
    kept, keep, give, rows = _call(
        first_kernel, 3, (*slots, part, peer, users), [SCORES, HALF, HALF, ROWS], [LACC, RACC],
        [pltpu.VMEM((NZ, NX, 2, 64, E), jnp.bfloat16), pltpu.VMEM((UB, BLOCK, E), jnp.bfloat16), CHUNKS[0],
         pltpu.SemaphoreType.DMA((NX, 2)), pltpu.SemaphoreType.DMA, CHUNKS[1]], any_in=1, any_out=1, limit=WIDE)
    parts = _camp_parts(rows)
    own, other = _sum_load(keep, give)
    keep, give, rows, lam, mu = _call(
        second_kernel, 3, (*slots, own, other, *parts, cap, lim, kept),
        [HALF, HALF, ROWS, LAM, ROWS], [LACC, RACC, LAMB, MUB], CHUNKS, any_in=1, limit=WIDE)
    parts = _camp_parts(rows)
    own, other = _sum_load(keep, give)
    keep, give, both_sums, lam, mu = _call(
        third_kernel, 3, (*slots, own, other, *parts, cap, lim, lam, mu, kept),
        [HALF, HALF, ((2, UB, BLOCK), F32), LAM, ROWS], [LACC, RACC, RACC, LAMB, MUB], CHUNKS, any_in=1, limit=WIDE)
    parts = _camp_parts(both_sums)
    own, other = _sum_load(keep, give)
    duals, user_duals, ratio, value = _call(
        last_kernel, 1, (where, own, other, *parts, cap, lim, lam, mu), [LAM, ROWS, LAM, ROWS])
    return duals.reshape(-1), user_duals.reshape(-1), ratio.reshape(-1), value.reshape(-1)


def solution(mesh):
    fine = Mesh(mesh.devices.reshape(NZ, NX, NCORE, NCAMP), ("z", "x", "core", "camp"))
    users = ("z", "x", "core")
    return jax.shard_map(
        shards,
        mesh=fine,
        in_specs=(P(users, None), P(("camp",) + users, None), P("camp", users), P("camp", users), P("camp"), P(users)),
        out_specs=(P("camp"), P(users), P("camp"), P(users)),
        check_vma=False,
    )
```

time: 140 us -> 133 us (0.950)
  local copies, waits for them, and re-layouts: 16 us -> 1.59 us
  Pallas kernels: 19.2 us -> 29.5 us
  starting transfers between devices: 43.9 us -> 34.6 us
  waiting for transfers between devices: 23.5 us -> 30.8 us
    unnamed x14 -> x8, local copies, waits for them, and re-layouts: 12.6 us -> 0.69 us
    pallas_call x4 -> x10, Pallas kernels: 18.9 us -> 29.5 us  [_call(): pl.pallas_call(kernel, in_specs=[SMEM] * n_smem + [VMEM] * (len(args) - n...]
    all_to_all x3, waiting for transfers between devices: 18.2 us -> 23.2 us  [_sum_load(): wide = lax.all_to_all(wide, ('z', 'x'), 0, 0, tiled=True)]
    ppermute x9, starting transfers between devices: 17.3 us -> 12.7 us  [_shift(): return lax.ppermute(x, 'camp', [((i + k) % NCAMP, i) for i in range(NCAMP)])]
    all_to_all x3, starting transfers between devices: 14.4 us -> 11.6 us  [_sum_load(): wide = lax.all_to_all(wide, ('z', 'x'), 0, 0, tiled=True)]
    ppermute x7, waiting for transfers between devices: 5.28 us -> 7.56 us  [_swap(): return lax.ppermute(x, 'core', [(0, 1), (1, 0)])]
    broadcast_in_dim x5 -> x2, local copies, waits for them, and re-layouts: 3.08 us -> 0.9 us  [_spread(): jnp.broadcast_to(x[None], (n,) + x.shape)]
    ppermute x7, starting transfers between devices: 12.2 us -> 10.2 us  [_swap(): return lax.ppermute(x, 'core', [(0, 1), (1, 0)])]
  transfers between devices with their start and end apart: 19 -> 19, of which waited for: 9 -> 10; matrix products, arithmetic and copies ran while one was open for 0% -> 0% of each run, Pallas kernels for 0% -> 0%
where the time goes in v3:
time: 133 us
  blocking collectives  35.1 us (26%)
  starting transfers between devices  34.6 us (26%)
  waiting for transfers between devices  30.8 us (23%)
  Pallas kernels  29.5 us (22%)
  local copies, waits for them, and re-layouts  1.59 us (1%)
  between operations  1.44 us (1%)
    all_to_all x2, blocking collectives, _spread(): lax.all_to_all(jnp.broadcast_to(x[None], (n,) + x.shape), axes, 0, 0, til...  35.1 us
    pallas_call x10, Pallas kernels, _call(): pl.pallas_call(kernel, in_specs=[SMEM] * n_smem + [VMEM] * (len(args) - n...  29.5 us
    all_to_all x3, waiting for transfers between devices, _sum_load(): wide = lax.all_to_all(wide, ('z', 'x'), 0, 0, tiled=True)  23.2 us
    ppermute x9, starting transfers between devices, _shift(): return lax.ppermute(x, 'camp', [((i + k) % NCAMP, i) for i in range(NCAMP)])  12.7 us
    all_to_all x3, starting transfers between devices, _sum_load(): wide = lax.all_to_all(wide, ('z', 'x'), 0, 0, tiled=True)  11.6 us
    ppermute x7, starting transfers between devices, _swap(): return lax.ppermute(x, 'core', [(0, 1), (1, 0)])  10.2 us
    ppermute x7, waiting for transfers between devices, _swap(): return lax.ppermute(x, 'core', [(0, 1), (1, 0)])  7.56 us
  transfers between devices with their start and end apart: 19, of which 10 were waited for; matrix products, arithmetic and copies ran while one was open for 0% of the time, Pallas kernels for 0%

profile of v3, /device:TPU:1, one launch (start us, length us, event | category | flops | bytes accessed | tf_op | source)
XLA Modules:
  0.0 132.9 jit_solution(12385623854674151545)
XLA Ops:
  0.7 0.8 broadcast_in_dim.4
  1.5 19.2 %all_to_all.25 = bf16[8,64,256]{2,1,0:T(8,128)(2,1)S(1)} all-to-all(bf16[8,64,256]{2,1,0:T(8,128)(2,1)S(1)} %broadcast_in_dim.4), channel_id=1, replica_groups=mesh['z'=8,'x'=4,'core'=2,'camp'=4] {'z'}, dimensions={0} | all-to-all | bytes 524288 | tf_op jit(solution)/shard_map/all_to_all | solution.py:223
  20.8 15.9 %all_to_all.26.part = bf16[4,8,64,256]{3,2,1,0:T(8,128)(2,1)S(1)} all-to-all(bf16[4,8,64,256]{3,2,1,0:T(8,128)(2,1)S(1)} %broadcast_in_dim.5), channel_id=1, replica_groups=mesh['z'=8,'x'=4,'core'=2,'camp'=4] {'x'}, dimensions={0} | all-to-all | bytes 2097152 | tf_op jit(solution)/shard_map/all_to_all | solution.py:223
  36.7 4.0 %collective-permute-start = (bf16[4,8,64,256]{3,2,1,0:T(8,128)(2,1)S(1)}, bf16[4,8,64,256]{3,2,1,0:T(8,128)(2,1)S(1)}, u32[]{:S(2)}, u32[]{:S(2)}) collective-permute-start(bf16[4,8,64,256]{3,2,1,0:T(8,128)(2,1)S(1)} %all_to_all.26.part), channel_id=1, source_target_pairs={{0,4},{4,0},{1,5},{5,1},{2,6},{6,2},{3,7},{7,3},{8,12},{12,8},{9,1... | collective-permute-start | bytes 3145736 | tf_op jit(solution)/shard_map/ppermute | solution.py:227
  41.3 1.6 %collective-permute-done.peer = bf16[4,8,64,256]{3,2,1,0:T(8,128)(2,1)S(1)} collective-permute-done((bf16[4,8,64,256]{3,2,1,0:T(8,128)(2,1)S(1)}, bf16[4,8,64,256]{3,2,1,0:T(8,128)(2,1)S(1)}, u32[]{:S(2)}, u32[]{:S(2)}) %collective-permute-start) | collective-permute-done | bytes 1048608 | tf_op jit(solution)/shard_map/ppermute | solution.py:227
  43.6 11.1 %shard_map.93 = (bf16[256,128,128]{2,1,0:T(8,128)(2,1)}, f32[16,128]{1,0:T(8,128)S(1)}, f32[16,128]{1,0:T(8,128)S(1)}, f32[64,128]{1,0:T(8,128)S(1)}) custom-call(s32[1]{0:T(128)} %bitcast.core, s32[1,256]{1,0:T(1,128)S(1)} %copy-done.2, s32[1,1]{1,0:T(1,128)S(6)} %copy.10.count, bf16[4,8,64,256]{3,2,1,0:T(8,128)(2,1)S(1)} %all_to_all.26.part, ...), custom_call_target="tpu_custom_call" | custom-call | tf_op jit(solution)/shard_map/pallas_call | solution.py:201
  54.8 1.2 collective-permute-done.1.got
  56.0 0.7 shard_map.94
  56.7 3.9 %all-to-all-start.2 = ((f32[32,16,128]{2,1,0:T(8,128)}), f32[32,16,128]{2,1,0:T(8,128)S(1)}, u32[]{:S(2)}, u32[]{:S(2)}) async-start(f32[32,16,128]{2,1,0:T(8,128)} %shard_map.94), calls=%async_computation.2 | async-start | bytes 524288 | tf_op jit(solution)/shard_map/all_to_all | solution.py:240
  60.6 1.2 collective-permute-start.5
  61.8 2.7 %collective-permute-start.4 = (f32[64,128]{1,0:T(8,128)S(1)}, f32[64,128]{1,0:T(8,128)S(1)}, u32[]{:S(2)}, u32[]{:S(2)}) collective-permute-start(f32[64,128]{1,0:T(8,128)S(1)} %get-tuple-element.28.r0), channel_id=1, source_target_pairs={{2,0},{3,1},{0,2},{1,3},{6,4},{7,5},{4,6},{5,7},{10,8},{11,9},{8,1... | collective-permute-start | bytes 98312 | tf_op jit(solution)/shard_map/ppermute | solution.py:246
  64.5 0.9 collective-permute-start.3
  65.4 7.1 %all-to-all-done.2.parts = f32[32,16,128]{2,1,0:T(8,128)S(1)} async-done(((f32[32,16,128]{2,1,0:T(8,128)}), f32[32,16,128]{2,1,0:T(8,128)S(1)}, u32[]{:S(2)}, u32[]{:S(2)}) %all-to-all-start.2) | async-done | bytes 262176 | tf_op jit(solution)/shard_map/all_to_all | solution.py:240
  72.5 2.1 %collective-permute-start.2 = (f32[16,128]{1,0:T(8,128)S(1)}, f32[16,128]{1,0:T(8,128)S(1)}, u32[]{:S(2)}, u32[]{:S(2)}) collective-permute-start(f32[16,128]{1,0:T(8,128)S(1)} %shard_map.95.own), channel_id=1, source_target_pairs={{0,4},{4,0},{1,5},{5,1},{2,6},{6,2},{3,7},{7,3},{8,12},{12,8},{9,1... | collective-permute-start | bytes 24584 | tf_op jit(solution)/shard_map/ppermute | solution.py:227
  74.6 0.8 collective-permute-done.2.other
  75.5 7.2 %shard_map.96 = (f32[16,128]{1,0:T(8,128)S(1)}, f32[16,128]{1,0:T(8,128)S(1)}, f32[64,128]{1,0:T(8,128)S(1)}, f32[32,128]{1,0:T(8,128)S(1)}, f32[64,128]{1,0:T(8,128)S(1)}) custom-call(s32[1]{0:T(128)} %bitcast.core, s32[1,256]{1,0:T(1,128)S(1)} %copy-done.3, s32[1,1]{1,0:T(1,128)S(6)} %copy.10.count, f32[16,128]{1,0:T(8,128)S(1)} %shard_map.95.own, ...), custom_call_target="tpu_custom_call" | custom-call | tf_op jit(solution)/shard_map/pallas_call | solution.py:201
  82.7 1.2 collective-permute-done.6.got
  83.9 0.7 shard_map.97
  84.6 3.9 %all-to-all-start.3 = ((f32[32,16,128]{2,1,0:T(8,128)}), f32[32,16,128]{2,1,0:T(8,128)S(1)}, u32[]{:S(2)}, u32[]{:S(2)}) async-start(f32[32,16,128]{2,1,0:T(8,128)} %shard_map.97), calls=%async_computation.3 | async-start | bytes 524288 | tf_op jit(solution)/shard_map/all_to_all | solution.py:240
  88.5 0.9 collective-permute-start.10
  89.4 2.7 %collective-permute-start.9 = (f32[64,128]{1,0:T(8,128)S(1)}, f32[64,128]{1,0:T(8,128)S(1)}, u32[]{:S(2)}, u32[]{:S(2)}) collective-permute-start(f32[64,128]{1,0:T(8,128)S(1)} %get-tuple-element.32.r0), channel_id=1, source_target_pairs={{2,0},{3,1},{0,2},{1,3},{6,4},{7,5},{4,6},{5,7},{10,8},{11,9},{8,1... | collective-permute-start | bytes 98312 | tf_op jit(solution)/shard_map/ppermute | solution.py:246
  92.8 7.8 %all-to-all-done.3.parts = f32[32,16,128]{2,1,0:T(8,128)S(1)} async-done(((f32[32,16,128]{2,1,0:T(8,128)}), f32[32,16,128]{2,1,0:T(8,128)S(1)}, u32[]{:S(2)}, u32[]{:S(2)}) %all-to-all-start.3) | async-done | bytes 262176 | tf_op jit(solution)/shard_map/all_to_all | solution.py:240
  100.6 2.0 %collective-permute-start.7 = (f32[16,128]{1,0:T(8,128)S(1)}, f32[16,128]{1,0:T(8,128)S(1)}, u32[]{:S(2)}, u32[]{:S(2)}) collective-permute-start(f32[16,128]{1,0:T(8,128)S(1)} %shard_map.98.own), channel_id=1, source_target_pairs={{0,4},{4,0},{1,5},{5,1},{2,6},{6,2},{3,7},{7,3},{8,12},{12,8},{9,1... | collective-permute-start | bytes 24584 | tf_op jit(solution)/shard_map/ppermute | solution.py:227
  102.5 0.8 collective-permute-done.7.other
  103.4 8.2 %shard_map.99 = (f32[16,128]{1,0:T(8,128)S(1)}, f32[16,128]{1,0:T(8,128)S(1)}, f32[2,64,128]{2,1,0:T(8,128)S(1)}, f32[32,128]{1,0:T(8,128)S(1)}, f32[64,128]{1,0:T(8,128)S(1)}) custom-call(s32[1]{0:T(128)} %bitcast.core, s32[1,256]{1,0:T(1,128)S(1)} %copy-done.3, s32[1,1]{1,0:T(1,128)S(6)} %copy.10.count, f32[16,128]{1,0:T(8,128)S(1)} %shard_map.98.own, ...), custom_call_target="tpu_custom_call" | custom-call | tf_op jit(solution)/shard_map/pallas_call | solution.py:201
  111.7 1.2 collective-permute-done.11.got
  112.8 0.7 shard_map.100
  113.6 3.9 %all-to-all-start.4 = ((f32[32,16,128]{2,1,0:T(8,128)}), f32[32,16,128]{2,1,0:T(8,128)S(1)}, u32[]{:S(2)}, u32[]{:S(2)}) async-start(f32[32,16,128]{2,1,0:T(8,128)} %shard_map.100), calls=%async_computation.4 | async-start | bytes 524288 | tf_op jit(solution)/shard_map/all_to_all | solution.py:240
  118.1 2.7 %collective-permute-start.14 = (f32[2,64,128]{2,1,0:T(8,128)S(1)}, f32[2,64,128]{2,1,0:T(8,128)S(1)}, u32[]{:S(2)}, u32[]{:S(2)}) collective-permute-start(f32[2,64,128]{2,1,0:T(8,128)S(1)} %get-tuple-element.37.p0), channel_id=1, source_target_pairs={{2,0},{3,1},{0,2},{1,3},{6,4},{7,5},{4,6},{5,7},{10,8},{11,9},{8,1... | collective-permute-start | bytes 196616 | tf_op jit(solution)/shard_map/ppermute | solution.py:246
  121.1 8.4 %all-to-all-done.4.parts = f32[32,16,128]{2,1,0:T(8,128)S(1)} async-done(((f32[32,16,128]{2,1,0:T(8,128)}), f32[32,16,128]{2,1,0:T(8,128)S(1)}, u32[]{:S(2)}, u32[]{:S(2)}) %all-to-all-start.4) | async-done | bytes 262176 | tf_op jit(solution)/shard_map/all_to_all | solution.py:240
  129.5 2.0 %collective-permute-start.12 = (f32[16,128]{1,0:T(8,128)S(1)}, f32[16,128]{1,0:T(8,128)S(1)}, u32[]{:S(2)}, u32[]{:S(2)}) collective-permute-start(f32[16,128]{1,0:T(8,128)S(1)} %shard_map.101.own), channel_id=1, source_target_pairs={{0,4},{4,0},{1,5},{5,1},{2,6},{6,2},{3,7},{7,3},{8,12},{12,8},{9,1... | collective-permute-start | bytes 24584 | tf_op jit(solution)/shard_map/ppermute | solution.py:227
  131.5 0.8 collective-permute-done.12.other
  (28 shorter events, 3.5 us)
Async XLA Ops:
  0.6 74.8 %copy-start.3 = (s32[1,256]{1,0:T(1,128)S(1)}, s32[1,256]{1,0:T(1,128)}, u32[]{:S(2)}) copy-start(s32[1,256]{1,0:T(1,128)} %ids.5) | copy-start | bytes 3076
  0.6 74.8 %copy-start = (s32[8192]{0:T(1024)S(1)}, s32[8192]{0:T(1024)}, u32[]{:S(2)}) copy-start(s32[8192]{0:T(1024)} %param.11) | copy-start | bytes 98308
  0.7 74.8 %copy-start.1 = (s32[4096]{0:T(1024)S(1)}, s32[4096]{0:T(1024)}, u32[]{:S(2)}) copy-start(s32[4096]{0:T(1024)} %param.10) | copy-start | bytes 49156
  36.7 6.2 %collective-permute-start = (bf16[4,8,64,256]{3,2,1,0:T(8,128)(2,1)S(1)}, bf16[4,8,64,256]{3,2,1,0:T(8,128)(2,1)S(1)}, u32[]{:S(2)}, u32[]{:S(2)}) collective-permute-start(bf16[4,8,64,256]{3,2,1,0:T(8,128)(2,1)S(1)} %all_to_all.26.part), channel_id=1, source_target_pairs={{0,4},{4,0},{1,5},{5,1},{2,6},{6,2},{3,7},{7,3},{8,12},{12,8},{9,1... | collective-permute-start | bytes 3145736 | tf_op jit(solution)/shard_map/ppermute | solution.py:227
  42.9 0.7 copy-start.2
  54.7 1.3 collective-permute-start.1
  56.7 15.8 %all-to-all-start.2 = ((f32[32,16,128]{2,1,0:T(8,128)}), f32[32,16,128]{2,1,0:T(8,128)S(1)}, u32[]{:S(2)}, u32[]{:S(2)}) async-start(f32[32,16,128]{2,1,0:T(8,128)} %shard_map.94), calls=%async_computation.2 | async-start | bytes 524288 | tf_op jit(solution)/shard_map/all_to_all | solution.py:240
  60.6 14.0 %collective-permute-start.5 = (f32[64,128]{1,0:T(8,128)S(1)}, f32[64,128]{1,0:T(8,128)S(1)}, u32[]{:S(2)}, u32[]{:S(2)}) collective-permute-start(f32[64,128]{1,0:T(8,128)S(1)} %get-tuple-element.28.r0), channel_id=1, source_target_pairs={{3,0},{0,1},{1,2},{2,3},{7,4},{4,5},{5,6},{6,7},{11,8},{8,9},{9,10... | collective-permute-start | bytes 98312 | tf_op jit(solution)/shard_map/ppermute | solution.py:246
  61.8 12.8 %collective-permute-start.4 = (f32[64,128]{1,0:T(8,128)S(1)}, f32[64,128]{1,0:T(8,128)S(1)}, u32[]{:S(2)}, u32[]{:S(2)}) collective-permute-start(f32[64,128]{1,0:T(8,128)S(1)} %get-tuple-element.28.r0), channel_id=1, source_target_pairs={{2,0},{3,1},{0,2},{1,3},{6,4},{7,5},{4,6},{5,7},{10,8},{11,9},{8,1... | collective-permute-start | bytes 98312 | tf_op jit(solution)/shard_map/ppermute | solution.py:246
  64.5 10.1 %collective-permute-start.3 = (f32[64,128]{1,0:T(8,128)S(1)}, f32[64,128]{1,0:T(8,128)S(1)}, u32[]{:S(2)}, u32[]{:S(2)}) collective-permute-start(f32[64,128]{1,0:T(8,128)S(1)} %get-tuple-element.28.r0), channel_id=1, source_target_pairs={{1,0},{2,1},{3,2},{0,3},{5,4},{6,5},{7,6},{4,7},{9,8},{10,9},{11,1... | collective-permute-start | bytes 98312 | tf_op jit(solution)/shard_map/ppermute | solution.py:246
  72.5 2.9 %collective-permute-start.2 = (f32[16,128]{1,0:T(8,128)S(1)}, f32[16,128]{1,0:T(8,128)S(1)}, u32[]{:S(2)}, u32[]{:S(2)}) collective-permute-start(f32[16,128]{1,0:T(8,128)S(1)} %shard_map.95.own), channel_id=1, source_target_pairs={{0,4},{4,0},{1,5},{5,1},{2,6},{6,2},{3,7},{7,3},{8,12},{12,8},{9,1... | collective-permute-start | bytes 24584 | tf_op jit(solution)/shard_map/ppermute | solution.py:227
  82.6 1.3 collective-permute-start.6
  84.6 15.9 %all-to-all-start.3 = ((f32[32,16,128]{2,1,0:T(8,128)}), f32[32,16,128]{2,1,0:T(8,128)S(1)}, u32[]{:S(2)}, u32[]{:S(2)}) async-start(f32[32,16,128]{2,1,0:T(8,128)} %shard_map.97), calls=%async_computation.3 | async-start | bytes 524288 | tf_op jit(solution)/shard_map/all_to_all | solution.py:240
  88.5 14.0 %collective-permute-start.10 = (f32[64,128]{1,0:T(8,128)S(1)}, f32[64,128]{1,0:T(8,128)S(1)}, u32[]{:S(2)}, u32[]{:S(2)}) collective-permute-start(f32[64,128]{1,0:T(8,128)S(1)} %get-tuple-element.32.r0), channel_id=1, source_target_pairs={{3,0},{0,1},{1,2},{2,3},{7,4},{4,5},{5,6},{6,7},{11,8},{8,9},{9,10... | collective-permute-start | bytes 98312 | tf_op jit(solution)/shard_map/ppermute | solution.py:246
  89.4 13.1 %collective-permute-start.9 = (f32[64,128]{1,0:T(8,128)S(1)}, f32[64,128]{1,0:T(8,128)S(1)}, u32[]{:S(2)}, u32[]{:S(2)}) collective-permute-start(f32[64,128]{1,0:T(8,128)S(1)} %get-tuple-element.32.r0), channel_id=1, source_target_pairs={{2,0},{3,1},{0,2},{1,3},{6,4},{7,5},{4,6},{5,7},{10,8},{11,9},{8,1... | collective-permute-start | bytes 98312 | tf_op jit(solution)/shard_map/ppermute | solution.py:246
  92.1 10.4 %collective-permute-start.8 = (f32[64,128]{1,0:T(8,128)S(1)}, f32[64,128]{1,0:T(8,128)S(1)}, u32[]{:S(2)}, u32[]{:S(2)}) collective-permute-start(f32[64,128]{1,0:T(8,128)S(1)} %get-tuple-element.32.r0), channel_id=1, source_target_pairs={{1,0},{2,1},{3,2},{0,3},{5,4},{6,5},{7,6},{4,7},{9,8},{10,9},{11,1... | collective-permute-start | bytes 98312 | tf_op jit(solution)/shard_map/ppermute | solution.py:246
  100.6 2.8 %collective-permute-start.7 = (f32[16,128]{1,0:T(8,128)S(1)}, f32[16,128]{1,0:T(8,128)S(1)}, u32[]{:S(2)}, u32[]{:S(2)}) collective-permute-start(f32[16,128]{1,0:T(8,128)S(1)} %shard_map.98.own), channel_id=1, source_target_pairs={{0,4},{4,0},{1,5},{5,1},{2,6},{6,2},{3,7},{7,3},{8,12},{12,8},{9,1... | collective-permute-start | bytes 24584 | tf_op jit(solution)/shard_map/ppermute | solution.py:227
  111.6 1.3 collective-permute-start.11
  113.6 15.9 %all-to-all-start.4 = ((f32[32,16,128]{2,1,0:T(8,128)}), f32[32,16,128]{2,1,0:T(8,128)S(1)}, u32[]{:S(2)}, u32[]{:S(2)}) async-start(f32[32,16,128]{2,1,0:T(8,128)} %shard_map.100), calls=%async_computation.4 | async-start | bytes 524288 | tf_op jit(solution)/shard_map/all_to_all | solution.py:240
  117.4 14.0 %collective-permute-start.15 = (f32[2,64,128]{2,1,0:T(8,128)S(1)}, f32[2,64,128]{2,1,0:T(8,128)S(1)}, u32[]{:S(2)}, u32[]{:S(2)}) collective-permute-start(f32[2,64,128]{2,1,0:T(8,128)S(1)} %get-tuple-element.37.p0), channel_id=1, source_target_pairs={{3,0},{0,1},{1,2},{2,3},{7,4},{4,5},{5,6},{6,7},{11,8},{8,9},{9,10... | collective-permute-start | bytes 196616 | tf_op jit(solution)/shard_map/ppermute | solution.py:246
  118.1 13.4 %collective-permute-start.14 = (f32[2,64,128]{2,1,0:T(8,128)S(1)}, f32[2,64,128]{2,1,0:T(8,128)S(1)}, u32[]{:S(2)}, u32[]{:S(2)}) collective-permute-start(f32[2,64,128]{2,1,0:T(8,128)S(1)} %get-tuple-element.37.p0), channel_id=1, source_target_pairs={{2,0},{3,1},{0,2},{1,3},{6,4},{7,5},{4,6},{5,7},{10,8},{11,9},{8,1... | collective-permute-start | bytes 196616 | tf_op jit(solution)/shard_map/ppermute | solution.py:246
  120.7 10.7 %collective-permute-start.13 = (f32[2,64,128]{2,1,0:T(8,128)S(1)}, f32[2,64,128]{2,1,0:T(8,128)S(1)}, u32[]{:S(2)}, u32[]{:S(2)}) collective-permute-start(f32[2,64,128]{2,1,0:T(8,128)S(1)} %get-tuple-element.37.p0), channel_id=1, source_target_pairs={{1,0},{2,1},{3,2},{0,3},{5,4},{6,5},{7,6},{4,7},{9,8},{10,9},{11,1... | collective-permute-start | bytes 196616 | tf_op jit(solution)/shard_map/ppermute | solution.py:246
  129.5 2.8 %collective-permute-start.12 = (f32[16,128]{1,0:T(8,128)S(1)}, f32[16,128]{1,0:T(8,128)S(1)}, u32[]{:S(2)}, u32[]{:S(2)}) collective-permute-start(f32[16,128]{1,0:T(8,128)S(1)} %shard_map.101.own), channel_id=1, source_target_pairs={{0,4},{4,0},{1,5},{5,1},{2,6},{6,2},{3,7},{7,3},{8,12},{12,8},{9,1... | collective-permute-start | bytes 24584 | tf_op jit(solution)/shard_map/ppermute | solution.py:227

commit v4 on v3

--- a/solution.py
+++ b/solution.py
@@ -14,6 +14,8 @@
 UNROLL = 4
 GROUP = 32
 WIDE = 50
+FIRST = 43
+AHEAD = 2
 F32 = jnp.float32
 
 
@@ -62,10 +64,16 @@
     return out
 
 
-def first_kernel(core, ids, count, part, peer, users_in, kept, keep, give, rows, lacc, racc, panel, users, scores,
+def fetch_kernel(users, out, sem):
+    copy = pltpu.make_async_copy(users, out, sem)
+    copy.start()
+    copy.wait()
+
+
+def first_kernel(core, count, users, part, peer, codes, kept, keep, give, rows, lacc, racc, panel, scores, ids,
                  sems, fetched, stored):
     me = core[0]
-    fetch = pltpu.make_async_copy(users_in, users, fetched)
+    fetch = pltpu.make_async_copy(codes, ids, fetched)
     fetch.start()
     copies = [
         pltpu.make_async_copy(src.at[x], panel.at[:, x, half], sems.at[x, k])
@@ -136,7 +144,7 @@
                   keep, give, rows, values, lam_out, mu_out, lacc, racc, vacc, lamb, mub, scores, loaded):
     cnt = count[0, 0]
     turns = (cnt + GROUP - 1) // GROUP
-    _each(turns, lambda g: _chunk(kept, scores, loaded, g).start())
+    _each(jnp.minimum(turns, AHEAD), lambda g: _chunk(kept, scores, loaded, g).start())
     _clear(lacc, racc)
     if vacc is not None:
         vacc[...] = jnp.zeros_like(vacc)
@@ -162,6 +170,11 @@
 
     def chunk(g):
         _chunk(kept, scores, loaded, g).wait()
+
+        @pl.when(g + AHEAD < turns)
+        def _():
+            _chunk(kept, scores, loaded, g + AHEAD).start()
+
         _each(GROUP // UNROLL, lambda i: some(g * GROUP + i * UNROLL))
 
     _each(turns, chunk)
@@ -259,13 +272,16 @@
 
     part = _spread(camp_emb, "z", NZ)
     part = _spread(part.reshape(NZ, 64, E), "x", NX).reshape(NX, NZ, 64, E)
+    part, users = lax.optimization_barrier((part, users))
+    (users,) = _call(
+        fetch_kernel, 0, (users,), [(users.shape, users.dtype)], [], [pltpu.SemaphoreType.DMA], any_in=1, limit=4)
     peer = _swap(part)
 
     slots = (where, block_ids, block_count)
     kept, keep, give, rows = _call(
-        first_kernel, 3, (*slots, part, peer, users), [SCORES, HALF, HALF, ROWS], [LACC, RACC],
-        [pltpu.VMEM((NZ, NX, 2, 64, E), jnp.bfloat16), pltpu.VMEM((UB, BLOCK, E), jnp.bfloat16), CHUNKS[0],
-         pltpu.SemaphoreType.DMA((NX, 2)), pltpu.SemaphoreType.DMA, CHUNKS[1]], any_in=1, any_out=1, limit=WIDE)
+        first_kernel, 2, (where, block_count, users, part, peer, block_ids), [SCORES, HALF, HALF, ROWS], [LACC, RACC],
+        [pltpu.VMEM((NZ, NX, 2, 64, E), jnp.bfloat16), CHUNKS[0], pltpu.SMEM((1, SLOTS), jnp.int32),
+         pltpu.SemaphoreType.DMA((NX, 2)), pltpu.SemaphoreType.DMA, CHUNKS[1]], any_in=1, any_out=1, limit=FIRST)
     parts = _camp_parts(rows)
     own, other = _sum_load(keep, give)
     keep, give, rows, lam, mu = _call(

time: 133 us -> 132 us (level)
    pallas_call x10 -> x11, Pallas kernels: 29.5 us -> 28.2 us  [_call(): pl.pallas_call(kernel, in_specs=[SMEM] * n_smem + [VMEM] * (len(args) - n...]
where the time goes in v4:
time: 132 us; the launch traced here: 131 us
  blocking collectives  35.2 us (27%)
  starting transfers between devices  34.4 us (26%)
  waiting for transfers between devices  30.6 us (23%)
  Pallas kernels  28.2 us (21%)
  between operations  1.46 us (1%)
    all_to_all x2, blocking collectives, _spread(): lax.all_to_all(jnp.broadcast_to(x[None], (n,) + x.shape), axes, 0, 0, til...  35.2 us
    pallas_call x11, Pallas kernels, _call(): pl.pallas_call(kernel, in_specs=[SMEM] * n_smem + [VMEM] * (len(args) - n...  28.2 us
    all_to_all x3, waiting for transfers between devices, _sum_load(): wide = lax.all_to_all(wide, ('z', 'x'), 0, 0, tiled=True)  23.4 us
    ppermute x9, starting transfers between devices, _shift(): return lax.ppermute(x, 'camp', [((i + k) % NCAMP, i) for i in range(NCAMP)])  12.4 us
    all_to_all x3, starting transfers between devices, _sum_load(): wide = lax.all_to_all(wide, ('z', 'x'), 0, 0, tiled=True)  11.6 us
    ppermute x7, starting transfers between devices, _swap(): return lax.ppermute(x, 'core', [(0, 1), (1, 0)])  10.4 us
    ppermute x7, waiting for transfers between devices, _swap(): return lax.ppermute(x, 'core', [(0, 1), (1, 0)])  7.22 us
  transfers between devices with their start and end apart: 19, of which 10 were waited for; matrix products, arithmetic and copies ran while one was open for 0% of the time, Pallas kernels for 0%

profile of v4, /device:TPU:1, one launch (start us, length us, event | category | flops | bytes accessed | tf_op | source)
XLA Modules:
  0.0 131.0 jit_solution(10409509881343118094)
XLA Ops:
  0.6 0.9 broadcast_in_dim.4
  1.6 19.3 %all_to_all.25 = bf16[8,64,256]{2,1,0:T(8,128)(2,1)S(1)} all-to-all(bf16[8,64,256]{2,1,0:T(8,128)(2,1)S(1)} %broadcast_in_dim.4), channel_id=1, replica_groups=mesh['z'=8,'x'=4,'core'=2,'camp'=4] {'z'}, dimensions={0} | all-to-all | bytes 524288 | tf_op jit(solution)/shard_map/all_to_all | solution.py:236
  21.0 15.9 %all_to_all.26.part = bf16[4,8,64,256]{3,2,1,0:T(8,128)(2,1)S(1)} all-to-all(bf16[4,8,64,256]{3,2,1,0:T(8,128)(2,1)S(1)} %broadcast_in_dim.5), channel_id=1, replica_groups=mesh['z'=8,'x'=4,'core'=2,'camp'=4] {'x'}, dimensions={0} | all-to-all | bytes 2097152 | tf_op jit(solution)/shard_map/all_to_all | solution.py:236
  36.9 4.0 %collective-permute-start = (bf16[4,8,64,256]{3,2,1,0:T(8,128)(2,1)S(1)}, bf16[4,8,64,256]{3,2,1,0:T(8,128)(2,1)S(1)}, u32[]{:S(2)}, u32[]{:S(2)}) collective-permute-start(bf16[4,8,64,256]{3,2,1,0:T(8,128)(2,1)S(1)} %all_to_all.26.part), channel_id=1, source_target_pairs={{0,4},{4,0},{1,5},{5,1},{2,6},{6,2},{3,7},{7,3},{8,12},{12,8},{9,1... | collective-permute-start | bytes 3145736 | tf_op jit(solution)/shard_map/ppermute | solution.py:240
  41.9 1.3 collective-permute-done.peer
  43.2 9.0 %shard_map.94 = (bf16[256,128,128]{2,1,0:T(8,128)(2,1)}, f32[16,128]{1,0:T(8,128)S(1)}, f32[16,128]{1,0:T(8,128)S(1)}, f32[64,128]{1,0:T(8,128)S(1)}) custom-call(s32[1]{0:T(128)} %bitcast.core, s32[1,1]{1,0:T(1,128)S(6)} %copy.10.count, bf16[64,128,256]{2,1,0:T(8,128)(2,1)S(1)} %shard_map.93.users, bf16[4,8,64,256]{3,2,1,0:T(8,128)(2,1)S(1)} %all_to_all.26.part, ...), custom_call_target="tpu_custom_call" | custom-call | tf_op jit(solution)/shard_map/pallas_call | solution.py:214
  52.3 1.2 collective-permute-done.1.got
  53.4 0.7 shard_map.95
  54.2 3.9 %all-to-all-start.2 = ((f32[32,16,128]{2,1,0:T(8,128)}), f32[32,16,128]{2,1,0:T(8,128)S(1)}, u32[]{:S(2)}, u32[]{:S(2)}) async-start(f32[32,16,128]{2,1,0:T(8,128)} %shard_map.95), calls=%async_computation.2 | async-start | bytes 524288 | tf_op jit(solution)/shard_map/all_to_all | solution.py:253
  58.1 0.9 collective-permute-start.5
  59.0 3.1 %collective-permute-start.4 = (f32[64,128]{1,0:T(8,128)S(1)}, f32[64,128]{1,0:T(8,128)S(1)}, u32[]{:S(2)}, u32[]{:S(2)}) collective-permute-start(f32[64,128]{1,0:T(8,128)S(1)} %get-tuple-element.32.r0), channel_id=1, source_target_pairs={{2,0},{3,1},{0,2},{1,3},{6,4},{7,5},{4,6},{5,7},{10,8},{11,9},{8,1... | collective-permute-start | bytes 98312 | tf_op jit(solution)/shard_map/ppermute | solution.py:259
  62.4 7.5 %all-to-all-done.2.parts = f32[32,16,128]{2,1,0:T(8,128)S(1)} async-done(((f32[32,16,128]{2,1,0:T(8,128)}), f32[32,16,128]{2,1,0:T(8,128)S(1)}, u32[]{:S(2)}, u32[]{:S(2)}) %all-to-all-start.2) | async-done | bytes 262176 | tf_op jit(solution)/shard_map/all_to_all | solution.py:253
  70.0 2.1 %collective-permute-start.2 = (f32[16,128]{1,0:T(8,128)S(1)}, f32[16,128]{1,0:T(8,128)S(1)}, u32[]{:S(2)}, u32[]{:S(2)}) collective-permute-start(f32[16,128]{1,0:T(8,128)S(1)} %shard_map.96.own), channel_id=1, source_target_pairs={{0,4},{4,0},{1,5},{5,1},{2,6},{6,2},{3,7},{7,3},{8,12},{12,8},{9,1... | collective-permute-start | bytes 24584 | tf_op jit(solution)/shard_map/ppermute | solution.py:240
  72.1 0.8 collective-permute-done.2.other
  72.9 7.8 %shard_map.97 = (f32[16,128]{1,0:T(8,128)S(1)}, f32[16,128]{1,0:T(8,128)S(1)}, f32[64,128]{1,0:T(8,128)S(1)}, f32[32,128]{1,0:T(8,128)S(1)}, f32[64,128]{1,0:T(8,128)S(1)}) custom-call(s32[1]{0:T(128)} %bitcast.core, s32[1,256]{1,0:T(1,128)S(1)} %copy-done.3, s32[1,1]{1,0:T(1,128)S(6)} %copy.10.count, f32[16,128]{1,0:T(8,128)S(1)} %shard_map.96.own, ...), custom_call_target="tpu_custom_call" | custom-call | tf_op jit(solution)/shard_map/pallas_call | solution.py:214
  80.8 1.2 collective-permute-done.6.got
  82.0 0.7 shard_map.98
  82.7 3.9 %all-to-all-start.3 = ((f32[32,16,128]{2,1,0:T(8,128)}), f32[32,16,128]{2,1,0:T(8,128)S(1)}, u32[]{:S(2)}, u32[]{:S(2)}) async-start(f32[32,16,128]{2,1,0:T(8,128)} %shard_map.98), calls=%async_computation.3 | async-start | bytes 524288 | tf_op jit(solution)/shard_map/all_to_all | solution.py:253
  86.6 0.6 collective-permute-start.10
  87.2 3.4 %collective-permute-start.9 = (f32[64,128]{1,0:T(8,128)S(1)}, f32[64,128]{1,0:T(8,128)S(1)}, u32[]{:S(2)}, u32[]{:S(2)}) collective-permute-start(f32[64,128]{1,0:T(8,128)S(1)} %get-tuple-element.36.r0), channel_id=1, source_target_pairs={{2,0},{3,1},{0,2},{1,3},{6,4},{7,5},{4,6},{5,7},{10,8},{11,9},{8,1... | collective-permute-start | bytes 98312 | tf_op jit(solution)/shard_map/ppermute | solution.py:259
  90.6 7.9 %all-to-all-done.3.parts = f32[32,16,128]{2,1,0:T(8,128)S(1)} async-done(((f32[32,16,128]{2,1,0:T(8,128)}), f32[32,16,128]{2,1,0:T(8,128)S(1)}, u32[]{:S(2)}, u32[]{:S(2)}) %all-to-all-start.3) | async-done | bytes 262176 | tf_op jit(solution)/shard_map/all_to_all | solution.py:253
  98.6 2.0 %collective-permute-start.7 = (f32[16,128]{1,0:T(8,128)S(1)}, f32[16,128]{1,0:T(8,128)S(1)}, u32[]{:S(2)}, u32[]{:S(2)}) collective-permute-start(f32[16,128]{1,0:T(8,128)S(1)} %shard_map.99.own), channel_id=1, source_target_pairs={{0,4},{4,0},{1,5},{5,1},{2,6},{6,2},{3,7},{7,3},{8,12},{12,8},{9,1... | collective-permute-start | bytes 24584 | tf_op jit(solution)/shard_map/ppermute | solution.py:240
  100.6 0.8 collective-permute-done.7.other
  101.4 8.2 %shard_map.100 = (f32[16,128]{1,0:T(8,128)S(1)}, f32[16,128]{1,0:T(8,128)S(1)}, f32[2,64,128]{2,1,0:T(8,128)S(1)}, f32[32,128]{1,0:T(8,128)S(1)}, f32[64,128]{1,0:T(8,128)S(1)}) custom-call(s32[1]{0:T(128)} %bitcast.core, s32[1,256]{1,0:T(1,128)S(1)} %copy-done.3, s32[1,1]{1,0:T(1,128)S(6)} %copy.10.count, f32[16,128]{1,0:T(8,128)S(1)} %shard_map.99.own, ...), custom_call_target="tpu_custom_call" | custom-call | tf_op jit(solution)/shard_map/pallas_call | solution.py:214
  109.7 1.2 collective-permute-done.11.got
  110.9 0.7 shard_map.101
  111.6 3.9 %all-to-all-start.4 = ((f32[32,16,128]{2,1,0:T(8,128)}), f32[32,16,128]{2,1,0:T(8,128)S(1)}, u32[]{:S(2)}, u32[]{:S(2)}) async-start(f32[32,16,128]{2,1,0:T(8,128)} %shard_map.101), calls=%async_computation.4 | async-start | bytes 524288 | tf_op jit(solution)/shard_map/all_to_all | solution.py:253
  115.8 3.7 %collective-permute-start.14 = (f32[2,64,128]{2,1,0:T(8,128)S(1)}, f32[2,64,128]{2,1,0:T(8,128)S(1)}, u32[]{:S(2)}, u32[]{:S(2)}) collective-permute-start(f32[2,64,128]{2,1,0:T(8,128)S(1)} %get-tuple-element.41.p0), channel_id=1, source_target_pairs={{2,0},{3,1},{0,2},{1,3},{6,4},{7,5},{4,6},{5,7},{10,8},{11,9},{8,1... | collective-permute-start | bytes 196616 | tf_op jit(solution)/shard_map/ppermute | solution.py:259
  119.5 7.9 %all-to-all-done.4.parts = f32[32,16,128]{2,1,0:T(8,128)S(1)} async-done(((f32[32,16,128]{2,1,0:T(8,128)}), f32[32,16,128]{2,1,0:T(8,128)S(1)}, u32[]{:S(2)}, u32[]{:S(2)}) %all-to-all-start.4) | async-done | bytes 262176 | tf_op jit(solution)/shard_map/all_to_all | solution.py:253
  127.5 2.0 %collective-permute-start.12 = (f32[16,128]{1,0:T(8,128)S(1)}, f32[16,128]{1,0:T(8,128)S(1)}, u32[]{:S(2)}, u32[]{:S(2)}) collective-permute-start(f32[16,128]{1,0:T(8,128)S(1)} %shard_map.102.own), channel_id=1, source_target_pairs={{0,4},{4,0},{1,5},{5,1},{2,6},{6,2},{3,7},{7,3},{8,12},{12,8},{9,1... | collective-permute-start | bytes 24584 | tf_op jit(solution)/shard_map/ppermute | solution.py:240
  129.5 0.8 collective-permute-done.12.other
  130.3 0.7 shard_map.103
  (29 shorter events, 1.5 us)
Async XLA Ops:
  0.6 40.9 %copy-start = (bf16[8192,256]{1,0:T(8,128)(2,1)S(1)}, bf16[8192,256]{1,0:T(8,128)(2,1)}, u32[]{:S(2)}) copy-start(bf16[8192,256]{1,0:T(8,128)(2,1)} %param.6) | copy-start | bytes 12582916
  36.9 6.2 %collective-permute-start = (bf16[4,8,64,256]{3,2,1,0:T(8,128)(2,1)S(1)}, bf16[4,8,64,256]{3,2,1,0:T(8,128)(2,1)S(1)}, u32[]{:S(2)}, u32[]{:S(2)}) collective-permute-start(bf16[4,8,64,256]{3,2,1,0:T(8,128)(2,1)S(1)} %all_to_all.26.part), channel_id=1, source_target_pairs={{0,4},{4,0},{1,5},{5,1},{2,6},{6,2},{3,7},{7,3},{8,12},{12,8},{9,1... | collective-permute-start | bytes 3145736 | tf_op jit(solution)/shard_map/ppermute | solution.py:240
  41.5 1.6 %copy-start.3 = (s32[1,256]{1,0:T(1,128)S(1)}, s32[1,256]{1,0:T(1,128)}, u32[]{:S(2)}) copy-start(s32[1,256]{1,0:T(1,128)} %ids.3) | copy-start | bytes 3076
  41.8 31.1 %copy-start.1 = (s32[8192]{0:T(1024)S(1)}, s32[8192]{0:T(1024)}, u32[]{:S(2)}) copy-start(s32[8192]{0:T(1024)} %param.11) | copy-start | bytes 98308
  41.9 31.1 %copy-start.2 = (s32[4096]{0:T(1024)S(1)}, s32[4096]{0:T(1024)}, u32[]{:S(2)}) copy-start(s32[4096]{0:T(1024)} %param.10) | copy-start | bytes 49156
  52.2 1.3 collective-permute-start.1
  54.2 15.8 %all-to-all-start.2 = ((f32[32,16,128]{2,1,0:T(8,128)}), f32[32,16,128]{2,1,0:T(8,128)S(1)}, u32[]{:S(2)}, u32[]{:S(2)}) async-start(f32[32,16,128]{2,1,0:T(8,128)} %shard_map.95), calls=%async_computation.2 | async-start | bytes 524288 | tf_op jit(solution)/shard_map/all_to_all | solution.py:253
  58.1 14.0 %collective-permute-start.5 = (f32[64,128]{1,0:T(8,128)S(1)}, f32[64,128]{1,0:T(8,128)S(1)}, u32[]{:S(2)}, u32[]{:S(2)}) collective-permute-start(f32[64,128]{1,0:T(8,128)S(1)} %get-tuple-element.32.r0), channel_id=1, source_target_pairs={{3,0},{0,1},{1,2},{2,3},{7,4},{4,5},{5,6},{6,7},{11,8},{8,9},{9,10... | collective-permute-start | bytes 98312 | tf_op jit(solution)/shard_map/ppermute | solution.py:259
  59.0 13.1 %collective-permute-start.4 = (f32[64,128]{1,0:T(8,128)S(1)}, f32[64,128]{1,0:T(8,128)S(1)}, u32[]{:S(2)}, u32[]{:S(2)}) collective-permute-start(f32[64,128]{1,0:T(8,128)S(1)} %get-tuple-element.32.r0), channel_id=1, source_target_pairs={{2,0},{3,1},{0,2},{1,3},{6,4},{7,5},{4,6},{5,7},{10,8},{11,9},{8,1... | collective-permute-start | bytes 98312 | tf_op jit(solution)/shard_map/ppermute | solution.py:259
  62.1 10.0 %collective-permute-start.3 = (f32[64,128]{1,0:T(8,128)S(1)}, f32[64,128]{1,0:T(8,128)S(1)}, u32[]{:S(2)}, u32[]{:S(2)}) collective-permute-start(f32[64,128]{1,0:T(8,128)S(1)} %get-tuple-element.32.r0), channel_id=1, source_target_pairs={{1,0},{2,1},{3,2},{0,3},{5,4},{6,5},{7,6},{4,7},{9,8},{10,9},{11,1... | collective-permute-start | bytes 98312 | tf_op jit(solution)/shard_map/ppermute | solution.py:259
  70.0 2.9 %collective-permute-start.2 = (f32[16,128]{1,0:T(8,128)S(1)}, f32[16,128]{1,0:T(8,128)S(1)}, u32[]{:S(2)}, u32[]{:S(2)}) collective-permute-start(f32[16,128]{1,0:T(8,128)S(1)} %shard_map.96.own), channel_id=1, source_target_pairs={{0,4},{4,0},{1,5},{5,1},{2,6},{6,2},{3,7},{7,3},{8,12},{12,8},{9,1... | collective-permute-start | bytes 24584 | tf_op jit(solution)/shard_map/ppermute | solution.py:240
  80.7 1.3 collective-permute-start.6
  82.7 15.8 %all-to-all-start.3 = ((f32[32,16,128]{2,1,0:T(8,128)}), f32[32,16,128]{2,1,0:T(8,128)S(1)}, u32[]{:S(2)}, u32[]{:S(2)}) async-start(f32[32,16,128]{2,1,0:T(8,128)} %shard_map.98), calls=%async_computation.3 | async-start | bytes 524288 | tf_op jit(solution)/shard_map/all_to_all | solution.py:253
  86.6 14.0 %collective-permute-start.10 = (f32[64,128]{1,0:T(8,128)S(1)}, f32[64,128]{1,0:T(8,128)S(1)}, u32[]{:S(2)}, u32[]{:S(2)}) collective-permute-start(f32[64,128]{1,0:T(8,128)S(1)} %get-tuple-element.36.r0), channel_id=1, source_target_pairs={{3,0},{0,1},{1,2},{2,3},{7,4},{4,5},{5,6},{6,7},{11,8},{8,9},{9,10... | collective-permute-start | bytes 98312 | tf_op jit(solution)/shard_map/ppermute | solution.py:259
  87.2 13.4 %collective-permute-start.9 = (f32[64,128]{1,0:T(8,128)S(1)}, f32[64,128]{1,0:T(8,128)S(1)}, u32[]{:S(2)}, u32[]{:S(2)}) collective-permute-start(f32[64,128]{1,0:T(8,128)S(1)} %get-tuple-element.36.r0), channel_id=1, source_target_pairs={{2,0},{3,1},{0,2},{1,3},{6,4},{7,5},{4,6},{5,7},{10,8},{11,9},{8,1... | collective-permute-start | bytes 98312 | tf_op jit(solution)/shard_map/ppermute | solution.py:259
  90.6 10.0 %collective-permute-start.8 = (f32[64,128]{1,0:T(8,128)S(1)}, f32[64,128]{1,0:T(8,128)S(1)}, u32[]{:S(2)}, u32[]{:S(2)}) collective-permute-start(f32[64,128]{1,0:T(8,128)S(1)} %get-tuple-element.36.r0), channel_id=1, source_target_pairs={{1,0},{2,1},{3,2},{0,3},{5,4},{6,5},{7,6},{4,7},{9,8},{10,9},{11,1... | collective-permute-start | bytes 98312 | tf_op jit(solution)/shard_map/ppermute | solution.py:259
  98.6 2.9 %collective-permute-start.7 = (f32[16,128]{1,0:T(8,128)S(1)}, f32[16,128]{1,0:T(8,128)S(1)}, u32[]{:S(2)}, u32[]{:S(2)}) collective-permute-start(f32[16,128]{1,0:T(8,128)S(1)} %shard_map.99.own), channel_id=1, source_target_pairs={{0,4},{4,0},{1,5},{5,1},{2,6},{6,2},{3,7},{7,3},{8,12},{12,8},{9,1... | collective-permute-start | bytes 24584 | tf_op jit(solution)/shard_map/ppermute | solution.py:240
  109.6 1.3 collective-permute-start.11
  111.6 15.8 %all-to-all-start.4 = ((f32[32,16,128]{2,1,0:T(8,128)}), f32[32,16,128]{2,1,0:T(8,128)S(1)}, u32[]{:S(2)}, u32[]{:S(2)}) async-start(f32[32,16,128]{2,1,0:T(8,128)} %shard_map.101), calls=%async_computation.4 | async-start | bytes 524288 | tf_op jit(solution)/shard_map/all_to_all | solution.py:253
  115.5 14.0 %collective-permute-start.15 = (f32[2,64,128]{2,1,0:T(8,128)S(1)}, f32[2,64,128]{2,1,0:T(8,128)S(1)}, u32[]{:S(2)}, u32[]{:S(2)}) collective-permute-start(f32[2,64,128]{2,1,0:T(8,128)S(1)} %get-tuple-element.41.p0), channel_id=1, source_target_pairs={{3,0},{0,1},{1,2},{2,3},{7,4},{4,5},{5,6},{6,7},{11,8},{8,9},{9,10... | collective-permute-start | bytes 196616 | tf_op jit(solution)/shard_map/ppermute | solution.py:259
  115.8 13.7 %collective-permute-start.14 = (f32[2,64,128]{2,1,0:T(8,128)S(1)}, f32[2,64,128]{2,1,0:T(8,128)S(1)}, u32[]{:S(2)}, u32[]{:S(2)}) collective-permute-start(f32[2,64,128]{2,1,0:T(8,128)S(1)} %get-tuple-element.41.p0), channel_id=1, source_target_pairs={{2,0},{3,1},{0,2},{1,3},{6,4},{7,5},{4,6},{5,7},{10,8},{11,9},{8,1... | collective-permute-start | bytes 196616 | tf_op jit(solution)/shard_map/ppermute | solution.py:259
  119.5 10.0 %collective-permute-start.13 = (f32[2,64,128]{2,1,0:T(8,128)S(1)}, f32[2,64,128]{2,1,0:T(8,128)S(1)}, u32[]{:S(2)}, u32[]{:S(2)}) collective-permute-start(f32[2,64,128]{2,1,0:T(8,128)S(1)} %get-tuple-element.41.p0), channel_id=1, source_target_pairs={{1,0},{2,1},{3,2},{0,3},{5,4},{6,5},{7,6},{4,7},{9,8},{10,9},{11,1... | collective-permute-start | bytes 196616 | tf_op jit(solution)/shard_map/ppermute | solution.py:259
  127.5 2.9 %collective-permute-start.12 = (f32[16,128]{1,0:T(8,128)S(1)}, f32[16,128]{1,0:T(8,128)S(1)}, u32[]{:S(2)}, u32[]{:S(2)}) collective-permute-start(f32[16,128]{1,0:T(8,128)S(1)} %shard_map.102.own), channel_id=1, source_target_pairs={{0,4},{4,0},{1,5},{5,1},{2,6},{6,2},{3,7},{7,3},{8,12},{12,8},{9,1... | collective-permute-start | bytes 24584 | tf_op jit(solution)/shard_map/ppermute | solution.py:240

commit v5 on v4

--- a/solution.py
+++ b/solution.py
@@ -11,11 +11,11 @@
 UB = 64
 CB = 32
 NZ, NX, NCORE, NCAMP = 8, 4, 2, 4
-UNROLL = 4
+UNROLL = 32
 GROUP = 32
 WIDE = 50
 FIRST = 43
-AHEAD = 2
+AHEAD = 8
 F32 = jnp.float32
 
 

time: 132 us -> 129 us (0.977)
  starting transfers between devices: 34.4 us -> 43.5 us
  Pallas kernels: 28.2 us -> 22.2 us
  waiting for transfers between devices: 30.6 us -> 24.9 us
    pallas_call x11, Pallas kernels: 28.2 us -> 22.2 us  [_call(): pl.pallas_call(kernel, in_specs=[SMEM] * n_smem + [VMEM] * (len(args) - n...]
    all_to_all x3, waiting for transfers between devices: 23.4 us -> 18.6 us  [_sum_load(): wide = lax.all_to_all(wide, ('z', 'x'), 0, 0, tiled=True)]
    ppermute x9, starting transfers between devices: 12.4 us -> 16.4 us  [_shift(): return lax.ppermute(x, 'camp', [((i + k) % NCAMP, i) for i in range(NCAMP)])]
    all_to_all x3, starting transfers between devices: 11.6 us -> 14.7 us  [_sum_load(): wide = lax.all_to_all(wide, ('z', 'x'), 0, 0, tiled=True)]
    ppermute x7, starting transfers between devices: 10.4 us -> 12.4 us  [_swap(): return lax.ppermute(x, 'core', [(0, 1), (1, 0)])]
where the time goes in v5:
time: 129 us; the launch traced here: 128 us
  starting transfers between devices  43.5 us (34%)
  blocking collectives  35.2 us (27%)
  waiting for transfers between devices  24.9 us (19%)
  Pallas kernels  22.2 us (17%)
  between operations  1.43 us (1%)
    all_to_all x2, blocking collectives, _spread(): lax.all_to_all(jnp.broadcast_to(x[None], (n,) + x.shape), axes, 0, 0, til...  35.2 us
    pallas_call x11, Pallas kernels, _call(): pl.pallas_call(kernel, in_specs=[SMEM] * n_smem + [VMEM] * (len(args) - n...  22.2 us
    all_to_all x3, waiting for transfers between devices, _sum_load(): wide = lax.all_to_all(wide, ('z', 'x'), 0, 0, tiled=True)  18.6 us
    ppermute x9, starting transfers between devices, _shift(): return lax.ppermute(x, 'camp', [((i + k) % NCAMP, i) for i in range(NCAMP)])  16.4 us
    all_to_all x3, starting transfers between devices, _sum_load(): wide = lax.all_to_all(wide, ('z', 'x'), 0, 0, tiled=True)  14.7 us
    ppermute x7, starting transfers between devices, _swap(): return lax.ppermute(x, 'core', [(0, 1), (1, 0)])  12.4 us
    ppermute x7, waiting for transfers between devices, _swap(): return lax.ppermute(x, 'core', [(0, 1), (1, 0)])  6.23 us
  transfers between devices with their start and end apart: 19, of which 10 were waited for; matrix products, arithmetic and copies ran while one was open for 0% of the time, Pallas kernels for 0%

profile of v5, /device:TPU:1, one launch (start us, length us, event | category | flops | bytes accessed | tf_op | source)
XLA Modules:
  0.0 128.3 jit_solution(1297756756046517892)
XLA Ops:
  0.6 0.9 broadcast_in_dim.4
  1.6 19.3 %all_to_all.25 = bf16[8,64,256]{2,1,0:T(8,128)(2,1)S(1)} all-to-all(bf16[8,64,256]{2,1,0:T(8,128)(2,1)S(1)} %broadcast_in_dim.4), channel_id=1, replica_groups=mesh['z'=8,'x'=4,'core'=2,'camp'=4] {'z'}, dimensions={0} | all-to-all | bytes 524288 | tf_op jit(solution)/shard_map/all_to_all | solution.py:236
  21.0 15.9 %all_to_all.26.part = bf16[4,8,64,256]{3,2,1,0:T(8,128)(2,1)S(1)} all-to-all(bf16[4,8,64,256]{3,2,1,0:T(8,128)(2,1)S(1)} %broadcast_in_dim.5), channel_id=1, replica_groups=mesh['z'=8,'x'=4,'core'=2,'camp'=4] {'x'}, dimensions={0} | all-to-all | bytes 2097152 | tf_op jit(solution)/shard_map/all_to_all | solution.py:236
  36.9 4.0 %collective-permute-start = (bf16[4,8,64,256]{3,2,1,0:T(8,128)(2,1)S(1)}, bf16[4,8,64,256]{3,2,1,0:T(8,128)(2,1)S(1)}, u32[]{:S(2)}, u32[]{:S(2)}) collective-permute-start(bf16[4,8,64,256]{3,2,1,0:T(8,128)(2,1)S(1)} %all_to_all.26.part), channel_id=1, source_target_pairs={{0,4},{4,0},{1,5},{5,1},{2,6},{6,2},{3,7},{7,3},{8,12},{12,8},{9,1... | collective-permute-start | bytes 3145736 | tf_op jit(solution)/shard_map/ppermute | solution.py:240
  41.9 1.3 %collective-permute-done.peer = bf16[4,8,64,256]{3,2,1,0:T(8,128)(2,1)S(1)} collective-permute-done((bf16[4,8,64,256]{3,2,1,0:T(8,128)(2,1)S(1)}, bf16[4,8,64,256]{3,2,1,0:T(8,128)(2,1)S(1)}, u32[]{:S(2)}, u32[]{:S(2)}) %collective-permute-start) | collective-permute-done | bytes 1048608 | tf_op jit(solution)/shard_map/ppermute | solution.py:240
  43.2 7.2 %shard_map.94 = (bf16[256,128,128]{2,1,0:T(8,128)(2,1)}, f32[16,128]{1,0:T(8,128)S(1)}, f32[16,128]{1,0:T(8,128)S(1)}, f32[64,128]{1,0:T(8,128)S(1)}) custom-call(s32[1]{0:T(128)} %bitcast.core, s32[1,1]{1,0:T(1,128)S(6)} %copy.10.count, bf16[64,128,256]{2,1,0:T(8,128)(2,1)S(1)} %shard_map.93.users, bf16[4,8,64,256]{3,2,1,0:T(8,128)(2,1)S(1)} %all_to_all.26.part, ...), custom_call_target="tpu_custom_call" | custom-call | tf_op jit(solution)/shard_map/pallas_call | solution.py:214
  50.8 0.8 collective-permute-done.1.got
  52.4 5.6 %all-to-all-start.2 = ((f32[32,16,128]{2,1,0:T(8,128)}), f32[32,16,128]{2,1,0:T(8,128)S(1)}, u32[]{:S(2)}, u32[]{:S(2)}) async-start(f32[32,16,128]{2,1,0:T(8,128)} %shard_map.95), calls=%async_computation.2 | async-start | bytes 524288 | tf_op jit(solution)/shard_map/all_to_all | solution.py:253
  58.0 1.5 %collective-permute-start.5 = (f32[64,128]{1,0:T(8,128)S(1)}, f32[64,128]{1,0:T(8,128)S(1)}, u32[]{:S(2)}, u32[]{:S(2)}) collective-permute-start(f32[64,128]{1,0:T(8,128)S(1)} %get-tuple-element.32.r0), channel_id=1, source_target_pairs={{3,0},{0,1},{1,2},{2,3},{7,4},{4,5},{5,6},{6,7},{11,8},{8,9},{9,10... | collective-permute-start | bytes 98312 | tf_op jit(solution)/shard_map/ppermute | solution.py:259
  59.5 2.6 %collective-permute-start.4 = (f32[64,128]{1,0:T(8,128)S(1)}, f32[64,128]{1,0:T(8,128)S(1)}, u32[]{:S(2)}, u32[]{:S(2)}) collective-permute-start(f32[64,128]{1,0:T(8,128)S(1)} %get-tuple-element.32.r0), channel_id=1, source_target_pairs={{2,0},{3,1},{0,2},{1,3},{6,4},{7,5},{4,6},{5,7},{10,8},{11,9},{8,1... | collective-permute-start | bytes 98312 | tf_op jit(solution)/shard_map/ppermute | solution.py:259
  62.1 1.0 collective-permute-start.3
  63.1 6.7 %all-to-all-done.2.parts = f32[32,16,128]{2,1,0:T(8,128)S(1)} async-done(((f32[32,16,128]{2,1,0:T(8,128)}), f32[32,16,128]{2,1,0:T(8,128)S(1)}, u32[]{:S(2)}, u32[]{:S(2)}) %all-to-all-start.2) | async-done | bytes 262176 | tf_op jit(solution)/shard_map/all_to_all | solution.py:253
  69.8 2.2 %collective-permute-start.2 = (f32[16,128]{1,0:T(8,128)S(1)}, f32[16,128]{1,0:T(8,128)S(1)}, u32[]{:S(2)}, u32[]{:S(2)}) collective-permute-start(f32[16,128]{1,0:T(8,128)S(1)} %shard_map.96.own), channel_id=1, source_target_pairs={{0,4},{4,0},{1,5},{5,1},{2,6},{6,2},{3,7},{7,3},{8,12},{12,8},{9,1... | collective-permute-start | bytes 24584 | tf_op jit(solution)/shard_map/ppermute | solution.py:240
  72.1 0.8 collective-permute-done.2.other
  72.9 5.4 %shard_map.97 = (f32[16,128]{1,0:T(8,128)S(1)}, f32[16,128]{1,0:T(8,128)S(1)}, f32[64,128]{1,0:T(8,128)S(1)}, f32[32,128]{1,0:T(8,128)S(1)}, f32[64,128]{1,0:T(8,128)S(1)}) custom-call(s32[1]{0:T(128)} %bitcast.core, s32[1,256]{1,0:T(1,128)S(1)} %copy-done.3, s32[1,1]{1,0:T(1,128)S(6)} %copy.10.count, f32[16,128]{1,0:T(8,128)S(1)} %shard_map.96.own, ...), custom_call_target="tpu_custom_call" | custom-call | tf_op jit(solution)/shard_map/pallas_call | solution.py:214
  78.8 0.8 collective-permute-done.6.got
  80.3 4.4 %all-to-all-start.3 = ((f32[32,16,128]{2,1,0:T(8,128)}), f32[32,16,128]{2,1,0:T(8,128)S(1)}, u32[]{:S(2)}, u32[]{:S(2)}) async-start(f32[32,16,128]{2,1,0:T(8,128)} %shard_map.98), calls=%async_computation.3 | async-start | bytes 524288 | tf_op jit(solution)/shard_map/all_to_all | solution.py:253
  84.7 1.8 %collective-permute-start.10 = (f32[64,128]{1,0:T(8,128)S(1)}, f32[64,128]{1,0:T(8,128)S(1)}, u32[]{:S(2)}, u32[]{:S(2)}) collective-permute-start(f32[64,128]{1,0:T(8,128)S(1)} %get-tuple-element.36.r0), channel_id=1, source_target_pairs={{3,0},{0,1},{1,2},{2,3},{7,4},{4,5},{5,6},{6,7},{11,8},{8,9},{9,10... | collective-permute-start | bytes 98312 | tf_op jit(solution)/shard_map/ppermute | solution.py:259
  86.5 2.6 %collective-permute-start.9 = (f32[64,128]{1,0:T(8,128)S(1)}, f32[64,128]{1,0:T(8,128)S(1)}, u32[]{:S(2)}, u32[]{:S(2)}) collective-permute-start(f32[64,128]{1,0:T(8,128)S(1)} %get-tuple-element.36.r0), channel_id=1, source_target_pairs={{2,0},{3,1},{0,2},{1,3},{6,4},{7,5},{4,6},{5,7},{10,8},{11,9},{8,1... | collective-permute-start | bytes 98312 | tf_op jit(solution)/shard_map/ppermute | solution.py:259
  89.1 1.0 collective-permute-start.8
  90.2 6.1 %all-to-all-done.3.parts = f32[32,16,128]{2,1,0:T(8,128)S(1)} async-done(((f32[32,16,128]{2,1,0:T(8,128)}), f32[32,16,128]{2,1,0:T(8,128)S(1)}, u32[]{:S(2)}, u32[]{:S(2)}) %all-to-all-start.3) | async-done | bytes 262176 | tf_op jit(solution)/shard_map/all_to_all | solution.py:253
  96.3 2.5 %collective-permute-start.7 = (f32[16,128]{1,0:T(8,128)S(1)}, f32[16,128]{1,0:T(8,128)S(1)}, u32[]{:S(2)}, u32[]{:S(2)}) collective-permute-start(f32[16,128]{1,0:T(8,128)S(1)} %shard_map.99.own), channel_id=1, source_target_pairs={{0,4},{4,0},{1,5},{5,1},{2,6},{6,2},{3,7},{7,3},{8,12},{12,8},{9,1... | collective-permute-start | bytes 24584 | tf_op jit(solution)/shard_map/ppermute | solution.py:240
  98.9 0.8 collective-permute-done.7.other
  99.7 6.3 %shard_map.100 = (f32[16,128]{1,0:T(8,128)S(1)}, f32[16,128]{1,0:T(8,128)S(1)}, f32[2,64,128]{2,1,0:T(8,128)S(1)}, f32[32,128]{1,0:T(8,128)S(1)}, f32[64,128]{1,0:T(8,128)S(1)}) custom-call(s32[1]{0:T(128)} %bitcast.core, s32[1,256]{1,0:T(1,128)S(1)} %copy-done.3, s32[1,1]{1,0:T(1,128)S(6)} %copy.10.count, f32[16,128]{1,0:T(8,128)S(1)} %shard_map.99.own, ...), custom_call_target="tpu_custom_call" | custom-call | tf_op jit(solution)/shard_map/pallas_call | solution.py:214
  106.5 0.8 collective-permute-done.11.got
  108.0 4.7 %all-to-all-start.4 = ((f32[32,16,128]{2,1,0:T(8,128)}), f32[32,16,128]{2,1,0:T(8,128)S(1)}, u32[]{:S(2)}, u32[]{:S(2)}) async-start(f32[32,16,128]{2,1,0:T(8,128)} %shard_map.101), calls=%async_computation.4 | async-start | bytes 524288 | tf_op jit(solution)/shard_map/all_to_all | solution.py:253
  112.8 2.1 %collective-permute-start.15 = (f32[2,64,128]{2,1,0:T(8,128)S(1)}, f32[2,64,128]{2,1,0:T(8,128)S(1)}, u32[]{:S(2)}, u32[]{:S(2)}) collective-permute-start(f32[2,64,128]{2,1,0:T(8,128)S(1)} %get-tuple-element.41.p0), channel_id=1, source_target_pairs={{3,0},{0,1},{1,2},{2,3},{7,4},{4,5},{5,6},{6,7},{11,8},{8,9},{9,10... | collective-permute-start | bytes 196616 | tf_op jit(solution)/shard_map/ppermute | solution.py:259
  114.9 2.6 %collective-permute-start.14 = (f32[2,64,128]{2,1,0:T(8,128)S(1)}, f32[2,64,128]{2,1,0:T(8,128)S(1)}, u32[]{:S(2)}, u32[]{:S(2)}) collective-permute-start(f32[2,64,128]{2,1,0:T(8,128)S(1)} %get-tuple-element.41.p0), channel_id=1, source_target_pairs={{2,0},{3,1},{0,2},{1,3},{6,4},{7,5},{4,6},{5,7},{10,8},{11,9},{8,1... | collective-permute-start | bytes 196616 | tf_op jit(solution)/shard_map/ppermute | solution.py:259
  117.5 1.0 collective-permute-start.13
  118.5 5.8 %all-to-all-done.4.parts = f32[32,16,128]{2,1,0:T(8,128)S(1)} async-done(((f32[32,16,128]{2,1,0:T(8,128)}), f32[32,16,128]{2,1,0:T(8,128)S(1)}, u32[]{:S(2)}, u32[]{:S(2)}) %all-to-all-start.4) | async-done | bytes 262176 | tf_op jit(solution)/shard_map/all_to_all | solution.py:253
  124.4 2.4 %collective-permute-start.12 = (f32[16,128]{1,0:T(8,128)S(1)}, f32[16,128]{1,0:T(8,128)S(1)}, u32[]{:S(2)}, u32[]{:S(2)}) collective-permute-start(f32[16,128]{1,0:T(8,128)S(1)} %shard_map.102.own), channel_id=1, source_target_pairs={{0,4},{4,0},{1,5},{5,1},{2,6},{6,2},{3,7},{7,3},{8,12},{12,8},{9,1... | collective-permute-start | bytes 24584 | tf_op jit(solution)/shard_map/ppermute | solution.py:240
  126.8 0.8 collective-permute-done.12.other
  (29 shorter events, 4.7 us)
Async XLA Ops:
  0.6 40.9 %copy-start = (bf16[8192,256]{1,0:T(8,128)(2,1)S(1)}, bf16[8192,256]{1,0:T(8,128)(2,1)}, u32[]{:S(2)}) copy-start(bf16[8192,256]{1,0:T(8,128)(2,1)} %param.6) | copy-start | bytes 12582916
  36.9 6.2 %collective-permute-start = (bf16[4,8,64,256]{3,2,1,0:T(8,128)(2,1)S(1)}, bf16[4,8,64,256]{3,2,1,0:T(8,128)(2,1)S(1)}, u32[]{:S(2)}, u32[]{:S(2)}) collective-permute-start(bf16[4,8,64,256]{3,2,1,0:T(8,128)(2,1)S(1)} %all_to_all.26.part), channel_id=1, source_target_pairs={{0,4},{4,0},{1,5},{5,1},{2,6},{6,2},{3,7},{7,3},{8,12},{12,8},{9,1... | collective-permute-start | bytes 3145736 | tf_op jit(solution)/shard_map/ppermute | solution.py:240
  41.5 1.6 %copy-start.3 = (s32[1,256]{1,0:T(1,128)S(1)}, s32[1,256]{1,0:T(1,128)}, u32[]{:S(2)}) copy-start(s32[1,256]{1,0:T(1,128)} %ids.3) | copy-start | bytes 3076
  41.8 31.1 %copy-start.1 = (s32[8192]{0:T(1024)S(1)}, s32[8192]{0:T(1024)}, u32[]{:S(2)}) copy-start(s32[8192]{0:T(1024)} %param.11) | copy-start | bytes 98308
  41.9 31.0 %copy-start.2 = (s32[4096]{0:T(1024)S(1)}, s32[4096]{0:T(1024)}, u32[]{:S(2)}) copy-start(s32[4096]{0:T(1024)} %param.10) | copy-start | bytes 49156
  50.3 1.3 %collective-permute-start.1 = (f32[16,128]{1,0:T(8,128)S(1)}, f32[16,128]{1,0:T(8,128)S(1)}, u32[]{:S(2)}, u32[]{:S(2)}) collective-permute-start(f32[16,128]{1,0:T(8,128)S(1)} %get-tuple-element.31), channel_id=1, source_target_pairs={{0,4},{4,0},{1,5},{5,1},{2,6},{6,2},{3,7},{7,3},{8,12},{12,8},{9,1... | collective-permute-start | bytes 24584 | tf_op jit(solution)/shard_map/ppermute | solution.py:240
  52.4 17.4 %all-to-all-start.2 = ((f32[32,16,128]{2,1,0:T(8,128)}), f32[32,16,128]{2,1,0:T(8,128)S(1)}, u32[]{:S(2)}, u32[]{:S(2)}) async-start(f32[32,16,128]{2,1,0:T(8,128)} %shard_map.95), calls=%async_computation.2 | async-start | bytes 524288 | tf_op jit(solution)/shard_map/all_to_all | solution.py:253
  58.0 14.1 %collective-permute-start.5 = (f32[64,128]{1,0:T(8,128)S(1)}, f32[64,128]{1,0:T(8,128)S(1)}, u32[]{:S(2)}, u32[]{:S(2)}) collective-permute-start(f32[64,128]{1,0:T(8,128)S(1)} %get-tuple-element.32.r0), channel_id=1, source_target_pairs={{3,0},{0,1},{1,2},{2,3},{7,4},{4,5},{5,6},{6,7},{11,8},{8,9},{9,10... | collective-permute-start | bytes 98312 | tf_op jit(solution)/shard_map/ppermute | solution.py:259
  59.5 12.6 %collective-permute-start.4 = (f32[64,128]{1,0:T(8,128)S(1)}, f32[64,128]{1,0:T(8,128)S(1)}, u32[]{:S(2)}, u32[]{:S(2)}) collective-permute-start(f32[64,128]{1,0:T(8,128)S(1)} %get-tuple-element.32.r0), channel_id=1, source_target_pairs={{2,0},{3,1},{0,2},{1,3},{6,4},{7,5},{4,6},{5,7},{10,8},{11,9},{8,1... | collective-permute-start | bytes 98312 | tf_op jit(solution)/shard_map/ppermute | solution.py:259
  62.1 10.0 %collective-permute-start.3 = (f32[64,128]{1,0:T(8,128)S(1)}, f32[64,128]{1,0:T(8,128)S(1)}, u32[]{:S(2)}, u32[]{:S(2)}) collective-permute-start(f32[64,128]{1,0:T(8,128)S(1)} %get-tuple-element.32.r0), channel_id=1, source_target_pairs={{1,0},{2,1},{3,2},{0,3},{5,4},{6,5},{7,6},{4,7},{9,8},{10,9},{11,1... | collective-permute-start | bytes 98312 | tf_op jit(solution)/shard_map/ppermute | solution.py:259
  69.8 3.1 %collective-permute-start.2 = (f32[16,128]{1,0:T(8,128)S(1)}, f32[16,128]{1,0:T(8,128)S(1)}, u32[]{:S(2)}, u32[]{:S(2)}) collective-permute-start(f32[16,128]{1,0:T(8,128)S(1)} %shard_map.96.own), channel_id=1, source_target_pairs={{0,4},{4,0},{1,5},{5,1},{2,6},{6,2},{3,7},{7,3},{8,12},{12,8},{9,1... | collective-permute-start | bytes 24584 | tf_op jit(solution)/shard_map/ppermute | solution.py:240
  78.3 1.3 collective-permute-start.6
  80.3 16.0 %all-to-all-start.3 = ((f32[32,16,128]{2,1,0:T(8,128)}), f32[32,16,128]{2,1,0:T(8,128)S(1)}, u32[]{:S(2)}, u32[]{:S(2)}) async-start(f32[32,16,128]{2,1,0:T(8,128)} %shard_map.98), calls=%async_computation.3 | async-start | bytes 524288 | tf_op jit(solution)/shard_map/all_to_all | solution.py:253
  84.7 14.2 %collective-permute-start.10 = (f32[64,128]{1,0:T(8,128)S(1)}, f32[64,128]{1,0:T(8,128)S(1)}, u32[]{:S(2)}, u32[]{:S(2)}) collective-permute-start(f32[64,128]{1,0:T(8,128)S(1)} %get-tuple-element.36.r0), channel_id=1, source_target_pairs={{3,0},{0,1},{1,2},{2,3},{7,4},{4,5},{5,6},{6,7},{11,8},{8,9},{9,10... | collective-permute-start | bytes 98312 | tf_op jit(solution)/shard_map/ppermute | solution.py:259
  86.5 12.4 %collective-permute-start.9 = (f32[64,128]{1,0:T(8,128)S(1)}, f32[64,128]{1,0:T(8,128)S(1)}, u32[]{:S(2)}, u32[]{:S(2)}) collective-permute-start(f32[64,128]{1,0:T(8,128)S(1)} %get-tuple-element.36.r0), channel_id=1, source_target_pairs={{2,0},{3,1},{0,2},{1,3},{6,4},{7,5},{4,6},{5,7},{10,8},{11,9},{8,1... | collective-permute-start | bytes 98312 | tf_op jit(solution)/shard_map/ppermute | solution.py:259
  89.1 9.8 %collective-permute-start.8 = (f32[64,128]{1,0:T(8,128)S(1)}, f32[64,128]{1,0:T(8,128)S(1)}, u32[]{:S(2)}, u32[]{:S(2)}) collective-permute-start(f32[64,128]{1,0:T(8,128)S(1)} %get-tuple-element.36.r0), channel_id=1, source_target_pairs={{1,0},{2,1},{3,2},{0,3},{5,4},{6,5},{7,6},{4,7},{9,8},{10,9},{11,1... | collective-permute-start | bytes 98312 | tf_op jit(solution)/shard_map/ppermute | solution.py:259
  96.3 3.4 %collective-permute-start.7 = (f32[16,128]{1,0:T(8,128)S(1)}, f32[16,128]{1,0:T(8,128)S(1)}, u32[]{:S(2)}, u32[]{:S(2)}) collective-permute-start(f32[16,128]{1,0:T(8,128)S(1)} %shard_map.99.own), channel_id=1, source_target_pairs={{0,4},{4,0},{1,5},{5,1},{2,6},{6,2},{3,7},{7,3},{8,12},{12,8},{9,1... | collective-permute-start | bytes 24584 | tf_op jit(solution)/shard_map/ppermute | solution.py:240
  106.0 1.3 collective-permute-start.11
  108.0 16.4 %all-to-all-start.4 = ((f32[32,16,128]{2,1,0:T(8,128)}), f32[32,16,128]{2,1,0:T(8,128)S(1)}, u32[]{:S(2)}, u32[]{:S(2)}) async-start(f32[32,16,128]{2,1,0:T(8,128)} %shard_map.101), calls=%async_computation.4 | async-start | bytes 524288 | tf_op jit(solution)/shard_map/all_to_all | solution.py:253
  112.8 14.0 %collective-permute-start.15 = (f32[2,64,128]{2,1,0:T(8,128)S(1)}, f32[2,64,128]{2,1,0:T(8,128)S(1)}, u32[]{:S(2)}, u32[]{:S(2)}) collective-permute-start(f32[2,64,128]{2,1,0:T(8,128)S(1)} %get-tuple-element.41.p0), channel_id=1, source_target_pairs={{3,0},{0,1},{1,2},{2,3},{7,4},{4,5},{5,6},{6,7},{11,8},{8,9},{9,10... | collective-permute-start | bytes 196616 | tf_op jit(solution)/shard_map/ppermute | solution.py:259
  114.9 11.9 %collective-permute-start.14 = (f32[2,64,128]{2,1,0:T(8,128)S(1)}, f32[2,64,128]{2,1,0:T(8,128)S(1)}, u32[]{:S(2)}, u32[]{:S(2)}) collective-permute-start(f32[2,64,128]{2,1,0:T(8,128)S(1)} %get-tuple-element.41.p0), channel_id=1, source_target_pairs={{2,0},{3,1},{0,2},{1,3},{6,4},{7,5},{4,6},{5,7},{10,8},{11,9},{8,1... | collective-permute-start | bytes 196616 | tf_op jit(solution)/shard_map/ppermute | solution.py:259
  117.5 9.3 %collective-permute-start.13 = (f32[2,64,128]{2,1,0:T(8,128)S(1)}, f32[2,64,128]{2,1,0:T(8,128)S(1)}, u32[]{:S(2)}, u32[]{:S(2)}) collective-permute-start(f32[2,64,128]{2,1,0:T(8,128)S(1)} %get-tuple-element.41.p0), channel_id=1, source_target_pairs={{1,0},{2,1},{3,2},{0,3},{5,4},{6,5},{7,6},{4,7},{9,8},{10,9},{11,1... | collective-permute-start | bytes 196616 | tf_op jit(solution)/shard_map/ppermute | solution.py:259
  124.4 3.2 %collective-permute-start.12 = (f32[16,128]{1,0:T(8,128)S(1)}, f32[16,128]{1,0:T(8,128)S(1)}, u32[]{:S(2)}, u32[]{:S(2)}) collective-permute-start(f32[16,128]{1,0:T(8,128)S(1)} %shard_map.102.own), channel_id=1, source_target_pairs={{0,4},{4,0},{1,5},{5,1},{2,6},{6,2},{3,7},{7,3},{8,12},{12,8},{9,1... | collective-permute-start | bytes 24584 | tf_op jit(solution)/shard_map/ppermute | solution.py:240

commit v6 on v0

v6 whole, which is shorter than its diff:
```python
import jax
import jax.numpy as jnp
from jax import lax
from jax.experimental import pallas as pl
from jax.experimental.pallas import tpu as pltpu
from jax.sharding import Mesh, PartitionSpec as P

BLOCK = 128
PART = 64
E = 256
SLOTS = 256
UB = 64
UB2 = 128
CB = 32
NZ, NX, NCORE, NCAMP = 8, 4, 2, 4
GROUP = 32
STEP = 32
CHUNKS = SLOTS // GROUP
WIDE = 50
FIRST = 50
F32 = jnp.float32


def _each(turns, do):
    def turn(g, carry):
        do(g)
        return carry

    lax.fori_loop(0, turns, turn, 0)


def _clear(*accs):
    for acc in accs:
        if acc is not None:
            acc[...] = jnp.zeros_like(acc)


def _chunk(src, dst, sems, g):
    at = pl.ds(g * GROUP, GROUP)
    return pltpu.make_async_copy(src.at[at], dst.at[at], sems.at[g])


def _fold(x):
    return x.reshape(PART // 8, 8, BLOCK).sum(0)


def _finish_load(lacc, out):
    def turn(r, carry):
        both = lacc[pl.ds(2 * r, 2)].reshape(BLOCK, BLOCK)
        out[pl.ds(r, 1), :] = jnp.sum(both.T, axis=0, keepdims=True)
        return carry

    lax.fori_loop(0, CB // 2, turn, 0, unroll=4)


def _turns(cnt):
    return (cnt + GROUP - 1) // GROUP


def _group(ids, cnt, first, size):
    out = []
    for k in range(size):
        slot = first + k
        code = ids[0, slot]
        out.append((slot, code >> 5, code & (CB - 1), slot < cnt))
    return out


def first_kernel(count0, count1, part, codes0, codes1, from0, from1, kept, load, rows, lacc, racc, scores, ids0, ids1,
                 users0, users1, fetched, stored):
    fetches = [
        pltpu.make_async_copy(src, dst, fetched.at[k])
        for k, (src, dst) in enumerate(((codes0, ids0), (from0, users0), (codes1, ids1), (from1, users1)))
    ]
    for fetch in fetches:
        fetch.start()
    _clear(lacc, racc)

    for which, (ids, count, users) in enumerate(((ids0, count0, users0), (ids1, count1, users1))):
        cnt = count[0, 0]
        turns = _turns(cnt)
        base = which * SLOTS
        fetches[2 * which].wait()
        fetches[2 * which + 1].wait()

        def products(g, ids=ids, cnt=cnt, users=users):
            return [
                lax.dot_general(
                    part[cb & (NX - 1), cb >> 2], users[ub], (((1,), (1,)), ((), ())), preferred_element_type=F32
                ).astype(jnp.bfloat16)
                for _, ub, cb, _ in _group(ids, cnt, g * GROUP, GROUP)
            ]

        def store(g, blocks, which=which, base=base):
            for k, block in enumerate(blocks):
                scores[base + g * GROUP + k] = block
            _chunk(scores, kept, stored, which * CHUNKS + g).start()

        def add(g, ids=ids, cnt=cnt, which=which, base=base):
            for slot, ub, cb, live in _group(ids, cnt, g * GROUP, GROUP):
                x = jnp.clip(scores[base + slot].astype(F32), 0.0, 1.0)
                lacc[jnp.where(live, cb, CB)] += x
                racc[jnp.where(live, ub + which * UB, UB2)] += _fold(x)

        store(0, products(0))

        def turn(g, carry, products=products, add=add, store=store):
            blocks = products(g)
            add(g - 1)
            store(g, blocks)
            return carry

        lax.fori_loop(1, turns, turn, 0)
        add(turns - 1)

    _finish_load(lacc, load)
    rows[...] = racc[:UB2].sum(axis=1)
    for which, count in enumerate((count0, count1)):
        _each(_turns(count[0, 0]), lambda g, w=which: _chunk(scores, kept, stored, w * CHUNKS + g).wait())


def _duals(load_in, r0, r1, r2, r3, cap_i, lim_i, lam_in, mu_in):
    load = load_in[...]
    rows = (r0[...] + r2[...]) + (r1[...] + r3[...])
    cap = cap_i[...].astype(F32)
    lim = lim_i[...].astype(F32)
    lam_new = jnp.maximum(0.0, lam_in + (load - cap) / cap)
    mu_new = jnp.maximum(0.0, mu_in + (rows - lim) / lim)
    return load, cap, lim, lam_new, mu_new


def _round_kernel(id0, id1, count0, count1, load_in, r0, r1, r2, r3, cap_i, lim_i, lam_in, mu_in, kept,
                  load, rows, values, lam_out, mu_out, lacc, racc, vacc, lamb, mub, scores, loaded):
    lists = ((id0, count0[0, 0]), (id1, count1[0, 0]))
    for which, (_, cnt) in enumerate(lists):
        _each(_turns(cnt), lambda g, w=which: _chunk(kept, scores, loaded, w * CHUNKS + g).start())
    _clear(lacc, racc, vacc)
    lam = 0.0 if lam_in is None else lam_in[...]
    mu = 0.0 if mu_in is None else mu_in[...]
    _, _, _, lam_new, mu_new = _duals(load_in, r0, r1, r2, r3, cap_i, lim_i, lam, mu)
    lam_out[...] = lam_new
    mu_out[...] = mu_new
    lam_bar = 2.0 * lam_new - lam
    mub[:UB2] = (2.0 * mu_new - mu)[:, None, :]
    for r in range(CB // 2):
        tall = jnp.broadcast_to(lam_bar[r:r + 1, :], (BLOCK, BLOCK)).T
        lamb[2 * r] = tall[:PART]
        lamb[2 * r + 1] = tall[PART:]

    for which, (ids, cnt) in enumerate(lists):

        def some(first, ids=ids, cnt=cnt, which=which):
            for slot, ub, cb, live in _group(ids, cnt, first, STEP):
                s = scores[which * SLOTS + slot].astype(F32)
                x = jnp.clip(s - lamb[cb] - mub[ub + which * UB], 0.0, 1.0)
                lacc[jnp.where(live, cb, CB)] += x
                to_u = jnp.where(live, ub + which * UB, UB2)
                racc[to_u] += _fold(x)
                if vacc is not None:
                    vacc[to_u] += _fold(x * s)

        def chunk(g, which=which, some=some):
            _chunk(kept, scores, loaded, which * CHUNKS + g).wait()
            _each(GROUP // STEP, lambda i: some(g * GROUP + i * STEP))

        _each(_turns(cnt), chunk)

    _finish_load(lacc, load)
    rows[...] = racc[:UB2].sum(axis=1)
    if vacc is not None:
        values[...] = vacc[:UB2].sum(axis=1)


def second_kernel(id0, id1, count0, count1, load_in, r0, r1, r2, r3, cap_i, lim_i, kept,
                  load, rows, lam_out, mu_out, lacc, racc, lamb, mub, scores, loaded):
    _round_kernel(id0, id1, count0, count1, load_in, r0, r1, r2, r3, cap_i, lim_i, None, None, kept,
                  load, rows, None, lam_out, mu_out, lacc, racc, None, lamb, mub, scores, loaded)


def third_kernel(id0, id1, count0, count1, load_in, r0, r1, r2, r3, cap_i, lim_i, lam_in, mu_in, kept,
                 load, out, lam_out, mu_out, lacc, racc, vacc, lamb, mub, scores, loaded):
    _round_kernel(id0, id1, count0, count1, load_in, r0, r1, r2, r3, cap_i, lim_i, lam_in, mu_in, kept,
                  load, out.at[0], out.at[1], lam_out, mu_out, lacc, racc, vacc, lamb, mub, scores, loaded)


def users_kernel(p0, p1, p2, p3, lim_i, mu_in, user_duals, user_value):
    mine = pl.ds(0, UB)
    rows, value = ((p0[k, mine] + p2[k, mine]) + (p1[k, mine] + p3[k, mine]) for k in range(2))
    lim = lim_i[mine].astype(F32)
    user_duals[...] = jnp.maximum(0.0, mu_in[mine] + (rows - lim) / lim)
    user_value[...] = value / lim


def campaigns_kernel(parts, cap_i, lam_in, out):
    load = parts[...].sum(0)
    cap = cap_i[...].astype(F32)
    out[0] = jnp.maximum(0.0, lam_in[...] + (load - cap) / cap)
    out[1] = load / cap


def spread_kernel(load, out):
    out[...] = jnp.broadcast_to(load[...][None], out.shape)


def sum_kernel(parts, out):
    out[...] = parts[...].sum(0)


def pair_kernel(mine, theirs, out):
    half = pl.ds(0, UB)
    rest = pl.ds(UB, UB)
    out[..., half, :] = mine[..., half, :] + theirs[..., rest, :]
    out[..., rest, :] = mine[..., rest, :] + theirs[..., half, :]


SMEM = pl.BlockSpec(memory_space=pltpu.SMEM)
VMEM = pl.BlockSpec(memory_space=pltpu.VMEM)
ANY = pl.BlockSpec(memory_space=pl.ANY)


def _call(kernel, n_smem, args, outs, scratch=(), more=(), any_in=0, any_out=0, limit=4):
    return pl.pallas_call(
        kernel,
        in_specs=[SMEM] * n_smem + [VMEM] * (len(args) - n_smem - any_in) + [ANY] * any_in,
        out_specs=[ANY] * any_out + [VMEM] * (len(outs) - any_out),
        out_shape=[jax.ShapeDtypeStruct(s, d) for s, d in outs],
        scratch_shapes=[pltpu.VMEM(s, F32) for s in scratch] + list(more),
        compiler_params=pltpu.CompilerParams(vmem_limit_bytes=limit * 2 ** 20),
    )(*args)


LACC = (CB + 1, PART, BLOCK)
RACC = (UB2 + 1, 8, BLOCK)
LOAD = ((CB // 2, BLOCK), F32)
ROWS = ((UB2, BLOCK), F32)
MUB = (UB2, 1, BLOCK)
LAMB = (CB, PART, BLOCK)
SCORES = ((2 * SLOTS, PART, BLOCK), jnp.bfloat16)
KEPT = [pltpu.VMEM(*SCORES), pltpu.SemaphoreType.DMA((2 * CHUNKS,))]


def _spread(x, axes, n):
    return lax.all_to_all(jnp.broadcast_to(x[None], (n,) + x.shape), axes, 0, 0, tiled=True)


def _swap(x):
    return lax.ppermute(x, "core", [(0, 1), (1, 0)])


def _load_parts(load):
    (wide,) = _call(spread_kernel, 0, (load,), [((NZ * NX,) + LOAD[0], F32)])
    return lax.all_to_all(wide, ("z", "x"), 0, 0, tiled=True)


def _shift(x, k):
    return lax.ppermute(x, "camp", [((i + k) % NCAMP, i) for i in range(NCAMP)])


def _camp_parts(x):
    (x,) = _call(pair_kernel, 0, (x, _swap(x)), [(x.shape, F32)])
    return x, _shift(x, 1), _shift(x, 2), _shift(x, 3)


def shards(user_emb, camp_emb, block_ids, block_count, capacity, user_limit):
    core = lax.axis_index("core")
    camp_emb, core = lax.optimization_barrier((camp_emb, core))
    users = user_emb.reshape(UB, BLOCK, E)
    users1 = _swap(users)
    ids1 = _swap(block_ids)
    count1 = _swap(block_count)
    lim1 = _swap(user_limit)

    part = _spread(camp_emb, "z", NZ)
    part = _spread(part.reshape(NZ, PART, E), "x", NX).reshape(NX, NZ, PART, E)

    kept, load, rows = _call(
        first_kernel, 2, (block_count, count1, part, block_ids, ids1, users, users1), [SCORES, LOAD, ROWS],
        [LACC, RACC],
        [KEPT[0], pltpu.SMEM((1, SLOTS), jnp.int32), pltpu.SMEM((1, SLOTS), jnp.int32),
         pltpu.VMEM((UB, BLOCK, E), jnp.bfloat16), pltpu.VMEM((UB, BLOCK, E), jnp.bfloat16),
         pltpu.SemaphoreType.DMA((4,)), KEPT[1]], any_in=4, any_out=1, limit=FIRST)
    halves = capacity.reshape(CB // 2, 2, 2, PART)
    cap = jnp.where(core == 0, halves[:, :, 0], halves[:, :, 1]).reshape(CB // 2, BLOCK)
    lim = jnp.concatenate([user_limit, lim1]).reshape(UB2, BLOCK)
    lists = (block_ids, ids1, block_count, count1)

    parts = _camp_parts(rows)
    (load,) = _call(sum_kernel, 0, (_load_parts(load),), [LOAD])
    load, rows, lam, mu = _call(
        second_kernel, 4, (*lists, load, *parts, cap, lim, kept),
        [LOAD, ROWS, LOAD, ROWS], [LACC, RACC, LAMB, MUB], KEPT, any_in=1, limit=WIDE)
    parts = _camp_parts(rows)
    (load,) = _call(sum_kernel, 0, (_load_parts(load),), [LOAD])
    load, sums, lam, mu = _call(
        third_kernel, 4, (*lists, load, *parts, cap, lim, lam, mu, kept),
        [LOAD, ((2, UB2, BLOCK), F32), LOAD, ROWS], [LACC, RACC, RACC, LAMB, MUB], KEPT, any_in=1, limit=WIDE)
    parts = _camp_parts(sums)
    (pair,) = _call(campaigns_kernel, 0, (_load_parts(load), cap, lam), [((2, CB // 2, BLOCK), F32)])
    user_duals, value = _call(users_kernel, 0, (*parts, lim, mu), [((UB, BLOCK), F32)] * 2)
    other = _swap(pair)
    first = core == 0
    both = jnp.stack([jnp.where(first, pair, other), jnp.where(first, other, pair)])
    both = both.reshape(2, 2, CB, PART).transpose(1, 2, 0, 3).reshape(2, CB * BLOCK)
    return both[0], user_duals.reshape(-1), both[1], value.reshape(-1)


def solution(mesh):
    fine = Mesh(mesh.devices.reshape(NZ, NX, NCORE, NCAMP), ("z", "x", "core", "camp"))
    users = ("z", "x", "core")
    return jax.shard_map(
        shards,
        mesh=fine,
        in_specs=(P(users, None), P(("camp",) + users, None), P("camp", users), P("camp", users), P("camp"), P(users)),
        out_specs=(P("camp"), P(users), P("camp"), P(users)),
        check_vma=False,
    )
```

time: 1180 us -> 137 us (0.12)
  blocking collectives: 880 us -> 18.6 us
  waiting for transfers between devices: 151 us -> 29.8 us
  local copies, waits for them, and re-layouts: 76.5 us -> 3.6 us
  matrix products: 54 us -> 0 us
  starting transfers between devices: 0.08 us -> 53.4 us
  Pallas kernels: 0 us -> 29.4 us
  between operations: 14.8 us -> 1.47 us
    psum x5 -> x0, blocking collectives: 880 us -> none  [the longest x3 761 us: shards(): load = lax.psum(loadp, 'users')]
    all_gather x1 -> x0, waiting for transfers between devices: 82.9 us -> none  [shards(): panel = lax.all_gather(camp_emb, 'users', axis=0, tiled=True)]
    gather x24 -> x0, local copies, waits for them, and re-layouts: 76.4 us -> none  [the longest x12 51.4 us: scores_of(): jnp.take(users, lax.dynamic_slice_in_dim(ublk, start, group), axis=0)]
    psum x1 -> x0, waiting for transfers between devices: 67.1 us -> none  [shards(): rows, value = lax.psum((rowp, valp), 'camp')]
    dot_general x64 -> x0, matrix products: 54 us -> none  [the longest x12 41.5 us: scores_of(): jnp.einsum('sue,sce->suc', u_part, c_part, preferred_element_type=jnp.flo...]
    pallas_call x0 -> x13, Pallas kernels: none -> 29.4 us  [_call(): pl.pallas_call(kernel, in_specs=[SMEM] * n_smem + [VMEM] * (len(args) - n...]
    all_to_all x0 -> x4, starting transfers between devices: none -> 27.9 us  [the longest x3 23.9 us: _load_parts(): return lax.all_to_all(wide, ('z', 'x'), 0, 0, tiled=True)]
    ppermute x0 -> x17, starting transfers between devices: none -> 25.5 us  [the longest x9 12.9 us: _shift(): return lax.ppermute(x, 'camp', [((i + k) % NCAMP, i) for i in range(NCAMP)])]
  transfers between devices with their start and end apart: 2 -> 21, of which waited for: 2 -> 11; matrix products, arithmetic and copies ran while one was open for 0% -> 2% of each run, Pallas kernels for 0% -> 1%
where the time goes in v6:
time: 137 us; the launch traced here: 136 us
  starting transfers between devices  53.4 us (39%)
  waiting for transfers between devices  29.8 us (22%)
  Pallas kernels  29.4 us (21%)
  blocking collectives  18.6 us (14%)
  local copies, waits for them, and re-layouts  3.6 us (3%)
  between operations  1.47 us (1%)
    pallas_call x13, Pallas kernels, _call(): pl.pallas_call(kernel, in_specs=[SMEM] * n_smem + [VMEM] * (len(args) - n...  29.4 us
    all_to_all x3, starting transfers between devices, _load_parts(): return lax.all_to_all(wide, ('z', 'x'), 0, 0, tiled=True)  23.9 us
    all_to_all x1, blocking collectives, _spread(): lax.all_to_all(jnp.broadcast_to(x[None], (n,) + x.shape), axes, 0, 0, til...  18.6 us
    ppermute x9, starting transfers between devices, _shift(): return lax.ppermute(x, 'camp', [((i + k) % NCAMP, i) for i in range(NCAMP)])  12.9 us
    ppermute x8, starting transfers between devices, _swap(): return lax.ppermute(x, 'core', [(0, 1), (1, 0)])  12.5 us
    all_to_all x1, waiting for transfers between devices, _spread(): lax.all_to_all(jnp.broadcast_to(x[None], (n,) + x.shape), axes, 0, 0, til...  12.4 us
    all_to_all x3, waiting for transfers between devices, _load_parts(): return lax.all_to_all(wide, ('z', 'x'), 0, 0, tiled=True)  10.3 us
    all_to_all x1, starting transfers between devices, _spread(): lax.all_to_all(jnp.broadcast_to(x[None], (n,) + x.shape), axes, 0, 0, til...  4.01 us
  transfers between devices with their start and end apart: 21, of which 11 were waited for; matrix products, arithmetic and copies ran while one was open for 2% of the time, Pallas kernels for 1%

profile of v6, /device:TPU:1, one launch (start us, length us, event | category | flops | bytes accessed | tf_op | source)
XLA Modules:
  0.0 136.4 jit_solution(1912994366384204655)
XLA Ops:
  0.6 3.3 %collective-permute-start.2 = (bf16[64,128,256]{2,1,0:T(8,128)(2,1)}, bf16[64,128,256]{2,1,0:T(8,128)(2,1)}, u32[]{:S(2)}, u32[]{:S(2)}) collective-permute-start(bf16[64,128,256]{2,1,0:T(8,128)(2,1)} %bitcast.9), channel_id=1, source_target_pairs={{0,4},{4,0},{1,5},{5,1},{2,6},{6,2},{3,7},{7,3},{8,12},{12,8},{9,1... | collective-permute-start | bytes 12582920 | tf_op jit(solution)/shard_map/ppermute | solution.py:247
  4.0 0.8 broadcast_in_dim.4
  4.7 18.6 %all_to_all.25 = bf16[8,64,256]{2,1,0:T(8,128)(2,1)S(1)} all-to-all(bf16[8,64,256]{2,1,0:T(8,128)(2,1)S(1)} %broadcast_in_dim.4), channel_id=1, replica_groups=mesh['z'=8,'x'=4,'core'=2,'camp'=4] {'z'}, dimensions={0} | all-to-all | bytes 524288 | tf_op jit(solution)/shard_map/all_to_all | solution.py:243
  23.4 1.1 broadcast_in_dim.5
  24.5 4.0 %all-to-all-start.1 = ((bf16[4,8,64,256]{3,2,1,0:T(8,128)(2,1)}), bf16[4,8,64,256]{3,2,1,0:T(8,128)(2,1)S(1)}, u32[]{:S(2)}, u32[]{:S(2)}) async-start(bf16[4,8,64,256]{3,2,1,0:T(8,128)(2,1)} %broadcast_in_dim.5), calls=%async_computation.1 | async-start | bytes 2097152 | tf_op jit(solution)/shard_map/all_to_all | solution.py:243
  28.5 0.7 collective-permute-start
  30.5 12.4 %all-to-all-done.1.part = bf16[4,8,64,256]{3,2,1,0:T(8,128)(2,1)S(1)} async-done(((bf16[4,8,64,256]{3,2,1,0:T(8,128)(2,1)}), bf16[4,8,64,256]{3,2,1,0:T(8,128)(2,1)S(1)}, u32[]{:S(2)}, u32[]{:S(2)}) %all-to-all-start.1) | async-done | bytes 1048608 | tf_op jit(solution)/shard_map/all_to_all | solution.py:243
  42.9 14.1 %shard_map.93 = (bf16[512,64,128]{2,1,0:T(8,128)(2,1)}, f32[16,128]{1,0:T(8,128)S(1)}, f32[128,128]{1,0:T(8,128)S(1)}) custom-call(s32[1,1]{1,0:T(1,128)S(6)} %copy.12.count0, s32[1,1]{1,0:T(1,128)} %collective-permute-done.1.count1, bf16[4,8,64,256]{3,2,1,0:T(8,128)(2,1)S(1)} %all-to-all-done.1.part, s32[1,256]{1,0:T(1,128)S(1)} %copy-done, ...), custom_call_target="tpu_custom_call" | custom-call | tf_op jit(solution)/shard_map/pallas_call | solution.py:222
  57.0 0.7 shard_map.94
  57.8 5.2 %all-to-all-start.2 = ((f32[32,16,128]{2,1,0:T(8,128)}), f32[32,16,128]{2,1,0:T(8,128)S(1)}, u32[]{:S(2)}, u32[]{:S(2)}) async-start(f32[32,16,128]{2,1,0:T(8,128)} %shard_map.94), calls=%async_computation.2 | async-start | bytes 524288 | tf_op jit(solution)/shard_map/all_to_all | solution.py:252
  63.0 2.0 %collective-permute-start.7 = (s32[8192]{0:T(1024)S(1)}, s32[8192]{0:T(1024)S(1)}, u32[]{:S(2)}, u32[]{:S(2)}) collective-permute-start(s32[8192]{0:T(1024)S(1)} %copy-done.1), channel_id=1, source_target_pairs={{0,4},{4,0},{1,5},{5,1},{2,6},{6,2},{3,7},{7,3},{8,12},{12,8},{9,1... | collective-permute-start | bytes 98312 | tf_op jit(solution)/shard_map/ppermute | solution.py:247
  65.4 1.1 collective-permute-done.3.theirs
  66.5 3.1 %collective-permute-start.4 = (f32[128,128]{1,0:T(8,128)S(1)}, f32[128,128]{1,0:T(8,128)S(1)}, u32[]{:S(2)}, u32[]{:S(2)}) collective-permute-start(f32[128,128]{1,0:T(8,128)S(1)} %shard_map.96.r0), channel_id=1, source_target_pairs={{1,0},{2,1},{3,2},{0,3},{5,4},{6,5},{7,6},{4,7},{9,8},{10,9},{11,1... | collective-permute-start | bytes 196616 | tf_op jit(solution)/shard_map/ppermute | solution.py:256
  69.5 0.8 collective-permute-start.5
  70.9 2.5 %all-to-all-done.2.parts = f32[32,16,128]{2,1,0:T(8,128)S(1)} async-done(((f32[32,16,128]{2,1,0:T(8,128)}), f32[32,16,128]{2,1,0:T(8,128)S(1)}, u32[]{:S(2)}, u32[]{:S(2)}) %all-to-all-start.2) | async-done | bytes 262176 | tf_op jit(solution)/shard_map/all_to_all | solution.py:252
  73.4 1.0 collective-permute-done.5.r2
  74.5 1.5 %collective-permute-done.6.r3 = f32[128,128]{1,0:T(8,128)S(1)} collective-permute-done((f32[128,128]{1,0:T(8,128)S(1)}, f32[128,128]{1,0:T(8,128)S(1)}, u32[]{:S(2)}, u32[]{:S(2)}) %collective-permute-start.6) | collective-permute-done | bytes 65568 | tf_op jit(solution)/shard_map/ppermute | solution.py:256
  75.9 5.8 %shard_map.97 = (f32[16,128]{1,0:T(8,128)S(1)}, f32[128,128]{1,0:T(8,128)S(1)}, f32[16,128]{1,0:T(8,128)S(1)}, f32[128,128]{1,0:T(8,128)S(1)}) custom-call(s32[1,256]{1,0:T(1,128)S(1)} %copy-done, s32[1,256]{1,0:T(1,128)S(1)} %collective-permute-done.codes1.id1, s32[1,1]{1,0:T(1,128)S(6)} %copy.12.count0, s32[1,1]{1,0:T(1,128)} %collective-permute-done.1.count1, ...), custom_call_target="tpu_custom_call" | custom-call | tf_op jit(solution)/shard_map/pallas_call | solution.py:222
  82.5 10.0 %all-to-all-start.3 = ((f32[32,16,128]{2,1,0:T(8,128)}), f32[32,16,128]{2,1,0:T(8,128)S(1)}, u32[]{:S(2)}, u32[]{:S(2)}) async-start(f32[32,16,128]{2,1,0:T(8,128)} %shard_map.98), calls=%async_computation.3 | async-start | bytes 524288 | tf_op jit(solution)/shard_map/all_to_all | solution.py:252
  92.5 1.4 collective-permute-start.8
  93.9 0.9 collective-permute-done.8.theirs
  94.8 1.6 %collective-permute-start.10 = (f32[128,128]{1,0:T(8,128)S(1)}, f32[128,128]{1,0:T(8,128)S(1)}, u32[]{:S(2)}, u32[]{:S(2)}) collective-permute-start(f32[128,128]{1,0:T(8,128)S(1)} %shard_map.100.r0), channel_id=1, source_target_pairs={{2,0},{3,1},{0,2},{1,3},{6,4},{7,5},{4,6},{5,7},{10,8},{11,9},{8,1... | collective-permute-start | bytes 196616 | tf_op jit(solution)/shard_map/ppermute | solution.py:256
  96.5 2.7 %collective-permute-start.9 = (f32[128,128]{1,0:T(8,128)S(1)}, f32[128,128]{1,0:T(8,128)S(1)}, u32[]{:S(2)}, u32[]{:S(2)}) collective-permute-start(f32[128,128]{1,0:T(8,128)S(1)} %shard_map.100.r0), channel_id=1, source_target_pairs={{1,0},{2,1},{3,2},{0,3},{5,4},{6,5},{7,6},{4,7},{9,8},{10,9},{11,1... | collective-permute-start | bytes 196616 | tf_op jit(solution)/shard_map/ppermute | solution.py:256
  99.1 3.9 %all-to-all-done.3.parts = f32[32,16,128]{2,1,0:T(8,128)S(1)} async-done(((f32[32,16,128]{2,1,0:T(8,128)}), f32[32,16,128]{2,1,0:T(8,128)S(1)}, u32[]{:S(2)}, u32[]{:S(2)}) %all-to-all-start.3) | async-done | bytes 262176 | tf_op jit(solution)/shard_map/all_to_all | solution.py:252
  103.1 6.5 %shard_map.101 = (f32[16,128]{1,0:T(8,128)S(1)}, f32[2,128,128]{2,1,0:T(8,128)S(1)}, f32[16,128]{1,0:T(8,128)S(1)}, f32[128,128]{1,0:T(8,128)S(1)}) custom-call(s32[1,256]{1,0:T(1,128)S(1)} %copy-done, s32[1,256]{1,0:T(1,128)S(1)} %collective-permute-done.codes1.id1, s32[1,1]{1,0:T(1,128)S(6)} %copy.12.count0, s32[1,1]{1,0:T(1,128)} %collective-permute-done.1.count1, ...), custom_call_target="tpu_custom_call" | custom-call | tf_op jit(solution)/shard_map/pallas_call | solution.py:222
  110.4 8.6 %all-to-all-start.4 = ((f32[32,16,128]{2,1,0:T(8,128)}), f32[32,16,128]{2,1,0:T(8,128)S(1)}, u32[]{:S(2)}, u32[]{:S(2)}) async-start(f32[32,16,128]{2,1,0:T(8,128)} %shard_map.102), calls=%async_computation.4 | async-start | bytes 524288 | tf_op jit(solution)/shard_map/all_to_all | solution.py:252
  119.0 1.4 %collective-permute-start.13 = (f32[2,128,128]{2,1,0:T(8,128)S(1)}, f32[2,128,128]{2,1,0:T(8,128)S(1)}, u32[]{:S(2)}, u32[]{:S(2)}) collective-permute-start(f32[2,128,128]{2,1,0:T(8,128)S(1)} %get-tuple-element.30.mine), channel_id=1, source_target_pairs={{0,4},{4,0},{1,5},{5,1},{2,6},{6,2},{3,7},{7,3},{8,12},{12,8},{9,1... | collective-permute-start | bytes 393224 | tf_op jit(solution)/shard_map/ppermute | solution.py:247
  120.4 1.0 collective-permute-done.13.theirs
  121.4 3.5 %collective-permute-start.14 = (f32[2,128,128]{2,1,0:T(8,128)S(1)}, f32[2,128,128]{2,1,0:T(8,128)S(1)}, u32[]{:S(2)}, u32[]{:S(2)}) collective-permute-start(f32[2,128,128]{2,1,0:T(8,128)S(1)} %shard_map.104.p0), channel_id=1, source_target_pairs={{1,0},{2,1},{3,2},{0,3},{5,4},{6,5},{7,6},{4,7},{9,8},{10,9},{11,1... | collective-permute-start | bytes 393224 | tf_op jit(solution)/shard_map/ppermute | solution.py:256
  125.6 3.9 %all-to-all-done.4.parts = f32[32,16,128]{2,1,0:T(8,128)S(1)} async-done(((f32[32,16,128]{2,1,0:T(8,128)}), f32[32,16,128]{2,1,0:T(8,128)S(1)}, u32[]{:S(2)}, u32[]{:S(2)}) %all-to-all-start.4) | async-done | bytes 262176 | tf_op jit(solution)/shard_map/all_to_all | solution.py:252
  129.5 3.5 %collective-permute-start.12 = (f32[2,16,128]{2,1,0:T(8,128)S(1)}, f32[2,16,128]{2,1,0:T(8,128)S(1)}, u32[]{:S(2)}, u32[]{:S(2)}) collective-permute-start(f32[2,16,128]{2,1,0:T(8,128)S(1)} %shard_map.103), channel_id=1, source_target_pairs={{0,4},{4,0},{1,5},{5,1},{2,6},{6,2},{3,7},{7,3},{8,12},{12,8},{9,1... | collective-permute-start | bytes 49160 | tf_op jit(solution)/shard_map/ppermute | solution.py:247
  133.0 1.1 collective-permute-done.16.p3
  (43 shorter events, 6.0 us)
Async XLA Ops:
  0.6 27.9 %copy-start = (s32[1,256]{1,0:T(1,128)S(1)}, s32[1,256]{1,0:T(1,128)}, u32[]{:S(2)}) copy-start(s32[1,256]{1,0:T(1,128)} %id0.3) | copy-start | bytes 3076
  0.6 42.3 %collective-permute-start.2 = (bf16[64,128,256]{2,1,0:T(8,128)(2,1)}, bf16[64,128,256]{2,1,0:T(8,128)(2,1)}, u32[]{:S(2)}, u32[]{:S(2)}) collective-permute-start(bf16[64,128,256]{2,1,0:T(8,128)(2,1)} %bitcast.9), channel_id=1, source_target_pairs={{0,4},{4,0},{1,5},{5,1},{2,6},{6,2},{3,7},{7,3},{8,12},{12,8},{9,1... | collective-permute-start | bytes 12582920 | tf_op jit(solution)/shard_map/ppermute | solution.py:247
  24.5 18.4 %all-to-all-start.1 = ((bf16[4,8,64,256]{3,2,1,0:T(8,128)(2,1)}), bf16[4,8,64,256]{3,2,1,0:T(8,128)(2,1)S(1)}, u32[]{:S(2)}, u32[]{:S(2)}) async-start(bf16[4,8,64,256]{3,2,1,0:T(8,128)(2,1)} %broadcast_in_dim.5), calls=%async_computation.1 | async-start | bytes 2097152 | tf_op jit(solution)/shard_map/all_to_all | solution.py:243
  28.5 2.0 %collective-permute-start = (s32[1,256]{1,0:T(1,128)S(1)}, s32[1,256]{1,0:T(1,128)S(1)}, u32[]{:S(2)}, u32[]{:S(2)}) collective-permute-start(s32[1,256]{1,0:T(1,128)S(1)} %copy-done), channel_id=1, source_target_pairs={{0,4},{4,0},{1,5},{5,1},{2,6},{6,2},{3,7},{7,3},{8,12},{12,8},{9,1... | collective-permute-start | bytes 3080 | tf_op jit(solution)/shard_map/ppermute | solution.py:247
  29.2 1.2 collective-permute-start.1
  30.0 33.0 %copy-start.1 = (s32[8192]{0:T(1024)S(1)}, s32[8192]{0:T(1024)}, u32[]{:S(2)}) copy-start(s32[8192]{0:T(1024)} %param.11) | copy-start | bytes 98308
  30.0 35.0 %copy-start.2 = (s32[4096]{0:T(1024)S(1)}, s32[4096]{0:T(1024)}, u32[]{:S(2)}) copy-start(s32[4096]{0:T(1024)} %param.10) | copy-start | bytes 49156
  57.8 15.6 %all-to-all-start.2 = ((f32[32,16,128]{2,1,0:T(8,128)}), f32[32,16,128]{2,1,0:T(8,128)S(1)}, u32[]{:S(2)}, u32[]{:S(2)}) async-start(f32[32,16,128]{2,1,0:T(8,128)} %shard_map.94), calls=%async_computation.2 | async-start | bytes 524288 | tf_op jit(solution)/shard_map/all_to_all | solution.py:252
  63.0 7.9 %collective-permute-start.7 = (s32[8192]{0:T(1024)S(1)}, s32[8192]{0:T(1024)S(1)}, u32[]{:S(2)}, u32[]{:S(2)}) collective-permute-start(s32[8192]{0:T(1024)S(1)} %copy-done.1), channel_id=1, source_target_pairs={{0,4},{4,0},{1,5},{5,1},{2,6},{6,2},{3,7},{7,3},{8,12},{12,8},{9,1... | collective-permute-start | bytes 98312 | tf_op jit(solution)/shard_map/ppermute | solution.py:247
  65.1 1.3 collective-permute-start.3
  66.5 7.0 %collective-permute-start.4 = (f32[128,128]{1,0:T(8,128)S(1)}, f32[128,128]{1,0:T(8,128)S(1)}, u32[]{:S(2)}, u32[]{:S(2)}) collective-permute-start(f32[128,128]{1,0:T(8,128)S(1)} %shard_map.96.r0), channel_id=1, source_target_pairs={{1,0},{2,1},{3,2},{0,3},{5,4},{6,5},{7,6},{4,7},{9,8},{10,9},{11,1... | collective-permute-start | bytes 196616 | tf_op jit(solution)/shard_map/ppermute | solution.py:256
  69.5 4.9 %collective-permute-start.5 = (f32[128,128]{1,0:T(8,128)S(1)}, f32[128,128]{1,0:T(8,128)S(1)}, u32[]{:S(2)}, u32[]{:S(2)}) collective-permute-start(f32[128,128]{1,0:T(8,128)S(1)} %shard_map.96.r0), channel_id=1, source_target_pairs={{2,0},{3,1},{0,2},{1,3},{6,4},{7,5},{4,6},{5,7},{10,8},{11,9},{8,1... | collective-permute-start | bytes 196616 | tf_op jit(solution)/shard_map/ppermute | solution.py:256
  70.4 5.6 %collective-permute-start.6 = (f32[128,128]{1,0:T(8,128)S(1)}, f32[128,128]{1,0:T(8,128)S(1)}, u32[]{:S(2)}, u32[]{:S(2)}) collective-permute-start(f32[128,128]{1,0:T(8,128)S(1)} %shard_map.96.r0), channel_id=1, source_target_pairs={{3,0},{0,1},{1,2},{2,3},{7,4},{4,5},{5,6},{6,7},{11,8},{8,9},{9,10... | collective-permute-start | bytes 196616 | tf_op jit(solution)/shard_map/ppermute | solution.py:256
  82.5 20.6 %all-to-all-start.3 = ((f32[32,16,128]{2,1,0:T(8,128)}), f32[32,16,128]{2,1,0:T(8,128)S(1)}, u32[]{:S(2)}, u32[]{:S(2)}) async-start(f32[32,16,128]{2,1,0:T(8,128)} %shard_map.98), calls=%async_computation.3 | async-start | bytes 524288 | tf_op jit(solution)/shard_map/all_to_all | solution.py:252
  92.5 2.3 %collective-permute-start.8 = (f32[128,128]{1,0:T(8,128)S(1)}, f32[128,128]{1,0:T(8,128)S(1)}, u32[]{:S(2)}, u32[]{:S(2)}) collective-permute-start(f32[128,128]{1,0:T(8,128)S(1)} %get-tuple-element.25.mine), channel_id=1, source_target_pairs={{0,4},{4,0},{1,5},{5,1},{2,6},{6,2},{3,7},{7,3},{8,12},{12,8},{9,1... | collective-permute-start | bytes 196616 | tf_op jit(solution)/shard_map/ppermute | solution.py:247
  94.8 8.3 %collective-permute-start.10 = (f32[128,128]{1,0:T(8,128)S(1)}, f32[128,128]{1,0:T(8,128)S(1)}, u32[]{:S(2)}, u32[]{:S(2)}) collective-permute-start(f32[128,128]{1,0:T(8,128)S(1)} %shard_map.100.r0), channel_id=1, source_target_pairs={{2,0},{3,1},{0,2},{1,3},{6,4},{7,5},{4,6},{5,7},{10,8},{11,9},{8,1... | collective-permute-start | bytes 196616 | tf_op jit(solution)/shard_map/ppermute | solution.py:256
  96.5 6.7 %collective-permute-start.11 = (f32[128,128]{1,0:T(8,128)S(1)}, f32[128,128]{1,0:T(8,128)S(1)}, u32[]{:S(2)}, u32[]{:S(2)}) collective-permute-start(f32[128,128]{1,0:T(8,128)S(1)} %shard_map.100.r0), channel_id=1, source_target_pairs={{3,0},{0,1},{1,2},{2,3},{7,4},{4,5},{5,6},{6,7},{11,8},{8,9},{9,10... | collective-permute-start | bytes 196616 | tf_op jit(solution)/shard_map/ppermute | solution.py:256
  96.5 6.7 %collective-permute-start.9 = (f32[128,128]{1,0:T(8,128)S(1)}, f32[128,128]{1,0:T(8,128)S(1)}, u32[]{:S(2)}, u32[]{:S(2)}) collective-permute-start(f32[128,128]{1,0:T(8,128)S(1)} %shard_map.100.r0), channel_id=1, source_target_pairs={{1,0},{2,1},{3,2},{0,3},{5,4},{6,5},{7,6},{4,7},{9,8},{10,9},{11,1... | collective-permute-start | bytes 196616 | tf_op jit(solution)/shard_map/ppermute | solution.py:256
  110.4 19.1 %all-to-all-start.4 = ((f32[32,16,128]{2,1,0:T(8,128)}), f32[32,16,128]{2,1,0:T(8,128)S(1)}, u32[]{:S(2)}, u32[]{:S(2)}) async-start(f32[32,16,128]{2,1,0:T(8,128)} %shard_map.102), calls=%async_computation.4 | async-start | bytes 524288 | tf_op jit(solution)/shard_map/all_to_all | solution.py:252
  119.0 2.4 %collective-permute-start.13 = (f32[2,128,128]{2,1,0:T(8,128)S(1)}, f32[2,128,128]{2,1,0:T(8,128)S(1)}, u32[]{:S(2)}, u32[]{:S(2)}) collective-permute-start(f32[2,128,128]{2,1,0:T(8,128)S(1)} %get-tuple-element.30.mine), channel_id=1, source_target_pairs={{0,4},{4,0},{1,5},{5,1},{2,6},{6,2},{3,7},{7,3},{8,12},{12,8},{9,1... | collective-permute-start | bytes 393224 | tf_op jit(solution)/shard_map/ppermute | solution.py:247
  121.4 11.6 %collective-permute-start.14 = (f32[2,128,128]{2,1,0:T(8,128)S(1)}, f32[2,128,128]{2,1,0:T(8,128)S(1)}, u32[]{:S(2)}, u32[]{:S(2)}) collective-permute-start(f32[2,128,128]{2,1,0:T(8,128)S(1)} %shard_map.104.p0), channel_id=1, source_target_pairs={{1,0},{2,1},{3,2},{0,3},{5,4},{6,5},{7,6},{4,7},{9,8},{10,9},{11,1... | collective-permute-start | bytes 393224 | tf_op jit(solution)/shard_map/ppermute | solution.py:256
  124.9 8.1 %collective-permute-start.15 = (f32[2,128,128]{2,1,0:T(8,128)S(1)}, f32[2,128,128]{2,1,0:T(8,128)S(1)}, u32[]{:S(2)}, u32[]{:S(2)}) collective-permute-start(f32[2,128,128]{2,1,0:T(8,128)S(1)} %shard_map.104.p0), channel_id=1, source_target_pairs={{2,0},{3,1},{0,2},{1,3},{6,4},{7,5},{4,6},{5,7},{10,8},{11,9},{8,1... | collective-permute-start | bytes 393224 | tf_op jit(solution)/shard_map/ppermute | solution.py:256
  124.9 9.1 %collective-permute-start.16 = (f32[2,128,128]{2,1,0:T(8,128)S(1)}, f32[2,128,128]{2,1,0:T(8,128)S(1)}, u32[]{:S(2)}, u32[]{:S(2)}) collective-permute-start(f32[2,128,128]{2,1,0:T(8,128)S(1)} %shard_map.104.p0), channel_id=1, source_target_pairs={{3,0},{0,1},{1,2},{2,3},{7,4},{4,5},{5,6},{6,7},{11,8},{8,9},{9,10... | collective-permute-start | bytes 393224 | tf_op jit(solution)/shard_map/ppermute | solution.py:256
  129.5 5.2 %collective-permute-start.12 = (f32[2,16,128]{2,1,0:T(8,128)S(1)}, f32[2,16,128]{2,1,0:T(8,128)S(1)}, u32[]{:S(2)}, u32[]{:S(2)}) collective-permute-start(f32[2,16,128]{2,1,0:T(8,128)S(1)} %shard_map.103), channel_id=1, source_target_pairs={{0,4},{4,0},{1,5},{5,1},{2,6},{6,2},{3,7},{7,3},{8,12},{12,8},{9,1... | collective-permute-start | bytes 49160 | tf_op jit(solution)/shard_map/ppermute | solution.py:247

commit v7 on v6

v7 whole, which is shorter than its diff:
```python
import jax
import jax.numpy as jnp
from jax import lax
from jax.experimental import pallas as pl
from jax.experimental.pallas import tpu as pltpu
from jax.sharding import Mesh, PartitionSpec as P

BLOCK = 128
PART = 64
E = 256
SLOTS = 256
UB = 64
UB2 = 128
CB = 32
NZ, NX, NCORE, NCAMP = 8, 4, 2, 4
GROUP = 32
STEP = 32
CHUNKS = SLOTS // GROUP
WIDE = 50
FIRST = 43
F32 = jnp.float32


def _each(turns, do):
    def turn(g, carry):
        do(g)
        return carry

    lax.fori_loop(0, turns, turn, 0)


def _clear(*accs):
    for acc in accs:
        if acc is not None:
            acc[...] = jnp.zeros_like(acc)


def _load(kept, scores, sems, which, g):
    to = pl.ds(which * SLOTS + g * GROUP, GROUP)
    return pltpu.make_async_copy(kept.at[pl.ds(g * GROUP, GROUP)], scores.at[to], sems.at[which * CHUNKS + g])


def _save(scores, kept, sems, which, g):
    at = pl.ds(g * GROUP, GROUP)
    return pltpu.make_async_copy(scores.at[at, pl.ds(which * PART, PART)], kept.at[at], sems.at[which, g])


def _fold(x):
    return x.reshape(x.shape[0] // 8, 8, BLOCK).sum(0)


def _finish_load(lacc, out):
    def turn(r, carry):
        both = lacc[pl.ds(2 * r, 2)].reshape(BLOCK, BLOCK)
        out[pl.ds(r, 1), :] = jnp.sum(both.T, axis=0, keepdims=True)
        return carry

    lax.fori_loop(0, CB // 2, turn, 0, unroll=4)


def _turns(cnt):
    return (cnt + GROUP - 1) // GROUP


def _group(ids, cnt, first, size):
    out = []
    for k in range(size):
        slot = first + k
        code = ids[0, slot]
        out.append((slot, code >> 5, code & (CB - 1), slot < cnt))
    return out


def fetch_kernel(users, out, sem):
    copy = pltpu.make_async_copy(users, out, sem)
    copy.start()
    copy.wait()


def first_kernel(count, users, part, peer, codes, kept0, kept1, keep, give, rows, lacc, racc, panel, scores, ids,
                 sems, fetched, stored):
    fetch = pltpu.make_async_copy(codes, ids, fetched)
    fetch.start()
    copies = [
        pltpu.make_async_copy(src.at[x], panel.at[:, x, half], sems.at[x, half])
        for x in range(NX)
        for half, src in enumerate((part, peer))
    ]
    for copy in copies:
        copy.start()
    _clear(lacc, racc)
    for copy in copies:
        copy.wait()
    fetch.wait()
    camps = panel.reshape(CB, BLOCK, E)
    cnt = count[0, 0]
    turns = _turns(cnt)
    kepts = (kept0, kept1)

    def products(g):
        return [
            lax.dot_general(
                camps[cb], users[ub], (((1,), (1,)), ((), ())), preferred_element_type=F32
            ).astype(jnp.bfloat16)
            for _, ub, cb, _ in _group(ids, cnt, g * GROUP, GROUP)
        ]

    def store(g, blocks):
        for k, block in enumerate(blocks):
            scores[g * GROUP + k] = block
        for which, kept in enumerate(kepts):
            _save(scores, kept, stored, which, g).start()

    def add(g):
        for slot, ub, cb, live in _group(ids, cnt, g * GROUP, GROUP):
            x = jnp.clip(scores[slot].astype(F32), 0.0, 1.0)
            lacc[jnp.where(live, cb, CB)] += x
            racc[jnp.where(live, ub, UB)] += _fold(x)

    store(0, products(0))

    def turn(g, carry):
        blocks = products(g)
        add(g - 1)
        store(g, blocks)
        return carry

    lax.fori_loop(1, turns, turn, 0)
    add(turns - 1)

    def finish(r, carry):
        pair = lacc[pl.ds(2 * r, 2)]
        for which, out in enumerate((keep, give)):
            both = pair[:, which * PART:(which + 1) * PART].reshape(BLOCK, BLOCK)
            out[pl.ds(r, 1), :] = jnp.sum(both.T, axis=0, keepdims=True)
        return carry

    lax.fori_loop(0, CB // 2, finish, 0, unroll=2)
    rows[...] = racc[:UB].sum(axis=1)
    for which, kept in enumerate(kepts):
        _each(turns, lambda g, w=which, k=kept: _save(scores, k, stored, w, g).wait())


def _duals(load_in, r0, r1, r2, r3, cap_i, lim_i, lam_in, mu_in):
    load = load_in[...]
    rows = (r0[...] + r2[...]) + (r1[...] + r3[...])
    cap = cap_i[...].astype(F32)
    lim = lim_i[...].astype(F32)
    lam_new = jnp.maximum(0.0, lam_in + (load - cap) / cap)
    mu_new = jnp.maximum(0.0, mu_in + (rows - lim) / lim)
    return load, cap, lim, lam_new, mu_new


def _round_kernel(id0, id1, count0, count1, load_in, r0, r1, r2, r3, cap_i, lim_i, lam_in, mu_in, kepts,
                  load, rows, values, lam_out, mu_out, lacc, racc, vacc, lamb, mub, scores, loaded):
    lists = ((id0, count0[0, 0]), (id1, count1[0, 0]))
    for which, (_, cnt) in enumerate(lists):
        _each(_turns(cnt), lambda g, w=which: _load(kepts[w], scores, loaded, w, g).start())
    _clear(lacc, racc, vacc)
    lam = 0.0 if lam_in is None else lam_in[...]
    mu = 0.0 if mu_in is None else mu_in[...]
    _, _, _, lam_new, mu_new = _duals(load_in, r0, r1, r2, r3, cap_i, lim_i, lam, mu)
    lam_out[...] = lam_new
    mu_out[...] = mu_new
    lam_bar = 2.0 * lam_new - lam
    mub[:UB2] = (2.0 * mu_new - mu)[:, None, :]
    for r in range(CB // 2):
        tall = jnp.broadcast_to(lam_bar[r:r + 1, :], (BLOCK, BLOCK)).T
        lamb[2 * r] = tall[:PART]
        lamb[2 * r + 1] = tall[PART:]

    for which, (ids, cnt) in enumerate(lists):

        def some(first, ids=ids, cnt=cnt, which=which):
            for slot, ub, cb, live in _group(ids, cnt, first, STEP):
                s = scores[which * SLOTS + slot].astype(F32)
                x = jnp.clip(s - lamb[cb] - mub[ub + which * UB], 0.0, 1.0)
                lacc[jnp.where(live, cb, CB)] += x
                to_u = jnp.where(live, ub + which * UB, UB2)
                racc[to_u] += _fold(x)
                if vacc is not None:
                    vacc[to_u] += _fold(x * s)

        def chunk(g, which=which, some=some):
            _load(kepts[which], scores, loaded, which, g).wait()
            _each(GROUP // STEP, lambda i: some(g * GROUP + i * STEP))

        _each(_turns(cnt), chunk)

    _finish_load(lacc, load)
    rows[...] = racc[:UB2].sum(axis=1)
    if vacc is not None:
        values[...] = vacc[:UB2].sum(axis=1)


def second_kernel(id0, id1, count0, count1, load_in, r0, r1, r2, r3, cap_i, lim_i, kept0, kept1,
                  load, rows, lam_out, mu_out, lacc, racc, lamb, mub, scores, loaded):
    _round_kernel(id0, id1, count0, count1, load_in, r0, r1, r2, r3, cap_i, lim_i, None, None, (kept0, kept1),
                  load, rows, None, lam_out, mu_out, lacc, racc, None, lamb, mub, scores, loaded)


def third_kernel(id0, id1, count0, count1, load_in, r0, r1, r2, r3, cap_i, lim_i, lam_in, mu_in, kept0, kept1,
                 load, out, lam_out, mu_out, lacc, racc, vacc, lamb, mub, scores, loaded):
    _round_kernel(id0, id1, count0, count1, load_in, r0, r1, r2, r3, cap_i, lim_i, lam_in, mu_in, (kept0, kept1),
                  load, out.at[0], out.at[1], lam_out, mu_out, lacc, racc, vacc, lamb, mub, scores, loaded)


def last_kernel(core, p0, p1, p2, p3, lim_i, mu_in, mine, theirs, duals, user_duals, ratio, user_value):
    half = pl.ds(0, UB)
    rows, value = ((p0[k, half] + p2[k, half]) + (p1[k, half] + p3[k, half]) for k in range(2))
    lim = lim_i[half].astype(F32)
    user_duals[...] = jnp.maximum(0.0, mu_in[half] + (rows - lim) / lim)
    user_value[...] = value / lim
    first = core[0] == 0
    for k, out in enumerate((duals, ratio)):
        a, b = jnp.where(first, mine[k], theirs[k]), jnp.where(first, theirs[k], mine[k])
        even = jnp.concatenate([a[:, :PART], b[:, :PART]], axis=1)
        odd = jnp.concatenate([a[:, PART:], b[:, PART:]], axis=1)
        for r in range(CB // 2):
            out[2 * r:2 * r + 1, :] = even[r:r + 1]
            out[2 * r + 1:2 * r + 2, :] = odd[r:r + 1]


def campaigns_kernel(parts, cap_i, lam_in, out):
    load = parts[...].sum(0)
    cap = cap_i[...].astype(F32)
    out[0] = jnp.maximum(0.0, lam_in[...] + (load - cap) / cap)
    out[1] = load / cap


def spread_kernel(load, out):
    out[...] = jnp.broadcast_to(load[...][None], out.shape)


def spread_sum_kernel(keep, got, out):
    out[...] = jnp.broadcast_to((keep[...] + got[...])[None], out.shape)


def join_kernel(mine, theirs, out):
    out[:UB] = mine[...]
    out[UB:] = theirs[...]


def sum_kernel(parts, out):
    out[...] = parts[...].sum(0)


def pair_kernel(mine, theirs, out):
    half = pl.ds(0, UB)
    rest = pl.ds(UB, UB)
    out[..., half, :] = mine[..., half, :] + theirs[..., rest, :]
    out[..., rest, :] = mine[..., rest, :] + theirs[..., half, :]


SMEM = pl.BlockSpec(memory_space=pltpu.SMEM)
VMEM = pl.BlockSpec(memory_space=pltpu.VMEM)
ANY = pl.BlockSpec(memory_space=pl.ANY)


def _call(kernel, n_smem, args, outs, scratch=(), more=(), any_in=0, any_out=0, limit=4):
    return pl.pallas_call(
        kernel,
        in_specs=[SMEM] * n_smem + [VMEM] * (len(args) - n_smem - any_in) + [ANY] * any_in,
        out_specs=[ANY] * any_out + [VMEM] * (len(outs) - any_out),
        out_shape=[jax.ShapeDtypeStruct(s, d) for s, d in outs],
        scratch_shapes=[pltpu.VMEM(s, F32) for s in scratch] + list(more),
        compiler_params=pltpu.CompilerParams(vmem_limit_bytes=limit * 2 ** 20),
    )(*args)


LACC = (CB + 1, PART, BLOCK)
LACC1 = (CB + 1, BLOCK, BLOCK)
RACC1 = (UB + 1, 8, BLOCK)
RACC = (UB2 + 1, 8, BLOCK)
LOAD = ((CB // 2, BLOCK), F32)
ROWS = ((UB2, BLOCK), F32)
MUB = (UB2, 1, BLOCK)
LAMB = (CB, PART, BLOCK)
SCORES = ((SLOTS, PART, BLOCK), jnp.bfloat16)
ROOMY = ((2 * SLOTS, PART, BLOCK), jnp.bfloat16)
KEPT = [pltpu.VMEM((2 * SLOTS, PART, BLOCK), jnp.bfloat16), pltpu.SemaphoreType.DMA((2 * CHUNKS,))]


def _spread(x, axes, n):
    return lax.all_to_all(jnp.broadcast_to(x[None], (n,) + x.shape), axes, 0, 0, tiled=True)


def _swap(x):
    return lax.ppermute(x, "core", [(0, 1), (1, 0)])


def _load_parts(load):
    (wide,) = _call(spread_kernel, 0, (load,), [((NZ * NX,) + LOAD[0], F32)])
    return lax.all_to_all(wide, ("z", "x"), 0, 0, tiled=True)


def _shift(x, k):
    return lax.ppermute(x, "camp", [((i + k) % NCAMP, i) for i in range(NCAMP)])


def _camp_parts(x, kernel, shape):
    (x,) = _call(kernel, 0, (x, _swap(x)), [(shape, F32)])
    return x, _shift(x, 1), _shift(x, 2), _shift(x, 3)


def shards(user_emb, camp_emb, block_ids, block_count, capacity, user_limit):
    where = jnp.reshape(lax.axis_index("core"), (1,)).astype(jnp.int32)
    camp_emb, where = lax.optimization_barrier((camp_emb, where))
    users = user_emb.reshape(UB, BLOCK, E)

    part = _spread(camp_emb, "z", NZ)
    part = _spread(part.reshape(NZ, PART, E), "x", NX).reshape(NX, NZ, PART, E)
    part, users = lax.optimization_barrier((part, users))
    (users,) = _call(
        fetch_kernel, 0, (users,), [(users.shape, users.dtype)], [], [pltpu.SemaphoreType.DMA], any_in=1)
    peer = _swap(part)

    kept0, give1, keep, give, rows = _call(
        first_kernel, 1, (block_count, users, part, peer, block_ids), [ROOMY, SCORES, LOAD, LOAD, ((UB, BLOCK), F32)],
        [LACC1, RACC1],
        [pltpu.VMEM((NZ, NX, 2, PART, E), jnp.bfloat16), pltpu.VMEM((SLOTS, BLOCK, BLOCK), jnp.bfloat16),
         pltpu.SMEM((1, SLOTS), jnp.int32), pltpu.SemaphoreType.DMA((NX, 2)), pltpu.SemaphoreType.DMA,
         pltpu.SemaphoreType.DMA((2, CHUNKS))], any_in=1, any_out=2, limit=FIRST)
    (wide,) = _call(spread_sum_kernel, 0, (keep, _swap(give)), [((NZ * NX,) + LOAD[0], F32)])
    wide, rows, give1, block_ids, block_count, user_limit, capacity = lax.optimization_barrier(
        (wide, rows, give1, block_ids, block_count, user_limit, capacity))
    wide = lax.all_to_all(wide, ("z", "x"), 0, 0, tiled=True)
    parts = _camp_parts(rows, join_kernel, ROWS[0])
    kept1 = _swap(give1)
    ids1, count1, lim1 = _swap(block_ids), _swap(block_count), _swap(user_limit)
    halves = capacity.reshape(CB // 2, 2, 2, PART)
    cap = jnp.where(where[0] == 0, halves[:, :, 0], halves[:, :, 1]).reshape(CB // 2, BLOCK)
    lim = jnp.concatenate([user_limit, lim1]).reshape(UB2, BLOCK)
    lists = (block_ids, ids1, block_count, count1)
    (load,) = _call(sum_kernel, 0, (wide,), [LOAD])

    load, rows, lam, mu = _call(
        second_kernel, 4, (*lists, load, *parts, cap, lim, kept0, kept1),
        [LOAD, ROWS, LOAD, ROWS], [LACC, RACC, LAMB, MUB], KEPT, any_in=2, limit=WIDE)
    parts = _camp_parts(rows, pair_kernel, ROWS[0])
    (load,) = _call(sum_kernel, 0, (_load_parts(load),), [LOAD])
    load, sums, lam, mu = _call(
        third_kernel, 4, (*lists, load, *parts, cap, lim, lam, mu, kept0, kept1),
        [LOAD, ((2, UB2, BLOCK), F32), LOAD, ROWS], [LACC, RACC, RACC, LAMB, MUB], KEPT, any_in=2, limit=WIDE)
    parts = _camp_parts(sums, pair_kernel, (2,) + ROWS[0])
    (pair,) = _call(campaigns_kernel, 0, (_load_parts(load), cap, lam), [((2, CB // 2, BLOCK), F32)])
    duals, user_duals, ratio, value = _call(
        last_kernel, 1, (where, *parts, lim, mu, pair, _swap(pair)),
        [((CB, BLOCK), F32), ((UB, BLOCK), F32)] * 2)
    return duals.reshape(-1), user_duals.reshape(-1), ratio.reshape(-1), value.reshape(-1)


def solution(mesh):
    fine = Mesh(mesh.devices.reshape(NZ, NX, NCORE, NCAMP), ("z", "x", "core", "camp"))
    users = ("z", "x", "core")
    return jax.shard_map(
        shards,
        mesh=fine,
        in_specs=(P(users, None), P(("camp",) + users, None), P("camp", users), P("camp", users), P("camp"), P(users)),
        out_specs=(P("camp"), P(users), P("camp"), P(users)),
        check_vma=False,
    )
```

time: 137 us -> 128 us (0.934)
  blocking collectives: 18.6 us -> 35.2 us
  starting transfers between devices: 53.4 us -> 40.8 us
  waiting for transfers between devices: 29.8 us -> 23.8 us
  Pallas kernels: 29.4 us -> 25.5 us
  local copies, waits for them, and re-layouts: 3.6 us -> 1.22 us
    all_to_all x1 -> x2, blocking collectives: 18.6 us -> 35.2 us  [_spread(): lax.all_to_all(jnp.broadcast_to(x[None], (n,) + x.shape), axes, 0, 0, til...]
    all_to_all x1, waiting for transfers between devices: 12.4 us -> 5.05 us  [shards(): wide = lax.all_to_all(wide, ('z', 'x'), 0, 0, tiled=True)]
    all_to_all x3 -> x2, starting transfers between devices: 23.9 us -> 17 us  [_load_parts(): return lax.all_to_all(wide, ('z', 'x'), 0, 0, tiled=True)]
    pallas_call x13 -> x14, Pallas kernels: 29.4 us -> 25.5 us  [_call(): pl.pallas_call(kernel, in_specs=[SMEM] * n_smem + [VMEM] * (len(args) - n...]
    ppermute x9, starting transfers between devices: 12.9 us -> 9.16 us  [_shift(): return lax.ppermute(x, 'camp', [((i + k) % NCAMP, i) for i in range(NCAMP)])]
    ppermute x8 -> x10, waiting for transfers between devices: 3.45 us -> 6.82 us  [_swap(): return lax.ppermute(x, 'core', [(0, 1), (1, 0)])]
    ppermute x9, waiting for transfers between devices: 3.58 us -> 0.43 us  [_shift(): return lax.ppermute(x, 'camp', [((i + k) % NCAMP, i) for i in range(NCAMP)])]
    ppermute x8 -> x10, starting transfers between devices: 12.5 us -> 10.8 us  [_swap(): return lax.ppermute(x, 'core', [(0, 1), (1, 0)])]
  transfers between devices with their start and end apart: 21 -> 22, of which waited for: 11 -> 10; matrix products, arithmetic and copies ran while one was open for 2% -> 0% of each run, Pallas kernels for 1% -> 0%
where the time goes in v7:
time: 128 us
  starting transfers between devices  40.8 us (32%)
  blocking collectives  35.2 us (28%)
  Pallas kernels  25.5 us (20%)
  waiting for transfers between devices  23.8 us (19%)
  between operations  1.51 us (1%)
    all_to_all x2, blocking collectives, _spread(): lax.all_to_all(jnp.broadcast_to(x[None], (n,) + x.shape), axes, 0, 0, til...  35.2 us
    pallas_call x14, Pallas kernels, _call(): pl.pallas_call(kernel, in_specs=[SMEM] * n_smem + [VMEM] * (len(args) - n...  25.5 us
    all_to_all x2, starting transfers between devices, _load_parts(): return lax.all_to_all(wide, ('z', 'x'), 0, 0, tiled=True)  17 us
    all_to_all x2, waiting for transfers between devices, _load_parts(): return lax.all_to_all(wide, ('z', 'x'), 0, 0, tiled=True)  11.5 us
    ppermute x10, starting transfers between devices, _swap(): return lax.ppermute(x, 'core', [(0, 1), (1, 0)])  10.8 us
    ppermute x9, starting transfers between devices, _shift(): return lax.ppermute(x, 'camp', [((i + k) % NCAMP, i) for i in range(NCAMP)])  9.16 us
    ppermute x10, waiting for transfers between devices, _swap(): return lax.ppermute(x, 'core', [(0, 1), (1, 0)])  6.82 us
    all_to_all x1, waiting for transfers between devices, shards(): wide = lax.all_to_all(wide, ('z', 'x'), 0, 0, tiled=True)  5.05 us
  transfers between devices with their start and end apart: 22, of which 10 were waited for; matrix products, arithmetic and copies ran while one was open for 0% of the time, Pallas kernels for 0%

profile of v7, /device:TPU:1, one launch (start us, length us, event | category | flops | bytes accessed | tf_op | source)
XLA Modules:
  0.0 128.1 jit_solution(100862386826275644)
XLA Ops:
  0.6 0.9 broadcast_in_dim.4
  1.6 19.3 %all_to_all.25 = bf16[8,64,256]{2,1,0:T(8,128)(2,1)S(1)} all-to-all(bf16[8,64,256]{2,1,0:T(8,128)(2,1)S(1)} %broadcast_in_dim.4), channel_id=1, replica_groups=mesh['z'=8,'x'=4,'core'=2,'camp'=4] {'z'}, dimensions={0} | all-to-all | bytes 524288 | tf_op jit(solution)/shard_map/all_to_all | solution.py:285
  21.0 15.9 %all_to_all.26.part = bf16[4,8,64,256]{3,2,1,0:T(8,128)(2,1)S(1)} all-to-all(bf16[4,8,64,256]{3,2,1,0:T(8,128)(2,1)S(1)} %broadcast_in_dim.5), channel_id=1, replica_groups=mesh['z'=8,'x'=4,'core'=2,'camp'=4] {'x'}, dimensions={0} | all-to-all | bytes 2097152 | tf_op jit(solution)/shard_map/all_to_all | solution.py:285
  36.9 4.0 %collective-permute-start = (bf16[4,8,64,256]{3,2,1,0:T(8,128)(2,1)S(1)}, bf16[4,8,64,256]{3,2,1,0:T(8,128)(2,1)S(1)}, u32[]{:S(2)}, u32[]{:S(2)}) collective-permute-start(bf16[4,8,64,256]{3,2,1,0:T(8,128)(2,1)S(1)} %all_to_all.26.part), channel_id=1, source_target_pairs={{0,4},{4,0},{1,5},{5,1},{2,6},{6,2},{3,7},{7,3},{8,12},{12,8},{9,1... | collective-permute-start | bytes 3145736 | tf_op jit(solution)/shard_map/ppermute | solution.py:289
  41.9 1.3 %collective-permute-done.peer = bf16[4,8,64,256]{3,2,1,0:T(8,128)(2,1)S(1)} collective-permute-done((bf16[4,8,64,256]{3,2,1,0:T(8,128)(2,1)S(1)}, bf16[4,8,64,256]{3,2,1,0:T(8,128)(2,1)S(1)}, u32[]{:S(2)}, u32[]{:S(2)}) %collective-permute-start) | collective-permute-done | bytes 1048608 | tf_op jit(solution)/shard_map/ppermute | solution.py:289
  43.2 9.4 %shard_map.94 = (bf16[512,64,128]{2,1,0:T(8,128)(2,1)}, bf16[256,64,128]{2,1,0:T(8,128)(2,1)}, f32[16,128]{1,0:T(8,128)S(1)}, f32[16,128]{1,0:T(8,128)S(1)}, f32[64,128]{1,0:T(8,128)S(1)}) custom-call(s32[1,1]{1,0:T(1,128)S(6)} %copy.10.count.count0, bf16[64,128,256]{2,1,0:T(8,128)(2,1)S(1)} %shard_map.93.users, ...), custom_call_target="tpu_custom_call" | custom-call | tf_op jit(solution)/shard_map/pallas_call | solution.py:261
  52.7 1.2 collective-permute-done.1.got
  53.8 0.7 shard_map.95
  54.7 3.9 %all-to-all-start.2 = ((f32[32,16,128]{2,1,0:T(8,128)}), f32[32,16,128]{2,1,0:T(8,128)S(1)}, u32[]{:S(2)}, u32[]{:S(2)}) async-start(f32[32,16,128]{2,1,0:T(8,128)} %shard_map.95), calls=%async_computation.2 | async-start | bytes 524288 | tf_op jit(solution)/shard_map/all_to_all | solution.py:327
  58.6 0.5 collective-permute-start.2
  60.1 1.6 %collective-permute-done.4.theirs = f32[64,128]{1,0:T(8,128)S(1)} collective-permute-done((f32[64,128]{1,0:T(8,128)S(1)}, f32[64,128]{1,0:T(8,128)S(1)}, u32[]{:S(2)}, u32[]{:S(2)}) %collective-permute-start.4) | collective-permute-done | bytes 32800 | tf_op jit(solution)/shard_map/ppermute | solution.py:289
  61.8 2.8 %collective-permute-start.5 = (f32[128,128]{1,0:T(8,128)S(1)}, f32[128,128]{1,0:T(8,128)S(1)}, u32[]{:S(2)}, u32[]{:S(2)}) collective-permute-start(f32[128,128]{1,0:T(8,128)S(1)} %shard_map.97.r0), channel_id=1, source_target_pairs={{1,0},{2,1},{3,2},{0,3},{5,4},{6,5},{7,6},{4,7},{9,8},{10,9},{11,1... | collective-permute-start | bytes 196616 | tf_op jit(solution)/shard_map/ppermute | solution.py:298
  65.4 5.1 %all-to-all-done.2.parts = f32[32,16,128]{2,1,0:T(8,128)S(1)} async-done(((f32[32,16,128]{2,1,0:T(8,128)}), f32[32,16,128]{2,1,0:T(8,128)S(1)}, u32[]{:S(2)}, u32[]{:S(2)}) %all-to-all-start.2) | async-done | bytes 262176 | tf_op jit(solution)/shard_map/all_to_all | solution.py:327
  70.9 6.0 %shard_map.98 = (f32[16,128]{1,0:T(8,128)S(1)}, f32[128,128]{1,0:T(8,128)S(1)}, f32[16,128]{1,0:T(8,128)S(1)}, f32[128,128]{1,0:T(8,128)S(1)}) custom-call(s32[1,256]{1,0:T(1,128)S(1)} %copy-done.1, s32[1,256]{1,0:T(1,128)S(1)} %collective-permute-done.2.id1, s32[1,1]{1,0:T(1,128)S(6)} %copy.10.count.count0, s32[1,1]{1,0:T(1,128)} %collective-permute-done.3.count1, ...), custom_call_target="tpu_custom_call" | custom-call | tf_op jit(solution)/shard_map/pallas_call | solution.py:261
  77.0 0.7 shard_map.99
  77.7 7.9 %all-to-all-start.3 = ((f32[32,16,128]{2,1,0:T(8,128)}), f32[32,16,128]{2,1,0:T(8,128)S(1)}, u32[]{:S(2)}, u32[]{:S(2)}) async-start(f32[32,16,128]{2,1,0:T(8,128)} %shard_map.99), calls=%async_computation.3 | async-start | bytes 524288 | tf_op jit(solution)/shard_map/all_to_all | solution.py:294
  85.6 1.4 %collective-permute-start.10 = (f32[128,128]{1,0:T(8,128)S(1)}, f32[128,128]{1,0:T(8,128)S(1)}, u32[]{:S(2)}, u32[]{:S(2)}) collective-permute-start(f32[128,128]{1,0:T(8,128)S(1)} %get-tuple-element.49.mine), channel_id=1, source_target_pairs={{0,4},{4,0},{1,5},{5,1},{2,6},{6,2},{3,7},{7,3},{8,12},{12,8},{9,1... | collective-permute-start | bytes 196616 | tf_op jit(solution)/shard_map/ppermute | solution.py:289
  87.0 0.9 collective-permute-done.10.theirs
  87.9 1.9 %collective-permute-start.11 = (f32[128,128]{1,0:T(8,128)S(1)}, f32[128,128]{1,0:T(8,128)S(1)}, u32[]{:S(2)}, u32[]{:S(2)}) collective-permute-start(f32[128,128]{1,0:T(8,128)S(1)} %shard_map.101.r0), channel_id=1, source_target_pairs={{1,0},{2,1},{3,2},{0,3},{5,4},{6,5},{7,6},{4,7},{9,8},{10,9},{11,1... | collective-permute-start | bytes 196616 | tf_op jit(solution)/shard_map/ppermute | solution.py:298
  89.9 0.8 collective-permute-start.13
  90.6 5.5 %all-to-all-done.3.parts = f32[32,16,128]{2,1,0:T(8,128)S(1)} async-done(((f32[32,16,128]{2,1,0:T(8,128)}), f32[32,16,128]{2,1,0:T(8,128)S(1)}, u32[]{:S(2)}, u32[]{:S(2)}) %all-to-all-start.3) | async-done | bytes 262176 | tf_op jit(solution)/shard_map/all_to_all | solution.py:294
  96.2 6.8 %shard_map.102 = (f32[16,128]{1,0:T(8,128)S(1)}, f32[2,128,128]{2,1,0:T(8,128)S(1)}, f32[16,128]{1,0:T(8,128)S(1)}, f32[128,128]{1,0:T(8,128)S(1)}) custom-call(s32[1,256]{1,0:T(1,128)S(1)} %copy-done.1, s32[1,256]{1,0:T(1,128)S(1)} %collective-permute-done.2.id1, s32[1,1]{1,0:T(1,128)S(6)} %copy.10.count.count0, s32[1,1]{1,0:T(1,128)} %collective-permute-done.3.count1, ...), custom_call_target="tpu_custom_call" | custom-call | tf_op jit(solution)/shard_map/pallas_call | solution.py:261
  103.0 0.7 shard_map.104
  103.7 9.1 %all-to-all-start.4 = ((f32[32,16,128]{2,1,0:T(8,128)}), f32[32,16,128]{2,1,0:T(8,128)S(1)}, u32[]{:S(2)}, u32[]{:S(2)}) async-start(f32[32,16,128]{2,1,0:T(8,128)} %shard_map.104), calls=%async_computation.4 | async-start | bytes 524288 | tf_op jit(solution)/shard_map/all_to_all | solution.py:294
  112.8 1.3 collective-permute-start.14
  114.1 1.0 collective-permute-done.14.theirs
  115.1 2.1 %collective-permute-start.15 = (f32[2,128,128]{2,1,0:T(8,128)S(1)}, f32[2,128,128]{2,1,0:T(8,128)S(1)}, u32[]{:S(2)}, u32[]{:S(2)}) collective-permute-start(f32[2,128,128]{2,1,0:T(8,128)S(1)} %shard_map.103.p0), channel_id=1, source_target_pairs={{1,0},{2,1},{3,2},{0,3},{5,4},{6,5},{7,6},{4,7},{9,8},{10,9},{11,1... | collective-permute-start | bytes 393224 | tf_op jit(solution)/shard_map/ppermute | solution.py:298
  117.2 0.7 collective-permute-start.17
  117.9 5.9 %all-to-all-done.4.parts = f32[32,16,128]{2,1,0:T(8,128)S(1)} async-done(((f32[32,16,128]{2,1,0:T(8,128)}), f32[32,16,128]{2,1,0:T(8,128)S(1)}, u32[]{:S(2)}, u32[]{:S(2)}) %all-to-all-start.4) | async-done | bytes 262176 | tf_op jit(solution)/shard_map/all_to_all | solution.py:294
  123.9 2.7 %collective-permute-start.18 = (f32[2,16,128]{2,1,0:T(8,128)S(1)}, f32[2,16,128]{2,1,0:T(8,128)S(1)}, u32[]{:S(2)}, u32[]{:S(2)}) collective-permute-start(f32[2,16,128]{2,1,0:T(8,128)S(1)} %shard_map.105.mine), channel_id=1, source_target_pairs={{0,4},{4,0},{1,5},{5,1},{2,6},{6,2},{3,7},{7,3},{8,12},{12,8},{9,1... | collective-permute-start | bytes 49160 | tf_op jit(solution)/shard_map/ppermute | solution.py:289
  126.6 0.8 collective-permute-done.18.theirs
  127.4 0.7 shard_map.106
  (42 shorter events, 3.1 us)
Async XLA Ops:
  0.6 40.9 %copy-start = (bf16[8192,256]{1,0:T(8,128)(2,1)S(1)}, bf16[8192,256]{1,0:T(8,128)(2,1)}, u32[]{:S(2)}) copy-start(bf16[8192,256]{1,0:T(8,128)(2,1)} %param.6) | copy-start | bytes 12582916
  36.9 6.2 %collective-permute-start = (bf16[4,8,64,256]{3,2,1,0:T(8,128)(2,1)S(1)}, bf16[4,8,64,256]{3,2,1,0:T(8,128)(2,1)S(1)}, u32[]{:S(2)}, u32[]{:S(2)}) collective-permute-start(bf16[4,8,64,256]{3,2,1,0:T(8,128)(2,1)S(1)} %all_to_all.26.part), channel_id=1, source_target_pairs={{0,4},{4,0},{1,5},{5,1},{2,6},{6,2},{3,7},{7,3},{8,12},{12,8},{9,1... | collective-permute-start | bytes 3145736 | tf_op jit(solution)/shard_map/ppermute | solution.py:289
  41.5 1.6 %copy-start.1 = (s32[1,256]{1,0:T(1,128)S(1)}, s32[1,256]{1,0:T(1,128)}, u32[]{:S(2)}) copy-start(s32[1,256]{1,0:T(1,128)} %id0.1) | copy-start | bytes 3076
  41.8 17.8 %copy-start.3 = (s32[4096]{0:T(1024)S(1)}, s32[4096]{0:T(1024)}, u32[]{:S(2)}) copy-start(s32[4096]{0:T(1024)} %param.10) | copy-start | bytes 49156
  41.9 17.9 %copy-start.2 = (s32[8192]{0:T(1024)S(1)}, s32[8192]{0:T(1024)}, u32[]{:S(2)}) copy-start(s32[8192]{0:T(1024)} %param.11) | copy-start | bytes 98308
  52.6 1.3 collective-permute-start.1
  54.6 16.4 %collective-permute-start.9 = (bf16[256,64,128]{2,1,0:T(8,128)(2,1)}, bf16[256,64,128]{2,1,0:T(8,128)(2,1)}, u32[]{:S(2)}, u32[]{:S(2)}) collective-permute-start(bf16[256,64,128]{2,1,0:T(8,128)(2,1)} %get-tuple-element.47), channel_id=1, source_target_pairs={{0,4},{4,0},{1,5},{5,1},{2,6},{6,2},{3,7},{7,3},{8,12},{12,8},{9,1... | collective-permute-start | bytes 12582920 | tf_op jit(solution)/shard_map/ppermute | solution.py:289
  54.7 15.7 %all-to-all-start.2 = ((f32[32,16,128]{2,1,0:T(8,128)}), f32[32,16,128]{2,1,0:T(8,128)S(1)}, u32[]{:S(2)}, u32[]{:S(2)}) async-start(f32[32,16,128]{2,1,0:T(8,128)} %shard_map.95), calls=%async_computation.2 | async-start | bytes 524288 | tf_op jit(solution)/shard_map/all_to_all | solution.py:327
  58.6 11.9 %collective-permute-start.2 = (s32[1,256]{1,0:T(1,128)S(1)}, s32[1,256]{1,0:T(1,128)S(1)}, u32[]{:S(2)}, u32[]{:S(2)}) collective-permute-start(s32[1,256]{1,0:T(1,128)S(1)} %copy-done.1), channel_id=1, source_target_pairs={{0,4},{4,0},{1,5},{5,1},{2,6},{6,2},{3,7},{7,3},{8,12},{12,8},{9,1... | collective-permute-start | bytes 3080 | tf_op jit(solution)/shard_map/ppermute | solution.py:289
  59.2 5.4 %collective-permute-start.3 = (s32[1,1]{1,0:T(1,128)}, s32[1,1]{1,0:T(1,128)}, u32[]{:S(2)}, u32[]{:S(2)}) collective-permute-start(s32[1,1]{1,0:T(1,128)} %param.9), channel_id=1, source_target_pairs={{0,4},{4,0},{1,5},{5,1},{2,6},{6,2},{3,7},{7,3},{8,12},{12,8},{9,1... | collective-permute-start | bytes 20 | tf_op jit(solution)/shard_map/ppermute | solution.py:289
  59.3 2.5 %collective-permute-start.4 = (f32[64,128]{1,0:T(8,128)S(1)}, f32[64,128]{1,0:T(8,128)S(1)}, u32[]{:S(2)}, u32[]{:S(2)}) collective-permute-start(f32[64,128]{1,0:T(8,128)S(1)} %get-tuple-element.43.mine), channel_id=1, source_target_pairs={{0,4},{4,0},{1,5},{5,1},{2,6},{6,2},{3,7},{7,3},{8,12},{12,8},{9,1... | collective-permute-start | bytes 98312 | tf_op jit(solution)/shard_map/ppermute | solution.py:289
  59.8 5.1 %collective-permute-start.8 = (s32[8192]{0:T(1024)S(1)}, s32[8192]{0:T(1024)S(1)}, u32[]{:S(2)}, u32[]{:S(2)}) collective-permute-start(s32[8192]{0:T(1024)S(1)} %copy-done.2), channel_id=1, source_target_pairs={{0,4},{4,0},{1,5},{5,1},{2,6},{6,2},{3,7},{7,3},{8,12},{12,8},{9,1... | collective-permute-start | bytes 98312 | tf_op jit(solution)/shard_map/ppermute | solution.py:289
  61.8 8.7 %collective-permute-start.5 = (f32[128,128]{1,0:T(8,128)S(1)}, f32[128,128]{1,0:T(8,128)S(1)}, u32[]{:S(2)}, u32[]{:S(2)}) collective-permute-start(f32[128,128]{1,0:T(8,128)S(1)} %shard_map.97.r0), channel_id=1, source_target_pairs={{1,0},{2,1},{3,2},{0,3},{5,4},{6,5},{7,6},{4,7},{9,8},{10,9},{11,1... | collective-permute-start | bytes 196616 | tf_op jit(solution)/shard_map/ppermute | solution.py:298
  64.5 6.0 %collective-permute-start.6 = (f32[128,128]{1,0:T(8,128)S(1)}, f32[128,128]{1,0:T(8,128)S(1)}, u32[]{:S(2)}, u32[]{:S(2)}) collective-permute-start(f32[128,128]{1,0:T(8,128)S(1)} %shard_map.97.r0), channel_id=1, source_target_pairs={{2,0},{3,1},{0,2},{1,3},{6,4},{7,5},{4,6},{5,7},{10,8},{11,9},{8,1... | collective-permute-start | bytes 196616 | tf_op jit(solution)/shard_map/ppermute | solution.py:298
  64.9 6.0 %collective-permute-start.7 = (f32[128,128]{1,0:T(8,128)S(1)}, f32[128,128]{1,0:T(8,128)S(1)}, u32[]{:S(2)}, u32[]{:S(2)}) collective-permute-start(f32[128,128]{1,0:T(8,128)S(1)} %shard_map.97.r0), channel_id=1, source_target_pairs={{3,0},{0,1},{1,2},{2,3},{7,4},{4,5},{5,6},{6,7},{11,8},{8,9},{9,10... | collective-permute-start | bytes 196616 | tf_op jit(solution)/shard_map/ppermute | solution.py:298
  77.7 18.5 %all-to-all-start.3 = ((f32[32,16,128]{2,1,0:T(8,128)}), f32[32,16,128]{2,1,0:T(8,128)S(1)}, u32[]{:S(2)}, u32[]{:S(2)}) async-start(f32[32,16,128]{2,1,0:T(8,128)} %shard_map.99), calls=%async_computation.3 | async-start | bytes 524288 | tf_op jit(solution)/shard_map/all_to_all | solution.py:294
  85.6 2.3 %collective-permute-start.10 = (f32[128,128]{1,0:T(8,128)S(1)}, f32[128,128]{1,0:T(8,128)S(1)}, u32[]{:S(2)}, u32[]{:S(2)}) collective-permute-start(f32[128,128]{1,0:T(8,128)S(1)} %get-tuple-element.49.mine), channel_id=1, source_target_pairs={{0,4},{4,0},{1,5},{5,1},{2,6},{6,2},{3,7},{7,3},{8,12},{12,8},{9,1... | collective-permute-start | bytes 196616 | tf_op jit(solution)/shard_map/ppermute | solution.py:289
  87.9 8.3 %collective-permute-start.11 = (f32[128,128]{1,0:T(8,128)S(1)}, f32[128,128]{1,0:T(8,128)S(1)}, u32[]{:S(2)}, u32[]{:S(2)}) collective-permute-start(f32[128,128]{1,0:T(8,128)S(1)} %shard_map.101.r0), channel_id=1, source_target_pairs={{1,0},{2,1},{3,2},{0,3},{5,4},{6,5},{7,6},{4,7},{9,8},{10,9},{11,1... | collective-permute-start | bytes 196616 | tf_op jit(solution)/shard_map/ppermute | solution.py:298
  89.8 6.4 %collective-permute-start.12 = (f32[128,128]{1,0:T(8,128)S(1)}, f32[128,128]{1,0:T(8,128)S(1)}, u32[]{:S(2)}, u32[]{:S(2)}) collective-permute-start(f32[128,128]{1,0:T(8,128)S(1)} %shard_map.101.r0), channel_id=1, source_target_pairs={{2,0},{3,1},{0,2},{1,3},{6,4},{7,5},{4,6},{5,7},{10,8},{11,9},{8,1... | collective-permute-start | bytes 196616 | tf_op jit(solution)/shard_map/ppermute | solution.py:298
  89.9 6.4 %collective-permute-start.13 = (f32[128,128]{1,0:T(8,128)S(1)}, f32[128,128]{1,0:T(8,128)S(1)}, u32[]{:S(2)}, u32[]{:S(2)}) collective-permute-start(f32[128,128]{1,0:T(8,128)S(1)} %shard_map.101.r0), channel_id=1, source_target_pairs={{3,0},{0,1},{1,2},{2,3},{7,4},{4,5},{5,6},{6,7},{11,8},{8,9},{9,10... | collective-permute-start | bytes 196616 | tf_op jit(solution)/shard_map/ppermute | solution.py:298
  103.7 20.1 %all-to-all-start.4 = ((f32[32,16,128]{2,1,0:T(8,128)}), f32[32,16,128]{2,1,0:T(8,128)S(1)}, u32[]{:S(2)}, u32[]{:S(2)}) async-start(f32[32,16,128]{2,1,0:T(8,128)} %shard_map.104), calls=%async_computation.4 | async-start | bytes 524288 | tf_op jit(solution)/shard_map/all_to_all | solution.py:294
  112.8 2.3 %collective-permute-start.14 = (f32[2,128,128]{2,1,0:T(8,128)S(1)}, f32[2,128,128]{2,1,0:T(8,128)S(1)}, u32[]{:S(2)}, u32[]{:S(2)}) collective-permute-start(f32[2,128,128]{2,1,0:T(8,128)S(1)} %get-tuple-element.52.mine), channel_id=1, source_target_pairs={{0,4},{4,0},{1,5},{5,1},{2,6},{6,2},{3,7},{7,3},{8,12},{12,8},{9,1... | collective-permute-start | bytes 393224 | tf_op jit(solution)/shard_map/ppermute | solution.py:289
  115.1 11.5 %collective-permute-start.15 = (f32[2,128,128]{2,1,0:T(8,128)S(1)}, f32[2,128,128]{2,1,0:T(8,128)S(1)}, u32[]{:S(2)}, u32[]{:S(2)}) collective-permute-start(f32[2,128,128]{2,1,0:T(8,128)S(1)} %shard_map.103.p0), channel_id=1, source_target_pairs={{1,0},{2,1},{3,2},{0,3},{5,4},{6,5},{7,6},{4,7},{9,8},{10,9},{11,1... | collective-permute-start | bytes 393224 | tf_op jit(solution)/shard_map/ppermute | solution.py:298
  117.2 9.4 %collective-permute-start.16 = (f32[2,128,128]{2,1,0:T(8,128)S(1)}, f32[2,128,128]{2,1,0:T(8,128)S(1)}, u32[]{:S(2)}, u32[]{:S(2)}) collective-permute-start(f32[2,128,128]{2,1,0:T(8,128)S(1)} %shard_map.103.p0), channel_id=1, source_target_pairs={{2,0},{3,1},{0,2},{1,3},{6,4},{7,5},{4,6},{5,7},{10,8},{11,9},{8,1... | collective-permute-start | bytes 393224 | tf_op jit(solution)/shard_map/ppermute | solution.py:298
  117.2 9.4 %collective-permute-start.17 = (f32[2,128,128]{2,1,0:T(8,128)S(1)}, f32[2,128,128]{2,1,0:T(8,128)S(1)}, u32[]{:S(2)}, u32[]{:S(2)}) collective-permute-start(f32[2,128,128]{2,1,0:T(8,128)S(1)} %shard_map.103.p0), channel_id=1, source_target_pairs={{3,0},{0,1},{1,2},{2,3},{7,4},{4,5},{5,6},{6,7},{11,8},{8,9},{9,10... | collective-permute-start | bytes 393224 | tf_op jit(solution)/shard_map/ppermute | solution.py:298
  123.9 3.6 %collective-permute-start.18 = (f32[2,16,128]{2,1,0:T(8,128)S(1)}, f32[2,16,128]{2,1,0:T(8,128)S(1)}, u32[]{:S(2)}, u32[]{:S(2)}) collective-permute-start(f32[2,16,128]{2,1,0:T(8,128)S(1)} %shard_map.105.mine), channel_id=1, source_target_pairs={{0,4},{4,0},{1,5},{5,1},{2,6},{6,2},{3,7},{7,3},{8,12},{12,8},{9,1... | collective-permute-start | bytes 49160 | tf_op jit(solution)/shard_map/ppermute | solution.py:289

commit v8 on v7

--- a/solution.py
+++ b/solution.py
@@ -154,8 +154,7 @@
 def _round_kernel(id0, id1, count0, count1, load_in, r0, r1, r2, r3, cap_i, lim_i, lam_in, mu_in, kepts,
                   load, rows, values, lam_out, mu_out, lacc, racc, vacc, lamb, mub, scores, loaded):
     lists = ((id0, count0[0, 0]), (id1, count1[0, 0]))
-    for which, (_, cnt) in enumerate(lists):
-        _each(_turns(cnt), lambda g, w=which: _load(kepts[w], scores, loaded, w, g).start())
+    _each(_turns(lists[0][1]), lambda g: _load(kepts[0], scores, loaded, 0, g).start())
     _clear(lacc, racc, vacc)
     lam = 0.0 if lam_in is None else lam_in[...]
     mu = 0.0 if mu_in is None else mu_in[...]
@@ -168,6 +167,7 @@
         tall = jnp.broadcast_to(lam_bar[r:r + 1, :], (BLOCK, BLOCK)).T
         lamb[2 * r] = tall[:PART]
         lamb[2 * r + 1] = tall[PART:]
+    _each(_turns(lists[1][1]), lambda g: _load(kepts[1], scores, loaded, 1, g).start())
 
     for which, (ids, cnt) in enumerate(lists):
 

time: 128 us -> 129 us (level)
  starting transfers between devices: 40.8 us -> 49.1 us
  Pallas kernels: 25.5 us -> 18.1 us
    pallas_call x14, Pallas kernels: 25.5 us -> 18.1 us  [_call(): pl.pallas_call(kernel, in_specs=[SMEM] * n_smem + [VMEM] * (len(args) - n...]
    all_to_all x2, starting transfers between devices: 17 us -> 21.8 us  [_load_parts(): return lax.all_to_all(wide, ('z', 'x'), 0, 0, tiled=True)]
    all_to_all x1, starting transfers between devices: 3.91 us -> 7.02 us  [shards(): wide = lax.all_to_all(wide, ('z', 'x'), 0, 0, tiled=True)]
    all_to_all x2, waiting for transfers between devices: 11.5 us -> 13.1 us  [_load_parts(): return lax.all_to_all(wide, ('z', 'x'), 0, 0, tiled=True)]
    ppermute x10, starting transfers between devices: 10.8 us -> 12.4 us  [_swap(): return lax.ppermute(x, 'core', [(0, 1), (1, 0)])]
    ppermute x10, waiting for transfers between devices: 6.82 us -> 5.27 us  [_swap(): return lax.ppermute(x, 'core', [(0, 1), (1, 0)])]
    ppermute x9, starting transfers between devices: 9.16 us -> 7.8 us  [_shift(): return lax.ppermute(x, 'camp', [((i + k) % NCAMP, i) for i in range(NCAMP)])]
  transfers between devices with their start and end apart: 22 -> 22, of which waited for: 10 -> 9; matrix products, arithmetic and copies ran while one was open for 0% -> 0% of each run, Pallas kernels for 0% -> 0%
where the time goes in v8:
time: 129 us
  starting transfers between devices  49.1 us (38%)
  blocking collectives  35.2 us (27%)
  waiting for transfers between devices  24.1 us (19%)
  Pallas kernels  18.1 us (14%)
  between operations  1.53 us (1%)
    all_to_all x2, blocking collectives, _spread(): lax.all_to_all(jnp.broadcast_to(x[None], (n,) + x.shape), axes, 0, 0, til...  35.2 us
    all_to_all x2, starting transfers between devices, _load_parts(): return lax.all_to_all(wide, ('z', 'x'), 0, 0, tiled=True)  21.8 us
    pallas_call x14, Pallas kernels, _call(): pl.pallas_call(kernel, in_specs=[SMEM] * n_smem + [VMEM] * (len(args) - n...  18.1 us
    all_to_all x2, waiting for transfers between devices, _load_parts(): return lax.all_to_all(wide, ('z', 'x'), 0, 0, tiled=True)  13.1 us
    ppermute x10, starting transfers between devices, _swap(): return lax.ppermute(x, 'core', [(0, 1), (1, 0)])  12.4 us
    ppermute x9, starting transfers between devices, _shift(): return lax.ppermute(x, 'camp', [((i + k) % NCAMP, i) for i in range(NCAMP)])  7.8 us
    all_to_all x1, starting transfers between devices, shards(): wide = lax.all_to_all(wide, ('z', 'x'), 0, 0, tiled=True)  7.02 us
    all_to_all x1, waiting for transfers between devices, shards(): wide = lax.all_to_all(wide, ('z', 'x'), 0, 0, tiled=True)  5.68 us
  transfers between devices with their start and end apart: 22, of which 9 were waited for; matrix products, arithmetic and copies ran while one was open for 0% of the time, Pallas kernels for 0%

profile of v8, /device:TPU:1, one launch (start us, length us, event | category | flops | bytes accessed | tf_op | source)
XLA Modules:
  0.0 129.3 jit_solution(7635516012637407701)
XLA Ops:
  0.6 0.9 broadcast_in_dim.4
  1.6 19.3 %all_to_all.25 = bf16[8,64,256]{2,1,0:T(8,128)(2,1)S(1)} all-to-all(bf16[8,64,256]{2,1,0:T(8,128)(2,1)S(1)} %broadcast_in_dim.4), channel_id=1, replica_groups=mesh['z'=8,'x'=4,'core'=2,'camp'=4] {'z'}, dimensions={0} | all-to-all | bytes 524288 | tf_op jit(solution)/shard_map/all_to_all | solution.py:285
  21.0 15.9 %all_to_all.26.part = bf16[4,8,64,256]{3,2,1,0:T(8,128)(2,1)S(1)} all-to-all(bf16[4,8,64,256]{3,2,1,0:T(8,128)(2,1)S(1)} %broadcast_in_dim.5), channel_id=1, replica_groups=mesh['z'=8,'x'=4,'core'=2,'camp'=4] {'x'}, dimensions={0} | all-to-all | bytes 2097152 | tf_op jit(solution)/shard_map/all_to_all | solution.py:285
  36.9 4.0 %collective-permute-start = (bf16[4,8,64,256]{3,2,1,0:T(8,128)(2,1)S(1)}, bf16[4,8,64,256]{3,2,1,0:T(8,128)(2,1)S(1)}, u32[]{:S(2)}, u32[]{:S(2)}) collective-permute-start(bf16[4,8,64,256]{3,2,1,0:T(8,128)(2,1)S(1)} %all_to_all.26.part), channel_id=1, source_target_pairs={{0,4},{4,0},{1,5},{5,1},{2,6},{6,2},{3,7},{7,3},{8,12},{12,8},{9,1... | collective-permute-start | bytes 3145736 | tf_op jit(solution)/shard_map/ppermute | solution.py:289
  41.9 1.3 collective-permute-done.peer
  43.2 4.9 %shard_map.94 = (bf16[512,64,128]{2,1,0:T(8,128)(2,1)}, bf16[256,64,128]{2,1,0:T(8,128)(2,1)}, f32[16,128]{1,0:T(8,128)S(1)}, f32[16,128]{1,0:T(8,128)S(1)}, f32[64,128]{1,0:T(8,128)S(1)}) custom-call(s32[1,1]{1,0:T(1,128)S(6)} %copy.10.count.count0, bf16[64,128,256]{2,1,0:T(8,128)(2,1)S(1)} %shard_map.93.users, ...), custom_call_target="tpu_custom_call" | custom-call | tf_op jit(solution)/shard_map/pallas_call | solution.py:261
  48.0 1.4 %collective-permute-start.1 = (f32[16,128]{1,0:T(8,128)S(1)}, f32[16,128]{1,0:T(8,128)S(1)}, u32[]{:S(2)}, u32[]{:S(2)}) collective-permute-start(f32[16,128]{1,0:T(8,128)S(1)} %get-tuple-element.37), channel_id=1, source_target_pairs={{0,4},{4,0},{1,5},{5,1},{2,6},{6,2},{3,7},{7,3},{8,12},{12,8},{9,1... | collective-permute-start | bytes 24584 | tf_op jit(solution)/shard_map/ppermute | solution.py:289
  49.4 0.8 collective-permute-done.1.got
  50.2 0.7 shard_map.95
  51.3 7.0 %all-to-all-start.2 = ((f32[32,16,128]{2,1,0:T(8,128)}), f32[32,16,128]{2,1,0:T(8,128)S(1)}, u32[]{:S(2)}, u32[]{:S(2)}) async-start(f32[32,16,128]{2,1,0:T(8,128)} %shard_map.95), calls=%async_computation.2 | async-start | bytes 524288 | tf_op jit(solution)/shard_map/all_to_all | solution.py:327
  58.3 0.5 collective-permute-start.2
  60.3 3.4 %collective-permute-start.5 = (f32[128,128]{1,0:T(8,128)S(1)}, f32[128,128]{1,0:T(8,128)S(1)}, u32[]{:S(2)}, u32[]{:S(2)}) collective-permute-start(f32[128,128]{1,0:T(8,128)S(1)} %shard_map.97.r0), channel_id=1, source_target_pairs={{1,0},{2,1},{3,2},{0,3},{5,4},{6,5},{7,6},{4,7},{9,8},{10,9},{11,1... | collective-permute-start | bytes 196616 | tf_op jit(solution)/shard_map/ppermute | solution.py:298
  64.0 0.5 collective-permute-start.7
  64.5 5.7 %all-to-all-done.2.parts = f32[32,16,128]{2,1,0:T(8,128)S(1)} async-done(((f32[32,16,128]{2,1,0:T(8,128)}), f32[32,16,128]{2,1,0:T(8,128)S(1)}, u32[]{:S(2)}, u32[]{:S(2)}) %all-to-all-start.2) | async-done | bytes 262176 | tf_op jit(solution)/shard_map/all_to_all | solution.py:327
  70.3 4.7 %shard_map.98 = (f32[16,128]{1,0:T(8,128)S(1)}, f32[128,128]{1,0:T(8,128)S(1)}, f32[16,128]{1,0:T(8,128)S(1)}, f32[128,128]{1,0:T(8,128)S(1)}) custom-call(s32[1,256]{1,0:T(1,128)S(1)} %copy-done.1, s32[1,256]{1,0:T(1,128)S(1)} %collective-permute-done.2.id1, s32[1,1]{1,0:T(1,128)S(6)} %copy.10.count.count0, s32[1,1]{1,0:T(1,128)} %collective-permute-done.3.count1, ...), custom_call_target="tpu_custom_call" | custom-call | tf_op jit(solution)/shard_map/pallas_call | solution.py:261
  75.0 0.7 shard_map.99
  75.8 10.3 %all-to-all-start.3 = ((f32[32,16,128]{2,1,0:T(8,128)}), f32[32,16,128]{2,1,0:T(8,128)S(1)}, u32[]{:S(2)}, u32[]{:S(2)}) async-start(f32[32,16,128]{2,1,0:T(8,128)} %shard_map.99), calls=%async_computation.3 | async-start | bytes 524288 | tf_op jit(solution)/shard_map/all_to_all | solution.py:294
  86.1 1.8 %collective-permute-start.10 = (f32[128,128]{1,0:T(8,128)S(1)}, f32[128,128]{1,0:T(8,128)S(1)}, u32[]{:S(2)}, u32[]{:S(2)}) collective-permute-start(f32[128,128]{1,0:T(8,128)S(1)} %get-tuple-element.49.mine), channel_id=1, source_target_pairs={{0,4},{4,0},{1,5},{5,1},{2,6},{6,2},{3,7},{7,3},{8,12},{12,8},{9,1... | collective-permute-start | bytes 196616 | tf_op jit(solution)/shard_map/ppermute | solution.py:289
  87.9 0.9 collective-permute-done.10.theirs
  89.1 0.6 collective-permute-start.12
  89.6 0.9 collective-permute-start.13
  90.5 6.0 %all-to-all-done.3.parts = f32[32,16,128]{2,1,0:T(8,128)S(1)} async-done(((f32[32,16,128]{2,1,0:T(8,128)}), f32[32,16,128]{2,1,0:T(8,128)S(1)}, u32[]{:S(2)}, u32[]{:S(2)}) %all-to-all-start.3) | async-done | bytes 262176 | tf_op jit(solution)/shard_map/all_to_all | solution.py:294
  96.5 5.2 %shard_map.102 = (f32[16,128]{1,0:T(8,128)S(1)}, f32[2,128,128]{2,1,0:T(8,128)S(1)}, f32[16,128]{1,0:T(8,128)S(1)}, f32[128,128]{1,0:T(8,128)S(1)}) custom-call(s32[1,256]{1,0:T(1,128)S(1)} %copy-done.1, s32[1,256]{1,0:T(1,128)S(1)} %collective-permute-done.2.id1, s32[1,1]{1,0:T(1,128)S(6)} %copy.10.count.count0, s32[1,1]{1,0:T(1,128)} %collective-permute-done.3.count1, ...), custom_call_target="tpu_custom_call" | custom-call | tf_op jit(solution)/shard_map/pallas_call | solution.py:261
  101.8 0.7 shard_map.104
  102.5 11.5 %all-to-all-start.4 = ((f32[32,16,128]{2,1,0:T(8,128)}), f32[32,16,128]{2,1,0:T(8,128)S(1)}, u32[]{:S(2)}, u32[]{:S(2)}) async-start(f32[32,16,128]{2,1,0:T(8,128)} %shard_map.104), calls=%async_computation.4 | async-start | bytes 524288 | tf_op jit(solution)/shard_map/all_to_all | solution.py:294
  114.0 1.2 collective-permute-start.14
  115.2 1.0 collective-permute-done.14.theirs
  116.3 1.8 %collective-permute-start.16 = (f32[2,128,128]{2,1,0:T(8,128)S(1)}, f32[2,128,128]{2,1,0:T(8,128)S(1)}, u32[]{:S(2)}, u32[]{:S(2)}) collective-permute-start(f32[2,128,128]{2,1,0:T(8,128)S(1)} %shard_map.103.p0), channel_id=1, source_target_pairs={{2,0},{3,1},{0,2},{1,3},{6,4},{7,5},{4,6},{5,7},{10,8},{11,9},{8,1... | collective-permute-start | bytes 393224 | tf_op jit(solution)/shard_map/ppermute | solution.py:298
  118.1 7.2 %all-to-all-done.4.parts = f32[32,16,128]{2,1,0:T(8,128)S(1)} async-done(((f32[32,16,128]{2,1,0:T(8,128)}), f32[32,16,128]{2,1,0:T(8,128)S(1)}, u32[]{:S(2)}, u32[]{:S(2)}) %all-to-all-start.4) | async-done | bytes 262176 | tf_op jit(solution)/shard_map/all_to_all | solution.py:294
  125.3 2.5 %collective-permute-start.18 = (f32[2,16,128]{2,1,0:T(8,128)S(1)}, f32[2,16,128]{2,1,0:T(8,128)S(1)}, u32[]{:S(2)}, u32[]{:S(2)}) collective-permute-start(f32[2,16,128]{2,1,0:T(8,128)S(1)} %shard_map.105.mine), channel_id=1, source_target_pairs={{0,4},{4,0},{1,5},{5,1},{2,6},{6,2},{3,7},{7,3},{8,12},{12,8},{9,1... | collective-permute-start | bytes 49160 | tf_op jit(solution)/shard_map/ppermute | solution.py:289
  127.8 0.8 collective-permute-done.18.theirs
  128.7 0.7 shard_map.106
  (42 shorter events, 3.0 us)
Async XLA Ops:
  0.6 40.9 %copy-start = (bf16[8192,256]{1,0:T(8,128)(2,1)S(1)}, bf16[8192,256]{1,0:T(8,128)(2,1)}, u32[]{:S(2)}) copy-start(bf16[8192,256]{1,0:T(8,128)(2,1)} %param.6) | copy-start | bytes 12582916
  36.9 6.2 %collective-permute-start = (bf16[4,8,64,256]{3,2,1,0:T(8,128)(2,1)S(1)}, bf16[4,8,64,256]{3,2,1,0:T(8,128)(2,1)S(1)}, u32[]{:S(2)}, u32[]{:S(2)}) collective-permute-start(bf16[4,8,64,256]{3,2,1,0:T(8,128)(2,1)S(1)} %all_to_all.26.part), channel_id=1, source_target_pairs={{0,4},{4,0},{1,5},{5,1},{2,6},{6,2},{3,7},{7,3},{8,12},{12,8},{9,1... | collective-permute-start | bytes 3145736 | tf_op jit(solution)/shard_map/ppermute | solution.py:289
  41.5 1.6 %copy-start.1 = (s32[1,256]{1,0:T(1,128)S(1)}, s32[1,256]{1,0:T(1,128)}, u32[]{:S(2)}) copy-start(s32[1,256]{1,0:T(1,128)} %id0.1) | copy-start | bytes 3076
  41.8 17.6 %copy-start.3 = (s32[4096]{0:T(1024)S(1)}, s32[4096]{0:T(1024)}, u32[]{:S(2)}) copy-start(s32[4096]{0:T(1024)} %param.10) | copy-start | bytes 49156
  41.9 17.6 %copy-start.2 = (s32[8192]{0:T(1024)S(1)}, s32[8192]{0:T(1024)}, u32[]{:S(2)}) copy-start(s32[8192]{0:T(1024)} %param.11) | copy-start | bytes 98308
  48.0 2.2 %collective-permute-start.1 = (f32[16,128]{1,0:T(8,128)S(1)}, f32[16,128]{1,0:T(8,128)S(1)}, u32[]{:S(2)}, u32[]{:S(2)}) collective-permute-start(f32[16,128]{1,0:T(8,128)S(1)} %get-tuple-element.37), channel_id=1, source_target_pairs={{0,4},{4,0},{1,5},{5,1},{2,6},{6,2},{3,7},{7,3},{8,12},{12,8},{9,1... | collective-permute-start | bytes 24584 | tf_op jit(solution)/shard_map/ppermute | solution.py:289
  51.0 19.3 %collective-permute-start.9 = (bf16[256,64,128]{2,1,0:T(8,128)(2,1)}, bf16[256,64,128]{2,1,0:T(8,128)(2,1)}, u32[]{:S(2)}, u32[]{:S(2)}) collective-permute-start(bf16[256,64,128]{2,1,0:T(8,128)(2,1)} %get-tuple-element.47), channel_id=1, source_target_pairs={{0,4},{4,0},{1,5},{5,1},{2,6},{6,2},{3,7},{7,3},{8,12},{12,8},{9,1... | collective-permute-start | bytes 12582920 | tf_op jit(solution)/shard_map/ppermute | solution.py:289
  51.3 18.9 %all-to-all-start.2 = ((f32[32,16,128]{2,1,0:T(8,128)}), f32[32,16,128]{2,1,0:T(8,128)S(1)}, u32[]{:S(2)}, u32[]{:S(2)}) async-start(f32[32,16,128]{2,1,0:T(8,128)} %shard_map.95), calls=%async_computation.2 | async-start | bytes 524288 | tf_op jit(solution)/shard_map/all_to_all | solution.py:327
  58.3 11.9 %collective-permute-start.2 = (s32[1,256]{1,0:T(1,128)S(1)}, s32[1,256]{1,0:T(1,128)S(1)}, u32[]{:S(2)}, u32[]{:S(2)}) collective-permute-start(s32[1,256]{1,0:T(1,128)S(1)} %copy-done.1), channel_id=1, source_target_pairs={{0,4},{4,0},{1,5},{5,1},{2,6},{6,2},{3,7},{7,3},{8,12},{12,8},{9,1... | collective-permute-start | bytes 3080 | tf_op jit(solution)/shard_map/ppermute | solution.py:289
  58.9 4.7 %collective-permute-start.3 = (s32[1,1]{1,0:T(1,128)}, s32[1,1]{1,0:T(1,128)}, u32[]{:S(2)}, u32[]{:S(2)}) collective-permute-start(s32[1,1]{1,0:T(1,128)} %param.9), channel_id=1, source_target_pairs={{0,4},{4,0},{1,5},{5,1},{2,6},{6,2},{3,7},{7,3},{8,12},{12,8},{9,1... | collective-permute-start | bytes 20 | tf_op jit(solution)/shard_map/ppermute | solution.py:289
  59.0 1.3 collective-permute-start.4
  59.5 4.5 %collective-permute-start.8 = (s32[8192]{0:T(1024)S(1)}, s32[8192]{0:T(1024)S(1)}, u32[]{:S(2)}, u32[]{:S(2)}) collective-permute-start(s32[8192]{0:T(1024)S(1)} %copy-done.2), channel_id=1, source_target_pairs={{0,4},{4,0},{1,5},{5,1},{2,6},{6,2},{3,7},{7,3},{8,12},{12,8},{9,1... | collective-permute-start | bytes 98312 | tf_op jit(solution)/shard_map/ppermute | solution.py:289
  60.3 10.0 %collective-permute-start.5 = (f32[128,128]{1,0:T(8,128)S(1)}, f32[128,128]{1,0:T(8,128)S(1)}, u32[]{:S(2)}, u32[]{:S(2)}) collective-permute-start(f32[128,128]{1,0:T(8,128)S(1)} %shard_map.97.r0), channel_id=1, source_target_pairs={{1,0},{2,1},{3,2},{0,3},{5,4},{6,5},{7,6},{4,7},{9,8},{10,9},{11,1... | collective-permute-start | bytes 196616 | tf_op jit(solution)/shard_map/ppermute | solution.py:298
  63.6 6.6 %collective-permute-start.6 = (f32[128,128]{1,0:T(8,128)S(1)}, f32[128,128]{1,0:T(8,128)S(1)}, u32[]{:S(2)}, u32[]{:S(2)}) collective-permute-start(f32[128,128]{1,0:T(8,128)S(1)} %shard_map.97.r0), channel_id=1, source_target_pairs={{2,0},{3,1},{0,2},{1,3},{6,4},{7,5},{4,6},{5,7},{10,8},{11,9},{8,1... | collective-permute-start | bytes 196616 | tf_op jit(solution)/shard_map/ppermute | solution.py:298
  64.0 6.2 %collective-permute-start.7 = (f32[128,128]{1,0:T(8,128)S(1)}, f32[128,128]{1,0:T(8,128)S(1)}, u32[]{:S(2)}, u32[]{:S(2)}) collective-permute-start(f32[128,128]{1,0:T(8,128)S(1)} %shard_map.97.r0), channel_id=1, source_target_pairs={{3,0},{0,1},{1,2},{2,3},{7,4},{4,5},{5,6},{6,7},{11,8},{8,9},{9,10... | collective-permute-start | bytes 196616 | tf_op jit(solution)/shard_map/ppermute | solution.py:298
  75.8 20.7 %all-to-all-start.3 = ((f32[32,16,128]{2,1,0:T(8,128)}), f32[32,16,128]{2,1,0:T(8,128)S(1)}, u32[]{:S(2)}, u32[]{:S(2)}) async-start(f32[32,16,128]{2,1,0:T(8,128)} %shard_map.99), calls=%async_computation.3 | async-start | bytes 524288 | tf_op jit(solution)/shard_map/all_to_all | solution.py:294
  86.1 2.7 %collective-permute-start.10 = (f32[128,128]{1,0:T(8,128)S(1)}, f32[128,128]{1,0:T(8,128)S(1)}, u32[]{:S(2)}, u32[]{:S(2)}) collective-permute-start(f32[128,128]{1,0:T(8,128)S(1)} %get-tuple-element.49.mine), channel_id=1, source_target_pairs={{0,4},{4,0},{1,5},{5,1},{2,6},{6,2},{3,7},{7,3},{8,12},{12,8},{9,1... | collective-permute-start | bytes 196616 | tf_op jit(solution)/shard_map/ppermute | solution.py:289
  88.8 7.7 %collective-permute-start.11 = (f32[128,128]{1,0:T(8,128)S(1)}, f32[128,128]{1,0:T(8,128)S(1)}, u32[]{:S(2)}, u32[]{:S(2)}) collective-permute-start(f32[128,128]{1,0:T(8,128)S(1)} %shard_map.101.r0), channel_id=1, source_target_pairs={{1,0},{2,1},{3,2},{0,3},{5,4},{6,5},{7,6},{4,7},{9,8},{10,9},{11,1... | collective-permute-start | bytes 196616 | tf_op jit(solution)/shard_map/ppermute | solution.py:298
  89.1 7.5 %collective-permute-start.12 = (f32[128,128]{1,0:T(8,128)S(1)}, f32[128,128]{1,0:T(8,128)S(1)}, u32[]{:S(2)}, u32[]{:S(2)}) collective-permute-start(f32[128,128]{1,0:T(8,128)S(1)} %shard_map.101.r0), channel_id=1, source_target_pairs={{2,0},{3,1},{0,2},{1,3},{6,4},{7,5},{4,6},{5,7},{10,8},{11,9},{8,1... | collective-permute-start | bytes 196616 | tf_op jit(solution)/shard_map/ppermute | solution.py:298
  89.6 6.9 %collective-permute-start.13 = (f32[128,128]{1,0:T(8,128)S(1)}, f32[128,128]{1,0:T(8,128)S(1)}, u32[]{:S(2)}, u32[]{:S(2)}) collective-permute-start(f32[128,128]{1,0:T(8,128)S(1)} %shard_map.101.r0), channel_id=1, source_target_pairs={{3,0},{0,1},{1,2},{2,3},{7,4},{4,5},{5,6},{6,7},{11,8},{8,9},{9,10... | collective-permute-start | bytes 196616 | tf_op jit(solution)/shard_map/ppermute | solution.py:298
  102.5 22.7 %all-to-all-start.4 = ((f32[32,16,128]{2,1,0:T(8,128)}), f32[32,16,128]{2,1,0:T(8,128)S(1)}, u32[]{:S(2)}, u32[]{:S(2)}) async-start(f32[32,16,128]{2,1,0:T(8,128)} %shard_map.104), calls=%async_computation.4 | async-start | bytes 524288 | tf_op jit(solution)/shard_map/all_to_all | solution.py:294
  114.0 2.2 %collective-permute-start.14 = (f32[2,128,128]{2,1,0:T(8,128)S(1)}, f32[2,128,128]{2,1,0:T(8,128)S(1)}, u32[]{:S(2)}, u32[]{:S(2)}) collective-permute-start(f32[2,128,128]{2,1,0:T(8,128)S(1)} %get-tuple-element.52.mine), channel_id=1, source_target_pairs={{0,4},{4,0},{1,5},{5,1},{2,6},{6,2},{3,7},{7,3},{8,12},{12,8},{9,1... | collective-permute-start | bytes 393224 | tf_op jit(solution)/shard_map/ppermute | solution.py:289
  116.2 11.6 %collective-permute-start.15 = (f32[2,128,128]{2,1,0:T(8,128)S(1)}, f32[2,128,128]{2,1,0:T(8,128)S(1)}, u32[]{:S(2)}, u32[]{:S(2)}) collective-permute-start(f32[2,128,128]{2,1,0:T(8,128)S(1)} %shard_map.103.p0), channel_id=1, source_target_pairs={{1,0},{2,1},{3,2},{0,3},{5,4},{6,5},{7,6},{4,7},{9,8},{10,9},{11,1... | collective-permute-start | bytes 393224 | tf_op jit(solution)/shard_map/ppermute | solution.py:298
  116.3 11.5 %collective-permute-start.16 = (f32[2,128,128]{2,1,0:T(8,128)S(1)}, f32[2,128,128]{2,1,0:T(8,128)S(1)}, u32[]{:S(2)}, u32[]{:S(2)}) collective-permute-start(f32[2,128,128]{2,1,0:T(8,128)S(1)} %shard_map.103.p0), channel_id=1, source_target_pairs={{2,0},{3,1},{0,2},{1,3},{6,4},{7,5},{4,6},{5,7},{10,8},{11,9},{8,1... | collective-permute-start | bytes 393224 | tf_op jit(solution)/shard_map/ppermute | solution.py:298
  118.1 9.7 %collective-permute-start.17 = (f32[2,128,128]{2,1,0:T(8,128)S(1)}, f32[2,128,128]{2,1,0:T(8,128)S(1)}, u32[]{:S(2)}, u32[]{:S(2)}) collective-permute-start(f32[2,128,128]{2,1,0:T(8,128)S(1)} %shard_map.103.p0), channel_id=1, source_target_pairs={{3,0},{0,1},{1,2},{2,3},{7,4},{4,5},{5,6},{6,7},{11,8},{8,9},{9,10... | collective-permute-start | bytes 393224 | tf_op jit(solution)/shard_map/ppermute | solution.py:298
  125.3 3.4 %collective-permute-start.18 = (f32[2,16,128]{2,1,0:T(8,128)S(1)}, f32[2,16,128]{2,1,0:T(8,128)S(1)}, u32[]{:S(2)}, u32[]{:S(2)}) collective-permute-start(f32[2,16,128]{2,1,0:T(8,128)S(1)} %shard_map.105.mine), channel_id=1, source_target_pairs={{0,4},{4,0},{1,5},{5,1},{2,6},{6,2},{3,7},{7,3},{8,12},{12,8},{9,1... | collective-permute-start | bytes 49160 | tf_op jit(solution)/shard_map/ppermute | solution.py:289
